TPU v7x, 32 devices: a whole 2x2x4 slice. The times are simulated.
32 devices in a mesh: blk: 8 (over y, x, core), tp: 4 (over z).
Axes of the slice: x: 2, y: 2, z: 4, core: 2. Of those that a mesh axis runs over, the one named last changes fastest.
Arguments:
- frames: bfloat16 [20, 512, 1024], P(None, 'blk'), may hold values from -6 to 6
- text_states: bfloat16 [20, 2, 64, 1024], replicated, may hold values from -6 to 6
- clip_lengths: int32 [20, 2], replicated, may hold values from 0 to 512, as said below
- text_lengths: int32 [20, 2], replicated, may hold values from 1 to 64
- cotangent: bfloat16 [20, 512, 1024], P(None, 'blk'), may hold values from -6 to 6
- norm_gain: float32 [3, 1024], replicated, may hold values from 0.5 to 1.5
- norm_bias: float32 [3, 1024], replicated, may hold values from -1.5 to 1.5
- self_proj: bfloat16 [3, 1024, 1024], P(None, None, 'tp'), may hold values from -0.1875 to 0.1875
- self_out: bfloat16 [1024, 1024], P('tp'), may hold values from -0.5 to 0.5
- cross_query: bfloat16 [1024, 1024], P(None, 'tp'), may hold values from -0.1875 to 0.1875
- cross_mem: bfloat16 [2, 1024, 1024], P(None, None, 'tp'), may hold values from -0.1875 to 0.1875
- cross_out: bfloat16 [1024, 1024], P('tp'), may hold values from -0.5 to 0.5
- ffn_up: bfloat16 [1024, 4096], P(None, 'tp'), may hold values from -0.1875 to 0.1875
- ffn_down: bfloat16 [4096, 1024], P('tp'), may hold values from -0.09375 to 0.09375
Outputs:
- out_frames: float32 [20, 512, 1024], P(None, 'blk')
- grad_frames: float32 [20, 512, 1024], P(None, 'blk')
- grad_text: float32 [20, 2, 64, 1024], replicated
- grad_gain: float32 [3, 1024], P(None, 'blk')
- grad_bias: float32 [3, 1024], P(None, 'blk')
- grad_self_proj: float32 [3, 1024, 1024], P(None, 'blk', 'tp')
- grad_self_out: float32 [1024, 1024], P('tp', 'blk')
- grad_cross_query: float32 [1024, 1024], P('blk', 'tp')
- grad_cross_mem: float32 [2, 1024, 1024], P(None, 'blk', 'tp')
- grad_cross_out: float32 [1024, 1024], P('tp', 'blk')
- grad_ffn_up: float32 [1024, 4096], P('blk', 'tp')
- grad_ffn_down: float32 [4096, 1024], P('tp', 'blk')
Inputs may be any that keep to these rules, and one draw needn't show every extreme that they name: `clip_lengths`: each stream's clip lengths add up to 512. In one stream, drawn from the seed, the first clip holds all 512 frames and the other slots none; every other stream holds one clip of 128 frames and one of 384 frames in its first two slots, in an order drawn from the seed, and its later slots are empty.
All inputs are finite; a program needn't handle non-finite values.
Results may differ from a plain program's by a relative error of at most 0.028.
Values may be sent and summed in bfloat16 or wider, within the bound.
No kernel may reach another device: no remote copies, remote signals or barrier semaphores. Data moves between devices by JAX's collectives and lax.ppermute only.
A program may use at most 512 MiB of HBM per device.

v0:
```python
import math

import jax
import jax.numpy as jnp
from jax import lax
from jax.sharding import PartitionSpec as P

HEAD_DIM = 64


score_scale = 0.125
masked_value = -1e30
norm_eps = 1e-05


def layer_norm(values, norm_scale, norm_shift):
    centre = values - jnp.mean(values, axis=-1, keepdims=True)
    spread = jnp.mean(centre * centre, axis=-1, keepdims=True)
    return centre * lax.rsqrt(spread + norm_eps) * norm_scale + norm_shift


def norm_backward(values, norm_scale, norm_shift, upstream):
    result, pullback = jax.vjp(layer_norm, values, norm_scale, norm_shift)
    return pullback(upstream)


def exact_gelu(values):
    return jax.nn.gelu(values, approximate=False)


def clip_index(lengths, positions):
    clip_ends = jnp.cumsum(lengths, axis=1)
    return jnp.sum((clip_ends[:, None, :] <= positions[None, :, None]).astype(jnp.int32), axis=2)


def split_heads(values):
    return values.reshape(values.shape[:-1] + (values.shape[-1] // HEAD_DIM, HEAD_DIM))


def pair_scores(queries, key_heads):
    return (
        jnp.einsum("sqhe,skhe->sqhk", queries, key_heads, preferred_element_type=jnp.float32)
        * score_scale
    )


def pair_allowed(lengths, query_pos, key_pos):
    causal = key_pos[None, None, :] <= query_pos[None, :, None]
    same_clip = (
        clip_index(lengths, key_pos)[:, None, :] == clip_index(lengths, query_pos)[:, :, None]
    )
    return (causal & same_clip)[:, :, None, :]


def in_blocks(step, running, pieces, block_rows):
    length = pieces[0].shape[1]

    def one_turn(turn_no, current):
        sliced = tuple(
            (
                lax.dynamic_slice_in_dim(member, turn_no * block_rows, block_rows, 1)
                for member in pieces
            )
        )
        return step(current, sliced, turn_no * block_rows)

    return lax.fori_loop(0, length // block_rows, one_turn, running)


def query_grad_terms(
    lengths, key_flat, value_flat, key_pos, query_heads, grad_heads, log_total, delta, query_pos
):
    key_heads = split_heads(key_flat)
    allowed = pair_allowed(lengths, query_pos, key_pos)
    scores = jnp.where(allowed, pair_scores(query_heads, key_heads), masked_value)
    weights = jnp.exp(scores - log_total[..., None])
    grad_weights = jnp.einsum(
        "sqhe,skhe->sqhk", grad_heads, split_heads(value_flat), preferred_element_type=jnp.float32
    )
    grad_scores = (weights * (grad_weights - delta[..., None])).astype(jnp.bfloat16)
    return score_scale * jnp.einsum(
        "sqhk,skhe->sqhe", grad_scores, key_heads, preferred_element_type=jnp.float32
    )


def key_grad_terms(
    lengths, key_flat, value_flat, key_pos, query_flat, grad_flat, lse_part, delta_part, query_pos
):
    query_heads = split_heads(query_flat)
    grad_heads = split_heads(grad_flat)
    allowed = pair_allowed(lengths, query_pos, key_pos)
    scores = jnp.where(allowed, pair_scores(query_heads, split_heads(key_flat)), masked_value)
    weights = jnp.exp(scores - lse_part[..., None])
    grad_weights = jnp.einsum(
        "sqhe,skhe->sqhk", grad_heads, split_heads(value_flat), preferred_element_type=jnp.float32
    )
    grad_scores = (weights * (grad_weights - delta_part[..., None])).astype(jnp.bfloat16)
    key_term = score_scale * jnp.einsum(
        "sqhk,sqhe->kshe", grad_scores, query_heads, preferred_element_type=jnp.float32
    )
    value_term = jnp.einsum(
        "sqhk,sqhe->kshe",
        weights.astype(jnp.bfloat16),
        grad_heads,
        preferred_element_type=jnp.float32,
    )
    stacked = jnp.stack([key_term, value_term], axis=2)
    return stacked.reshape(
        stacked.shape[0], stacked.shape[1], 2, stacked.shape[3] * stacked.shape[4]
    )


def shards(
    frames,
    text_states,
    clip_lengths,
    text_lengths,
    cotangent,
    norm_gain,
    norm_bias,
    self_proj,
    self_out,
    cross_query,
    cross_mem,
    cross_out,
    ffn_up,
    ffn_down,
):
    streams, row_count, model_width = frames.shape
    clip_slots = text_states.shape[1]
    text_count = text_states.shape[2]
    local_width = self_out.shape[0]
    head_count = local_width // HEAD_DIM
    cycle_size = lax.axis_size("blk")
    cycle_index = lax.axis_index("blk")
    first_row = cycle_index * row_count
    last_row = first_row + row_count - 1

    def keys_needed(offset):
        return offset <= last_row

    my_positions = first_row + jnp.arange(row_count, dtype=jnp.int32)
    my_clips = clip_index(clip_lengths, my_positions)
    inputs = frames.astype(jnp.float32)
    normed_one = layer_norm(inputs, norm_gain[0], norm_bias[0]).astype(jnp.bfloat16)
    projected = jnp.einsum(
        "sqd,kde->ksqe", normed_one, self_proj, preferred_element_type=jnp.float32
    ).astype(jnp.bfloat16)
    query_flat = projected[0]
    key_flat = projected[1]
    value_flat = projected[2]
    query_heads = split_heads(query_flat)

    def forward_step(running, pieces, offset):
        peaks, totals, accumulated = running
        key_pos = offset + jnp.arange(pieces[0].shape[1], dtype=jnp.int32)
        allowed = pair_allowed(clip_lengths, my_positions, key_pos)
        scores = jnp.where(allowed, pair_scores(query_heads, split_heads(pieces[0])), masked_value)
        new_peaks = jnp.maximum(peaks, jnp.max(scores, axis=-1))
        weights = jnp.where(allowed, jnp.exp(scores - new_peaks[..., None]), 0.0)
        factor = jnp.exp(peaks - new_peaks)
        totals = totals * factor + jnp.sum(weights, axis=-1)
        accumulated = accumulated * factor[..., None] + jnp.einsum(
            "sqhk,skhe->sqhe",
            weights.astype(jnp.bfloat16),
            split_heads(pieces[1]),
            preferred_element_type=jnp.float32,
        )
        return (new_peaks, totals, accumulated)

    start_state = (
        jnp.full((streams, row_count, head_count), masked_value, jnp.float32),
        jnp.zeros((streams, row_count, head_count), jnp.float32),
        jnp.zeros((streams, row_count, head_count, HEAD_DIM), jnp.float32),
    )
    pieces = (
        lax.all_gather(key_flat, "blk", axis=1, tiled=True),
        lax.all_gather(value_flat, "blk", axis=1, tiled=True),
    )
    peaks, totals, accumulated = lax.cond(
        keys_needed(jnp.int32(0)),
        lambda current: in_blocks(forward_step, current, pieces, row_count),
        lambda current: current,
        start_state,
    )
    attn_full = accumulated / totals[..., None]
    log_total = peaks + jnp.log(totals)
    attn_low = attn_full.astype(jnp.bfloat16).reshape(streams, row_count, local_width)
    second = inputs + lax.psum(
        jnp.einsum("sqe,ed->sqd", attn_low, self_out, preferred_element_type=jnp.float32).astype(
            jnp.bfloat16
        ),
        "tp",
    ).astype(jnp.float32)
    normed_two = layer_norm(second, norm_gain[1], norm_bias[1]).astype(jnp.bfloat16)
    cross_heads = split_heads(
        jnp.einsum(
            "sqd,de->sqe", normed_two, cross_query, preferred_element_type=jnp.float32
        ).astype(jnp.bfloat16)
    )
    memory = jnp.einsum(
        "scxd,kde->kscxe", text_states, cross_mem, preferred_element_type=jnp.float32
    ).astype(jnp.bfloat16)
    text_rows = clip_slots * text_count
    memory_keys = split_heads(memory[0].reshape(streams, text_rows, local_width))
    memory_values = split_heads(memory[1].reshape(streams, text_rows, local_width))
    row_ids = jnp.arange(text_rows, dtype=jnp.int32)
    row_valid = (row_ids % text_count)[None, :] < jnp.broadcast_to(
        text_lengths[:, :, None], (streams, clip_slots, text_count)
    ).reshape(streams, text_rows)
    cross_allowed = (
        ((row_ids // text_count)[None, None, :] == my_clips[:, :, None]) & row_valid[:, None, :]
    )[:, :, None, :]
    cross_scores = jnp.where(cross_allowed, pair_scores(cross_heads, memory_keys), masked_value)
    cross_exp = jnp.where(
        cross_allowed, jnp.exp(cross_scores - jnp.max(cross_scores, axis=-1, keepdims=True)), 0.0
    )
    cross_weights = cross_exp / jnp.sum(cross_exp, axis=-1, keepdims=True)
    cross_low = cross_weights.astype(jnp.bfloat16)
    cross_attn = (
        jnp.einsum("sqhk,skhe->sqhe", cross_low, memory_values, preferred_element_type=jnp.float32)
        .astype(jnp.bfloat16)
        .reshape(streams, row_count, local_width)
    )
    third = second + lax.psum(
        jnp.einsum("sqe,ed->sqd", cross_attn, cross_out, preferred_element_type=jnp.float32).astype(
            jnp.bfloat16
        ),
        "tp",
    ).astype(jnp.float32)
    normed_three = layer_norm(third, norm_gain[2], norm_bias[2]).astype(jnp.bfloat16)
    hidden = jnp.einsum("sqd,df->sqf", normed_three, ffn_up, preferred_element_type=jnp.float32)
    active = exact_gelu(hidden).astype(jnp.bfloat16)
    out_frames = third + lax.psum(
        jnp.einsum("sqf,fd->sqd", active, ffn_down, preferred_element_type=jnp.float32).astype(
            jnp.bfloat16
        ),
        "tp",
    ).astype(jnp.float32)
    upstream = cotangent.astype(jnp.float32)
    grad_ffn_down = jnp.einsum("sqf,sqd->fd", active, cotangent, preferred_element_type=jnp.float32)
    grad_active = jnp.einsum("sqd,fd->sqf", cotangent, ffn_down, preferred_element_type=jnp.float32)
    unused_value, gelu_pull = jax.vjp(exact_gelu, hidden)
    grad_hidden = gelu_pull(grad_active)[0].astype(jnp.bfloat16)
    grad_ffn_up = jnp.einsum(
        "sqd,sqf->df", normed_three, grad_hidden, preferred_element_type=jnp.float32
    )
    grad_normed_three = lax.psum(
        jnp.einsum("sqf,df->sqd", grad_hidden, ffn_up, preferred_element_type=jnp.float32).astype(
            jnp.bfloat16
        ),
        "tp",
    ).astype(jnp.float32)
    grad_third_in, gain_three, bias_three = norm_backward(
        third, norm_gain[2], norm_bias[2], grad_normed_three
    )
    grad_third = upstream + grad_third_in
    grad_cross_branch = grad_third.astype(jnp.bfloat16)
    grad_cross_out = jnp.einsum(
        "sqe,sqd->ed", cross_attn, grad_cross_branch, preferred_element_type=jnp.float32
    )
    grad_cross_attn = split_heads(
        jnp.einsum(
            "sqd,ed->sqe", grad_cross_branch, cross_out, preferred_element_type=jnp.float32
        ).astype(jnp.bfloat16)
    )
    grad_cross_weights = jnp.einsum(
        "sqhe,skhe->sqhk", grad_cross_attn, memory_values, preferred_element_type=jnp.float32
    )
    value_grad_part = jnp.einsum(
        "sqhk,sqhe->skhe", cross_low, grad_cross_attn, preferred_element_type=jnp.float32
    )
    cross_delta = jnp.sum(cross_weights * grad_cross_weights, axis=-1, keepdims=True)
    grad_cross_scores = (cross_weights * (grad_cross_weights - cross_delta)).astype(jnp.bfloat16)
    grad_cross_heads = (
        (
            score_scale
            * jnp.einsum(
                "sqhk,skhe->sqhe",
                grad_cross_scores,
                memory_keys,
                preferred_element_type=jnp.float32,
            )
        )
        .astype(jnp.bfloat16)
        .reshape(streams, row_count, local_width)
    )
    key_grad_part = score_scale * jnp.einsum(
        "sqhk,sqhe->skhe", grad_cross_scores, cross_heads, preferred_element_type=jnp.float32
    )
    memory_partial = jnp.stack([key_grad_part, value_grad_part]).reshape(
        2, streams, text_rows, local_width
    )
    memory_grads = lax.psum(memory_partial.astype(jnp.bfloat16), "blk").astype(jnp.float32)
    memory_grads = memory_grads.astype(jnp.bfloat16).reshape(
        2, streams, clip_slots, text_count, local_width
    )
    grad_mem_full = jnp.einsum(
        "scxd,kscxe->kde", text_states, memory_grads, preferred_element_type=jnp.float32
    )
    text_part = jnp.einsum(
        "kscxe,kde->scxd", memory_grads, cross_mem, preferred_element_type=jnp.float32
    )
    grad_cross_query = jnp.einsum(
        "sqd,sqe->de", normed_two, grad_cross_heads, preferred_element_type=jnp.float32
    )
    normed_part = jnp.einsum(
        "sqe,de->sqd", grad_cross_heads, cross_query, preferred_element_type=jnp.float32
    )
    grad_normed_two, grad_text = (
        lax.psum(normed_part.astype(jnp.bfloat16), "tp").astype(jnp.float32),
        lax.psum(text_part.astype(jnp.bfloat16), "tp").astype(jnp.float32),
    )
    grad_second_in, gain_two, bias_two = norm_backward(
        second, norm_gain[1], norm_bias[1], grad_normed_two
    )
    grad_second = grad_third + grad_second_in
    grad_branch = grad_second.astype(jnp.bfloat16)
    grad_self_out = jnp.einsum(
        "sqe,sqd->ed", attn_low, grad_branch, preferred_element_type=jnp.float32
    )
    grad_attn_flat = jnp.einsum(
        "sqd,ed->sqe", grad_branch, self_out, preferred_element_type=jnp.float32
    ).astype(jnp.bfloat16)
    grad_heads = split_heads(grad_attn_flat)
    delta = jnp.sum(grad_heads.astype(jnp.float32) * attn_full, axis=-1)
    key_all, value_all = (
        lax.all_gather(key_flat, "blk", axis=1, tiled=True),
        lax.all_gather(value_flat, "blk", axis=1, tiled=True),
    )
    total_rows = key_all.shape[1]
    sweep_rows = math.gcd(total_rows, 512)

    def query_turn(turn_no, running):
        offset = turn_no * sweep_rows

        def add_block(current):
            key_part = lax.dynamic_slice_in_dim(key_all, offset, sweep_rows, 1)
            value_part = lax.dynamic_slice_in_dim(value_all, offset, sweep_rows, 1)
            key_pos = offset + jnp.arange(sweep_rows, dtype=jnp.int32)
            return current + query_grad_terms(
                clip_lengths,
                key_part,
                value_part,
                key_pos,
                query_heads,
                grad_heads,
                log_total,
                delta,
                my_positions,
            )

        return lax.cond(keys_needed(offset), add_block, lambda current: current, running)

    query_zero = jnp.zeros((streams, row_count, head_count, HEAD_DIM), jnp.float32)
    query_grads = lax.fori_loop(0, total_rows // sweep_rows, query_turn, query_zero)
    count = row_count * lax.axis_size("blk")
    piece_rows = math.gcd(count, 512)

    def one_piece(piece_no):
        offset = piece_no * piece_rows

        def compute(unused):
            key_part = lax.dynamic_slice_in_dim(key_all, offset, piece_rows, 1)
            value_part = lax.dynamic_slice_in_dim(value_all, offset, piece_rows, 1)
            key_pos = offset + jnp.arange(piece_rows, dtype=jnp.int32)
            return key_grad_terms(
                clip_lengths,
                key_part,
                value_part,
                key_pos,
                query_flat,
                grad_attn_flat,
                log_total,
                delta,
                my_positions,
            )

        def nothing(unused):
            return jnp.zeros((piece_rows, streams, 2, local_width), jnp.float32)

        return lax.cond(keys_needed(offset), compute, nothing, 0)

    key_pieces = lax.map(one_piece, jnp.arange(count // piece_rows, dtype=jnp.int32))
    key_grads = lax.psum_scatter(
        key_pieces.reshape(count, streams, 2, local_width).astype(jnp.bfloat16),
        "blk",
        scatter_dimension=0,
        tiled=True,
    )
    query_low = query_grads.astype(jnp.bfloat16).reshape(streams, row_count, local_width)
    grad_query_proj = jnp.einsum(
        "sqd,sqe->de", normed_one, query_low, preferred_element_type=jnp.float32
    )
    grad_kv_proj = jnp.einsum(
        "sqd,qske->kde", normed_one, key_grads, preferred_element_type=jnp.float32
    )
    grad_self_proj = jnp.concatenate([grad_query_proj[None], grad_kv_proj], axis=0)
    first_part = jnp.einsum(
        "sqe,de->sqd", query_low, self_proj[0], preferred_element_type=jnp.float32
    ) + jnp.einsum("qske,kde->sqd", key_grads, self_proj[1:], preferred_element_type=jnp.float32)
    grad_normed_one = lax.psum(first_part.astype(jnp.bfloat16), "tp").astype(jnp.float32)
    grad_first_in, gain_one, bias_one = norm_backward(
        inputs, norm_gain[0], norm_bias[0], grad_normed_one
    )
    grad_frames = grad_second + grad_first_in
    grad_gain = jnp.stack([gain_one, gain_two, gain_three])
    grad_bias = jnp.stack([bias_one, bias_two, bias_three])
    summed = (
        lax.psum_scatter(
            grad_self_proj.astype(jnp.bfloat16), "blk", scatter_dimension=1, tiled=True
        ).astype(jnp.float32),
        lax.psum_scatter(
            grad_self_out.astype(jnp.bfloat16), "blk", scatter_dimension=1, tiled=True
        ).astype(jnp.float32),
        lax.psum_scatter(
            grad_cross_query.astype(jnp.bfloat16), "blk", scatter_dimension=0, tiled=True
        ).astype(jnp.float32),
        lax.psum_scatter(
            grad_cross_out.astype(jnp.bfloat16), "blk", scatter_dimension=1, tiled=True
        ).astype(jnp.float32),
        lax.psum_scatter(
            grad_ffn_up.astype(jnp.bfloat16), "blk", scatter_dimension=0, tiled=True
        ).astype(jnp.float32),
        lax.psum_scatter(
            grad_ffn_down.astype(jnp.bfloat16), "blk", scatter_dimension=1, tiled=True
        ).astype(jnp.float32),
        lax.psum_scatter(
            grad_gain.astype(jnp.bfloat16), "blk", scatter_dimension=1, tiled=True
        ).astype(jnp.float32),
        lax.psum_scatter(
            grad_bias.astype(jnp.bfloat16), "blk", scatter_dimension=1, tiled=True
        ).astype(jnp.float32),
    )
    share = model_width // cycle_size
    grad_cross_mem = lax.dynamic_slice_in_dim(grad_mem_full, cycle_index * share, share, 1)
    return (
        out_frames,
        grad_frames,
        grad_text,
        summed[6],
        summed[7],
        summed[0],
        summed[1],
        summed[2],
        grad_cross_mem,
        summed[3],
        summed[4],
        summed[5],
    )


def solution(mesh):
    in_specs = (
        P(None, "blk", None),
        P(),
        P(),
        P(),
        P(None, "blk", None),
        P(),
        P(),
        P(None, None, "tp"),
        P("tp", None),
        P(None, "tp"),
        P(None, None, "tp"),
        P("tp", None),
        P(None, "tp"),
        P("tp", None),
    )
    out_specs = (
        P(None, "blk", None),
        P(None, "blk", None),
        P(),
        P(None, "blk"),
        P(None, "blk"),
        P(None, "blk", "tp"),
        P("tp", "blk"),
        P("blk", "tp"),
        P(None, "blk", "tp"),
        P("tp", "blk"),
        P("blk", "tp"),
        P("tp", "blk"),
    )
    return jax.shard_map(shards, mesh=mesh, in_specs=in_specs, out_specs=out_specs, check_vma=False)
```

profile of v0, /device:TPU:0, one launch (start us, length us, event | category | flops | bytes accessed | tf_op | source)
XLA Modules:
  0.0 1735.5 jit_solution(1168318631202748598)
XLA Ops:
  19.3 41.6 %all-gather.7.cloned.1.call-done = bf16[1,20,512,256]{3,2,0,1:T(8,128)(2,1)} async-done(((bf16[1,20,64,256]{3,2,0,1:T(8,128)(2,1)}), bf16[1,20,512,256]{3,2,0,1:T(8,128)(2,1)}) %all-gather.7.cloned.1.call-update) | async-done | bytes 5242896 | tf_op jit(solution)/shard_map/all_gather | solution.py:178
  60.9 43.6 %all-gather.5.cloned.1.call-done = bf16[1,20,512,256]{3,2,0,1:T(8,128)(2,1)} async-done(((bf16[1,20,64,256]{3,2,0,1:T(8,128)(2,1)}), bf16[1,20,512,256]{3,2,0,1:T(8,128)(2,1)}) %all-gather.5.cloned.1.call-update) | async-done | bytes 5242896 | tf_op jit(solution)/shard_map/all_gather | solution.py:177
  104.5 139.0 %conditional.3 = (f32[20,64,4]{1,2,0:T(4,128)}, f32[20,64,4]{1,2,0:T(4,128)}, f32[20,64,4,64]{1,3,2,0:T(8,128)}, f32[20,64,4]{1,2,0:T(4,128)S(1)}) conditional(s32[]{:T(128)} %convert_element_type.232, () %tuple.66, (s32[20,2]{0,1:T(2,128)S(1)}, s32[64]{0:T(128)S(1)}, bf16[20,512,256]{2,1,0:T(8,128)(2,1)}, bf16[20,64,4,64]{3,2,1,0:T(4,128)(2,1)}, ...), branch_computations={%region_2.3_spmd, %region_3.11_spmd} | conditional | flops 89335400 | bytes 16128407 | solution.py:180
  107.3 135.5 %while.21 = (s32[]{:T(128)}, f32[20,64,4]{1,2,0:T(4,128)}, f32[20,64,4]{1,2,0:T(4,128)}, f32[20,64,4,64]{1,3,2,0:T(8,128)}, s32[64]{0:T(128)S(1)}, /*index=5*/s3...) while((s32[]{:T(128)}, f32[20,64,4]{1,2,0:T(4,128)}, ...), condition=%wide.region_10.10_spmd.clone, body=%wide.region_5.9_spmd.clone.sunk | while | flops 89335360 | bytes 14776259 | solution.py:67
  133.9 4.2 bitcast_add_fusion.4
  151.2 4.1 bitcast_add_fusion.4
  168.6 4.2 bitcast_add_fusion.4
  185.9 4.2 bitcast_add_fusion.4
  203.3 4.2 bitcast_add_fusion.4
  220.6 4.2 bitcast_add_fusion.4
  238.0 4.2 bitcast_add_fusion.4
  251.3 5.6 convert_bitcast_fusion
  258.2 4.9 reshape_reshape_squeeze.7
  263.1 4.7 copy.166
  269.9 4.7 copy.168
  275.6 79.0 %all-reduce.10.cloned.1.call-done = bf16[20,64,1024]{2,1,0:T(8,128)(2,1)} async-done(((bf16[20,64,1024]{2,1,0:T(8,128)(2,1)}), bf16[20,64,1024]{2,1,0:T(8,128)(2,1)}) %all-reduce.10.cloned.1.call-update) | async-done | bytes 2621456 | tf_op jit(solution)/shard_map/psum | solution.py:189
  364.7 4.8 fusion.186
  376.2 103.1 %all-reduce.12.cloned.1.call-done = bf16[20,64,1024]{2,1,0:T(8,128)(2,1)} async-done(((bf16[20,64,1024]{2,1,0:T(8,128)(2,1)}), bf16[20,64,1024]{2,1,0:T(8,128)(2,1)}) %all-reduce.12.cloned.1.call-update) | async-done | bytes 2621456 | tf_op jit(solution)/shard_map/psum | solution.py:225
  479.3 4.4 fusion.181
  484.4 4.3 convert_reduce_fusion.2
  488.8 12.4 multiply_convert_fusion
  501.1 4.8 add_convert_fusion
  507.5 4.3 fusion.117
  512.1 103.1 %all-reduce.14.cloned.1.call-done = bf16[20,64,1024]{2,1,0:T(8,128)(2,1)} async-done(((bf16[20,64,1024]{2,1,0:T(8,128)(2,1)}), bf16[20,64,1024]{2,1,0:T(8,128)(2,1)}) %all-reduce.14.cloned.1.call-update) | async-done | bytes 2621456 | tf_op jit(solution)/shard_map/psum | solution.py:248
  615.2 4.4 fusion.82
  619.6 5.2 fusion.83
  630.2 4.5 fusion.103
  654.7 90.2 %all-reduce.16.cloned.1.call-done = bf16[20,64,1024]{2,1,0:T(8,128)(2,1)} async-done(((bf16[20,64,1024]{2,1,0:T(8,128)(2,1)}), bf16[20,64,1024]{2,1,0:T(8,128)(2,1)}) %all-reduce.16.cloned.1.call-update) | async-done | bytes 2621456 | tf_op jit(solution)/shard_map/psum | solution.py:311
  744.8 4.9 fusion.81
  749.8 6.3 fusion.84
  756.2 5.7 add_add_fusion.4
  771.1 60.0 %conditional.5 = (bf16[512,20,2,256]{0,3,1,2:T(8,128)(2,1)}) conditional(s32[]{:T(128)} %convert_element_type.264, () %tuple.69, (s32[64]{0:T(128)S(1)}, s32[20,2]{0,1:T(2,128)S(1)}, bf16[20,512,256]{2,1,0:T(8,128)(2,1)}, bf16[1,20,64,256]{3,2,0,1:T(8,128)(2,1)S(1)}, f32[20,64,4]{1,2,0:T(4,128)S(1)}, /*index=5*/bf16[20,512,256]{2,1,0:T(8,128)(2,1)}, ...), branch_computations={%region_35.36_spmd, %region_36.40_spmd} | conditional | flops 1380278528 | bytes 104545800 | solution.py:382
  776.8 7.9 copy.186
  784.7 8.0 copy.184
  792.8 8.1 fusion.187
  800.9 10.9 broadcast_multiply_fusion
  811.8 10.3 fusion.28
  822.0 9.1 pad_maximum_fusion
  831.1 26.6 %copy.189 = bf16[512,20,2,256]{3,2,1,0:T(2,128)(2,1)} copy(bf16[512,20,2,256]{0,3,1,2:T(8,128)(2,1)} %get-tuple-element.736) | data formatting | bytes 20971520 | tf_op jit(solution)/shard_map/while/body/eval_jaxpr/cond | solution.py:382
  857.8 6.8 bitcast_convert_fusion.1
  868.6 8.2 bitcast_convert_fusion.2
  884.3 5.9 fusion.147
  890.5 5.4 fusion.144
  899.7 38.1 %conditional.4 = (f32[20,64,4,64]{3,1,2,0:T(8,128)}) conditional(s32[]{:T(128)} %convert_element_type.264, f32[20,64,4,64]{3,1,2,0:T(8,128)} %broadcast.534, (s32[64]{0:T(128)S(1)}, s32[20,2]{0,1:T(2,128)S(1)}, bf16[20,512,256]{2,1,0:T(8,128)(2,1)}, bf16[20,64,4,64]{3,2,1,0:T(4,128)(2,1)S(1)}, f32[20,64,4]{1,2,0:T(4,128)S(1)}, ...), branch_computations={%region_30.31_spmd, %region_31.35_spmd} | conditional | flops 1024418048 | bytes 57912780 | solution.py:353
  901.1 8.0 copy.179
  909.1 8.1 fusion.15
  917.2 7.9 copy.177
  925.2 12.7 bitcast_add_fusion
  946.0 89.4 %all-reduce.18.cloned.1.call-done = (bf16[512,20,2,256]{3,2,1,0:T(2,128)(2,1)}, bf16[2,20,2,64,256]{4,3,0,2,1:T(8,128)(2,1)}) async-done(((bf16[512,20,2,256]{3,2,1,0:T(2,128)(2,1)}, bf16[2,20,2,64,256]{4,3,0,2,1:T(8,128)(2,1)}), (bf16[512,20,2,256]{3,2,1,0:T(2,128)(2,1)}, bf16[2,20,2,64,256]{4,3,0,2,1:T(8,128)(2,1)})) %all-reduce.18.cloned.1.call-update) | async-done | bytes 13107216
  1047.1 7.1 fusion.120
  1058.2 4.6 bitcast_convert_fusion
  1065.4 15.1 reduce-scatter.35.cloned.1.call-done
  1082.4 42.6 %reduce-scatter.23.cloned.1.call-done = bf16[128,1024]{1,0:T(8,128)(2,1)} async-done(((bf16[1024,1024]{1,0:T(8,128)(2,1)}), bf16[128,1024]{1,0:T(8,128)(2,1)}) %reduce-scatter.23.cloned.1.call-update) | async-done | bytes 262160 | tf_op jit(solution)/shard_map/reduce_scatter | solution.py:422
  1126.7 35.6 %reduce-scatter.33.cloned.1.call-done = bf16[128,256]{1,0:T(8,128)(2,1)} async-done(((bf16[1024,256]{1,0:T(8,128)(2,1)}), bf16[128,256]{1,0:T(8,128)(2,1)}) %reduce-scatter.33.cloned.1.call-update) | async-done | bytes 65552
  1164.0 35.6 %reduce-scatter.21.cloned.1.call-done = bf16[128,256]{1,0:T(8,128)(2,1)} async-done(((bf16[1024,256]{1,0:T(8,128)(2,1)}), bf16[128,256]{1,0:T(8,128)(2,1)}) %reduce-scatter.21.cloned.1.call-update) | async-done | bytes 65552 | tf_op jit(solution)/shard_map/reduce_scatter | solution.py:416
  1203.3 33.7 %reduce-scatter.31.cloned.1.call-done = bf16[128,256]{1,0:T(8,128)(2,1)} async-done(((bf16[1024,256]{1,0:T(8,128)(2,1)}), bf16[128,256]{1,0:T(8,128)(2,1)}) %reduce-scatter.31.cloned.1.call-update) | async-done | bytes 65552
  1238.7 5.7 fusion.128
  1245.2 33.6 %reduce-scatter.29.cloned.1.call-done = bf16[128,768]{1,0:T(8,128)(2,1)} async-done(((bf16[1024,768]{1,0:T(8,128)(2,1)}), bf16[128,768]{1,0:T(8,128)(2,1)}) %reduce-scatter.29.cloned.1.call-update) | async-done | bytes 196624
  1280.9 360.9 %all-reduce.20.cloned.1.call-done = (bf16[20,64,1024]{2,1,0:T(8,128)(2,1)}, bf16[20,64,1024]{2,1,0:T(8,128)(2,1)}, bf16[20,2,64,1024]{3,2,1,0:T(8,128)(2,1)}) async-done(((bf16[20,64,1024]{2,1,0:T(8,128)(2,1)}, bf16[20,64,1024]{2,1,0:T(8,128)(2,1)}, bf16[20,2,64,1024]{3,2,1,0:T(8,128)(2,1)}), (bf16[20,64,1024]{2,1,0:T(8,128)(2,1)}, bf16[20,64,1024]{2,1,0:T(8,128)(2,1)}, ...) | async-done | bytes 10485776 | tf_op jit(solution)/shard_map/psum | solution.py:234
  1648.1 5.1 fusion.85
  1658.9 7.2 convert_add_fusion.1
  1666.1 5.5 convert_element_type.273
  1671.5 19.0 %reduce-scatter.25.cloned.1.call-done = bf16[128,3]{1,0:T(8,128)(2,1)} async-done(((bf16[1024,3]{1,0:T(8,128)(2,1)}), bf16[128,3]{1,0:T(8,128)(2,1)}) %reduce-scatter.25.cloned.1.call-update) | async-done | bytes 784
  1692.0 35.4 %reduce-scatter.27.cloned.1.call-done = bf16[128,3]{1,0:T(8,128)(2,1)} async-done(((bf16[1024,3]{1,0:T(8,128)(2,1)}), bf16[128,3]{1,0:T(8,128)(2,1)}) %reduce-scatter.27.cloned.1.call-update) | async-done | bytes 784
  (432 shorter events, 263.7 us)
Async XLA Ops:
  7.2 477.2 %copy-start = (bf16[1024,1024]{1,0:T(8,128)(2,1)S(1)}, bf16[1024,1024]{1,0:T(8,128)(2,1)}, u32[]{:S(2)}) copy-start(bf16[1024,1024]{1,0:T(8,128)(2,1)} %param.34) | copy-start | bytes 6291460
  7.2 5.1 copy-start.50
  7.2 5.1 copy-start.51
  7.2 53.7 %all-gather.7.cloned.1.call-start = ((), (), s32[]{:S(2)}) async-start(), calls=%async_computation.15 | async-start | bytes 5898240 | tf_op jit(solution)/shard_map/all_gather | solution.py:178
  7.3 5.7 copy-start.2
  7.3 5.7 copy-start.30
  9.6 6.0 copy-start.39
  12.4 347.5 %copy-start.56 = (f32[1,1024]{1,0:T(1,128)}, f32[1,1024]{1,0:T(1,128)S(1)}, u32[]{:S(2)}) copy-start(f32[1,1024]{1,0:T(1,128)S(1)} %get-tuple-element.606) | copy-start | bytes 12292
  15.6 88.9 %copy-start.49 = (s32[20,2]{0,1:T(2,128)S(1)}, s32[20,2]{0,1:T(2,128)}, u32[]{:S(2)}) copy-start(s32[20,2]{0,1:T(2,128)} %param.24) | copy-start | bytes 484
  16.9 87.6 %copy-start.17 = (bf16[1,20,64,256]{3,2,0,1:T(8,128)(2,1)}, bf16[1,20,64,256]{3,2,0,1:T(8,128)(2,1)S(1)}, u32[]{:S(2)}) copy-start(bf16[1,20,64,256]{3,2,0,1:T(8,128)(2,1)S(1)} %get-tuple-element.599) | copy-start | bytes 1966084
  16.9 87.6 %all-gather.5.cloned.1.call-start = ((), (), s32[]{:S(2)}) async-start(), calls=%async_computation.14 | async-start | bytes 5898240 | tf_op jit(solution)/shard_map/all_gather | solution.py:177
  17.7 337.0 %all-reduce.10.cloned.1.call-start = ((), (), s32[]{:S(2)}) async-start(), calls=%async_computation.8 | async-start | bytes 5242880 | tf_op jit(solution)/shard_map/psum | solution.py:189
  243.6 7.5 copy-start.58
  243.6 7.7 copy-start.61
  250.4 228.9 %all-reduce.12.cloned.1.call-start = ((), (), s32[]{:S(2)}) async-start(), calls=%async_computation.9 | async-start | bytes 5242880 | tf_op jit(solution)/shard_map/psum | solution.py:225
  354.6 5.2 copy-start.37
  359.9 4.8 copy-start.24
  376.0 239.2 %all-reduce.14.cloned.1.call-start = ((), (), s32[]{:S(2)}) async-start(), calls=%async_computation.10 | async-start | bytes 5242880 | tf_op jit(solution)/shard_map/psum | solution.py:248
  483.7 5.1 copy-start.6
  488.7 12.4 copy-start.15
  488.7 12.4 copy-start.60
  511.8 233.0 %all-reduce.16.cloned.1.call-start = ((), (), s32[]{:S(2)}) async-start(), calls=%async_computation.11 | async-start | bytes 5242880 | tf_op jit(solution)/shard_map/psum | solution.py:311
  615.2 4.5 copy-start.9
  615.2 9.7 slice-start
  619.6 5.3 copy-start.16
  619.6 5.3 slice-start.1
  630.2 4.6 copy-start.32
  630.2 4.5 copy-start.25
  637.3 5.1 copy-start.33
  641.5 393.8 %all-reduce.18.cloned.1.call-start = ((), (), s32[]{:S(2)}) async-start(), calls=%async_computation.22 | async-start | bytes 26214400
  744.8 5.0 copy-start.4
  744.8 11.3 slice-start.2
  744.8 11.3 copy-start.14
  749.8 6.3 copy-start.8
  749.8 6.3 copy-start.10
  749.8 6.3 slice-start.3
  756.1 8.1 copy-start.29
  765.1 6.0 copy-start.18
  784.7 8.0 copy-start.19
  792.8 8.2 copy-start.48
  857.8 222.6 %reduce-scatter.35.cloned.1.call-start = ((), (), s32[]{:S(2)}) async-start(), calls=%async_computation.21 | async-start | bytes 2359296
  868.6 256.4 %reduce-scatter.23.cloned.1.call-start = ((), (), s32[]{:S(2)}) async-start(), calls=%async_computation.13 | async-start | bytes 2359296 | tf_op jit(solution)/shard_map/reduce_scatter | solution.py:422
  876.9 6.2 copy-start.63
  876.9 7.4 copy-start.23
  876.9 7.4 copy-start.57
  876.9 285.5 %reduce-scatter.33.cloned.1.call-start = ((), (), s32[]{:S(2)}) async-start(), calls=%async_computation.20 | async-start | bytes 589824
  883.0 316.6 %reduce-scatter.21.cloned.1.call-start = ((), (), s32[]{:S(2)}) async-start(), calls=%async_computation.12 | async-start | bytes 589824 | tf_op jit(solution)/shard_map/reduce_scatter | solution.py:416
  890.2 9.5 copy-start.20
  890.2 346.8 %reduce-scatter.31.cloned.1.call-start = ((), (), s32[]{:S(2)}) async-start(), calls=%async_computation.19 | async-start | bytes 589824
  945.5 333.3 %reduce-scatter.29.cloned.1.call-start = ((), (), s32[]{:S(2)}) async-start(), calls=%async_computation.18 | async-start | bytes 1769472
  1047.0 7.2 copy-start.27
  1047.0 594.8 %all-reduce.20.cloned.1.call-start = ((), (), s32[]{:S(2)}) async-start(), calls=%async_computation.23 | async-start | bytes 20971520 | tf_op jit(solution)/shard_map/psum | solution.py:234
  1047.1 7.2 copy-start.31
  1062.9 140.4 %copy-start.53 = (bf16[1024]{0:T(1024)(128)(2,1)S(1)}, bf16[1024]{0:T(1024)(128)(2,1)}, u32[]{:S(2)}) copy-start(bf16[1024]{0:T(1024)(128)(2,1)} %get-tuple-element.555) | copy-start | bytes 6148
  1062.9 627.6 %reduce-scatter.25.cloned.1.call-start = ((), (), s32[]{:S(2)}) async-start(), calls=%async_computation.16 | async-start | bytes 294912
  1244.3 403.7 %copy-start.42 = (f32[20,64]{1,0:T(8,128)S(1)}, f32[20,64]{1,0:T(8,128)}, u32[]{:S(2)}) copy-start(f32[20,64]{1,0:T(8,128)} %copy-done.41) | copy-start | bytes 15364
  1641.9 11.3 slice-start.4
  1644.2 9.1 copy-start.5
  1644.2 9.1 slice-start.5
  1644.2 9.1 copy-start.13
  1657.8 69.5 %reduce-scatter.27.cloned.1.call-start = ((), (), s32[]{:S(2)}) async-start(), calls=%async_computation.17 | async-start | bytes 294912
  1657.9 8.1 slice-start.6
  1658.9 7.2 slice-start.7
  1666.0 62.7 %copy-start.1 = (bf16[1024,1024]{1,0:T(8,128)(2,1)S(1)}, bf16[1024,1024]{1,0:T(8,128)(2,1)}, u32[]{:S(2)}) copy-start(bf16[1024,1024]{1,0:T(8,128)(2,1)} %param.34) | copy-start | bytes 6291460
  (32 other events, 91.7 us)
Sparse Core Ops, SparseCore 0:
  17.0 43.8 all-gather.6
  63.4 41.1 all-gather.4
  250.5 104.1 all-reduce.9
  376.1 103.1 all-reduce.11
  511.9 103.1 all-reduce.13
  641.7 103.1 all-reduce.15
  857.9 177.4 all-reduce.17
  1039.0 41.3 reduce-scatter.34
  1083.7 41.1 reduce-scatter.22
  1128.2 34.1 reduce-scatter.32
  1165.5 34.1 reduce-scatter.20
  1202.8 34.1 reduce-scatter.30
  1240.3 38.4 reduce-scatter.28
  1282.0 359.7 all-reduce.19
  1658.0 32.5 reduce-scatter.24
  1693.7 33.5 reduce-scatter.26
where the time goes:
time: 1750 us; the launch traced here: 1740 us
  waiting for transfers between devices  1160 us (66%)
  matrix products  215 us (12%)
  local copies, waits for them, and re-layouts  187 us (11%)
  other arithmetic  152 us (9%)
    psum x1, waiting for transfers between devices, shards(): lax.psum(jnp.einsum('sqf,fd->sqd', active, ffn_down, preferred_element_ty...  361 us
    unnamed x23, waiting for transfers between devices  263 us
    psum x1, waiting for transfers between devices, shards(): lax.psum(jnp.einsum('sqf,df->sqd', grad_hidden, ffn_up, preferred_element...  103 us
    psum x1, waiting for transfers between devices, shards(): lax.psum(jnp.einsum('sqe,ed->sqd', cross_attn, cross_out, preferred_eleme...  103 us
    psum x1, waiting for transfers between devices, shards(): lax.psum(normed_part.astype(jnp.bfloat16), 'tp').astype(jnp.float32)  90.2 us
    psum x1, waiting for transfers between devices, shards(): lax.psum(jnp.einsum('sqe,ed->sqd', attn_low, self_out, preferred_element_...  79 us
    all_gather x1, waiting for transfers between devices, shards(): lax.all_gather(key_flat, 'blk', axis=1, tiled=True)  43.6 us
    reduce_scatter x1, waiting for transfers between devices, shards(): lax.psum_scatter(grad_ffn_up.astype(jnp.bfloat16), 'blk', scatter_dimensi...  42.6 us
  transfers between devices with their start and end apart: 16, of which 16 were waited for; matrix products, arithmetic and copies ran while one was open for 11% of the time, Pallas kernels for 0%

commit v1 on v0

v1 whole, which is shorter than its diff:
```python
import functools

import jax
import jax.numpy as jnp
from jax import lax
from jax.experimental import pallas as pl
from jax.experimental.pallas import tpu as pltpu
from jax.sharding import PartitionSpec as P

HEAD_DIM = 64
SCALE = 0.125
MASKED = -1e30
EPS = 1e-05
LANES = 128
BF = jnp.bfloat16
F32 = jnp.float32


def dot(a, b, dims):
    return lax.dot_general(a, b, (dims, ((), ())), preferred_element_type=F32)


NN = ((1,), (0,))
NT = ((1,), (1,))
TN = ((0,), (0,))


def head_masks(width):
    lane = lax.broadcasted_iota(jnp.int32, (1, width), 1) // HEAD_DIM
    return [lane == h for h in range(width // HEAD_DIM)]


def pick(mask, values):
    return jnp.where(mask, values, jnp.zeros_like(values))


def causal_probs(ends_ref, stream, slots, q, k, first, block):
    rows = first + lax.broadcasted_iota(jnp.int32, (block, 1), 0)
    begin = jnp.zeros((block, 1), jnp.int32)
    for c in range(slots):
        end = ends_ref[stream, c]
        begin = jnp.where(rows >= end, jnp.maximum(begin, end), begin)
    cols = lax.broadcasted_iota(jnp.int32, (block, k.shape[0]), 1)
    allowed = (cols <= rows) & (cols >= begin)
    scores = jnp.where(allowed, dot(q, k, NT), MASKED)
    weights = jnp.exp(scores - jnp.max(scores, axis=1, keepdims=True))
    return weights * (1.0 / jnp.sum(weights, axis=1, keepdims=True))


def self_forward_kernel(ends_ref, qkv_ref, out_ref, *, slots, width, block):
    stream = pl.program_id(0)
    parts, _, rows, _ = qkv_ref.shape
    length = parts * rows
    qkv = qkv_ref[...].reshape(length, 3 * width)
    q = qkv[:, :width] * jnp.asarray(SCALE, BF)
    k = qkv[:, width : 2 * width]
    v = qkv[:, 2 * width :]
    masks = head_masks(width)
    q_of = [pick(m, q) for m in masks]
    v_of = [pick(m, v) for m in masks]
    per = block // rows
    for first in range(0, length, block):
        top = first + block
        total = jnp.zeros((block, width), F32)
        for h in range(len(masks)):
            probs = causal_probs(
                ends_ref, stream, slots, q_of[h][first:top], k[:top], first, block
            )
            total += dot(probs.astype(BF), v_of[h][:top], NN)
        at = first // rows
        out_ref[at : at + per, 0] = total.astype(BF).reshape(per, rows, width)


def self_backward_kernel(ends_ref, qkv_ref, grad_ref, out_ref, dk_ref, dv_ref, *, slots, width, block):
    stream = pl.program_id(0)
    parts, _, rows, _ = qkv_ref.shape
    length = parts * rows
    qkv = qkv_ref[...].reshape(length, 3 * width)
    q = qkv[:, :width] * jnp.asarray(SCALE, BF)
    k = qkv[:, width : 2 * width]
    v = qkv[:, 2 * width :]
    grad = grad_ref[...].reshape(length, width)
    masks = head_masks(width)
    q_of = [pick(m, q) for m in masks]
    k_of = [pick(m, k) for m in masks]
    g_of = [pick(m, grad) for m in masks]
    dk_ref[...] = jnp.zeros_like(dk_ref)
    dv_ref[...] = jnp.zeros_like(dv_ref)
    per = block // rows
    for first in range(0, length, block):
        top = first + block
        dq = jnp.zeros((block, width), F32)
        for h in range(len(masks)):
            q_part = q_of[h][first:top]
            g_part = g_of[h][first:top]
            probs = causal_probs(ends_ref, stream, slots, q_part, k[:top], first, block)
            d_probs = dot(g_part, v[:top], NT)
            delta = jnp.sum(probs * d_probs, axis=1, keepdims=True)
            d_scores = (probs * (d_probs - delta)).astype(BF)
            dq += dot(d_scores, k_of[h][:top], NN)
            dk_ref[:top] += dot(d_scores, q_part, TN)
            dv_ref[:top] += dot(probs.astype(BF), g_part, TN)
        at = first // rows
        out_ref[at : at + per, 0, :, :width] = (dq * SCALE).astype(BF).reshape(per, rows, width)
    out_ref[:, 0, :, width : 2 * width] = dk_ref[...].astype(BF).reshape(parts, rows, width)
    out_ref[:, 0, :, 2 * width :] = dv_ref[...].astype(BF).reshape(parts, rows, width)


def piece_spec(parts, rows, width):
    return pl.BlockSpec((parts, 1, rows, width), lambda s, *_: (0, s, 0, 0))


def block_rows(rows):
    return rows * max(1, 256 // rows)


def self_forward(ends, qkv, width):
    parts, streams, rows, _ = qkv.shape
    length = parts * rows
    kernel = functools.partial(
        self_forward_kernel, slots=ends.shape[1], width=width, block=min(length, block_rows(rows))
    )
    work = streams * (width // HEAD_DIM) * length * length
    return pl.pallas_call(
        kernel,
        out_shape=jax.ShapeDtypeStruct((parts, streams, rows, width), BF),
        grid_spec=pltpu.PrefetchScalarGridSpec(
            num_scalar_prefetch=1,
            grid=(streams,),
            in_specs=[piece_spec(parts, rows, 3 * width)],
            out_specs=piece_spec(parts, rows, width),
        ),
        compiler_params=pltpu.CompilerParams(vmem_limit_bytes=48 << 20),
        cost_estimate=pl.CostEstimate(
            flops=4 * work * HEAD_DIM, bytes_accessed=8 * streams * length * width, transcendentals=work
        ),
        name="self_forward",
    )(ends, qkv)


def self_backward(ends, qkv, grad, width):
    parts, streams, rows, _ = qkv.shape
    length = parts * rows
    kernel = functools.partial(
        self_backward_kernel, slots=ends.shape[1], width=width, block=min(length, block_rows(rows))
    )
    work = streams * (width // HEAD_DIM) * length * length
    return pl.pallas_call(
        kernel,
        out_shape=jax.ShapeDtypeStruct((parts, streams, rows, 3 * width), BF),
        grid_spec=pltpu.PrefetchScalarGridSpec(
            num_scalar_prefetch=1,
            grid=(streams,),
            in_specs=[piece_spec(parts, rows, 3 * width), piece_spec(parts, rows, width)],
            out_specs=piece_spec(parts, rows, 3 * width),
            scratch_shapes=[pltpu.VMEM((length, width), F32), pltpu.VMEM((length, width), F32)],
        ),
        compiler_params=pltpu.CompilerParams(vmem_limit_bytes=48 << 20),
        cost_estimate=pl.CostEstimate(
            flops=10 * work * HEAD_DIM, bytes_accessed=14 * streams * length * width, transcendentals=work
        ),
        name="self_backward",
    )(ends, qkv, grad)


def cross_allowed(info_ref, stream, slots, rows, keys):
    text = keys // slots
    pos = info_ref[stream, 2 * slots] + lax.broadcasted_iota(jnp.int32, (rows, 1), 0)
    clip = jnp.zeros((rows, 1), jnp.int32)
    for c in range(slots):
        clip += jnp.where(pos >= info_ref[stream, c], 1, 0)
    begin = clip * text
    count = jnp.zeros((rows, 1), jnp.int32)
    for c in range(slots):
        count = jnp.where(clip == c, info_ref[stream, slots + c], count)
    key = lax.broadcasted_iota(jnp.int32, (rows, keys), 1)
    return (key >= begin) & (key < begin + count)


def stacked_heads(values):
    masks = head_masks(values.shape[1])
    return jnp.concatenate([pick(m, values) for m in masks], axis=0)


def merged_heads(values, rows):
    masks = head_masks(values.shape[1])
    total = values[:rows]
    for h in range(1, len(masks)):
        total = jnp.where(masks[h], values[h * rows : (h + 1) * rows], total)
    return total


def cross_probs(q, k, allowed):
    scores = jnp.where(allowed, dot(q, k, NT), MASKED)
    weights = jnp.exp(scores - jnp.max(scores, axis=1, keepdims=True))
    return weights * (1.0 / jnp.sum(weights, axis=1, keepdims=True))


def cross_forward_kernel(info_ref, q_ref, kv_ref, out_ref, *, slots):
    stream = pl.program_id(0)
    rows, width = q_ref.shape[1:]
    keys = kv_ref.shape[1]
    once = cross_allowed(info_ref, stream, slots, rows, keys)
    allowed = jnp.concatenate([once] * (LANES // HEAD_DIM), axis=0)
    for at in range(0, width, LANES):
        q = stacked_heads(q_ref[0, :, at : at + LANES] * jnp.asarray(SCALE, BF))
        probs = cross_probs(q, kv_ref[0, :, at : at + LANES], allowed)
        result = dot(probs.astype(BF), kv_ref[0, :, width + at : width + at + LANES], NN)
        out_ref[0, :, at : at + LANES] = merged_heads(result, rows).astype(BF)


def cross_backward_kernel(info_ref, q_ref, kv_ref, grad_ref, dq_ref, dkv_ref, *, slots):
    stream = pl.program_id(0)
    rows, width = q_ref.shape[1:]
    keys = kv_ref.shape[1]
    once = cross_allowed(info_ref, stream, slots, rows, keys)
    allowed = jnp.concatenate([once] * (LANES // HEAD_DIM), axis=0)
    for at in range(0, width, LANES):
        k = kv_ref[0, :, at : at + LANES]
        v = kv_ref[0, :, width + at : width + at + LANES]
        q = stacked_heads(q_ref[0, :, at : at + LANES] * jnp.asarray(SCALE, BF))
        grad = stacked_heads(grad_ref[0, :, at : at + LANES])
        probs = cross_probs(q, k, allowed)
        d_probs = dot(grad, v, NT)
        delta = jnp.sum(probs * d_probs, axis=1, keepdims=True)
        d_scores = (probs * (d_probs - delta)).astype(BF)
        dq = merged_heads(dot(d_scores, k, NN), rows) * SCALE
        dq_ref[0, :, at : at + LANES] = dq.astype(BF)
        dkv_ref[0, :, at : at + LANES] = dot(d_scores, q, TN).astype(BF)
        dkv_ref[0, :, width + at : width + at + LANES] = dot(probs.astype(BF), grad, TN).astype(BF)


def stream_spec(array):
    return pl.BlockSpec((1,) + array.shape[1:], lambda s, *_: (s, 0, 0))


def cross_call(kernel, info, arrays, outs, name):
    streams, rows, width = arrays[0].shape
    keys = arrays[1].shape[1]
    slots = info.shape[1] // 2
    work = streams * (width // HEAD_DIM) * rows * keys
    return pl.pallas_call(
        functools.partial(kernel, slots=slots),
        out_shape=outs,
        grid_spec=pltpu.PrefetchScalarGridSpec(
            num_scalar_prefetch=1,
            grid=(streams,),
            in_specs=[stream_spec(a) for a in arrays],
            out_specs=[stream_spec(o) for o in outs],
        ),
        compiler_params=pltpu.CompilerParams(vmem_limit_bytes=48 << 20),
        cost_estimate=pl.CostEstimate(
            flops=8 * work * HEAD_DIM,
            bytes_accessed=2 * sum(a.size for a in (*arrays, *outs)),
            transcendentals=work,
        ),
        name=name,
    )(info, *arrays)


def normalize(values):
    centre = values - jnp.mean(values, axis=-1, keepdims=True)
    inverse = lax.rsqrt(jnp.mean(centre * centre, axis=-1, keepdims=True) + EPS)
    return centre * inverse, inverse


def norm_backward(normal, inverse, gain, upstream):
    g = upstream * gain
    mean_g = jnp.mean(g, axis=-1, keepdims=True)
    mean_gn = jnp.mean(g * normal, axis=-1, keepdims=True)
    d_values = inverse * (g - mean_g - normal * mean_gn)
    return d_values, jnp.sum(upstream * normal, axis=0), jnp.sum(upstream, axis=0)


def gelu_parts(u):
    cdf = 0.5 * (1.0 + lax.erf(u * (0.5**0.5)))
    slope = cdf + u * jnp.exp(-0.5 * u * u) * (0.5 / jnp.pi) ** 0.5
    return u * cdf, slope


def shards(
    frames,
    text_states,
    clip_lengths,
    text_lengths,
    cotangent,
    norm_gain,
    norm_bias,
    self_proj,
    self_out,
    cross_query,
    cross_mem,
    cross_out,
    ffn_up,
    ffn_down,
):
    streams, rows, model = frames.shape
    slots, text = text_states.shape[1:3]
    text_rows = slots * text
    blk, tp = lax.axis_size("blk"), lax.axis_size("tp")
    b, t = lax.axis_index("blk"), lax.axis_index("tp")
    mine = streams // tp
    head_parts = min(blk, model // HEAD_DIM)
    stream_parts = blk // head_parts
    width = model // head_parts
    group = -(-mine // stream_parts)
    local = self_out.shape[0]
    per = local // width
    share = model // blk
    hidden = ffn_up.shape[1]
    count = mine * rows

    def of_rank(values, rank):
        return lax.dynamic_slice_in_dim(values, rank * mine, mine, 0)

    def share_rows(w):
        return lax.dynamic_slice_in_dim(w, b * share, share, w.ndim - 2)

    def share_cols(w):
        return lax.dynamic_slice_in_dim(w, b * share, share, 1).T

    first = share_rows(self_proj).reshape(3, share, per, width)
    first = first.transpose(1, 2, 0, 3).reshape(share, 3 * local)
    first = lax.all_gather(first, "tp").transpose(1, 0, 2).reshape(share, tp * 3 * local)
    w_qkv = lax.all_gather(first, "blk", axis=0, tiled=True)

    mem = share_rows(cross_mem)
    second = jnp.stack(
        [share_cols(self_out), share_rows(cross_query), share_cols(cross_out), mem[0], mem[1]]
    )
    second = lax.all_gather(second, "tp").transpose(2, 1, 0, 3).reshape(share, 5 * model)
    w_attn = lax.all_gather(second, "blk", axis=0, tiled=True)
    w_out, w_query, w_cross_out = (w_attn[:, i * model : (i + 1) * model] for i in range(3))
    w_mem = w_attn[:, 3 * model :]

    groups = tp // 2
    piece = jnp.concatenate([share_rows(ffn_up), share_cols(ffn_down)], axis=1)
    up_parts, down_parts = [ffn_up], [ffn_down.T]
    if groups > 1:
        others = [
            lax.ppermute(piece, "tp", [(i, (i + 2 * j) % tp) for i in range(tp)])
            for j in range(1, groups)
        ]
        w_others = lax.all_gather(jnp.concatenate(others, axis=1), "blk", axis=0, tiled=True)
        for j in range(groups - 1):
            up_parts.append(w_others[:, 2 * j * hidden : (2 * j + 1) * hidden])
            down_parts.append(w_others[:, (2 * j + 1) * hidden : (2 * j + 2) * hidden])
    w_up = jnp.concatenate(up_parts, axis=1)
    w_down = jnp.concatenate(down_parts, axis=1)

    ends = jnp.cumsum(of_rank(clip_lengths, t), axis=1).astype(jnp.int32)
    info = jnp.concatenate(
        [ends, of_rank(text_lengths, t), jnp.full((mine, 1), b * rows, jnp.int32)], axis=1
    )
    x = of_rank(frames, t).reshape(count, model).astype(F32)
    n1, r1 = normalize(x)
    h1 = (n1 * norm_gain[0] + norm_bias[0]).astype(BF)

    def to_heads(values):
        c = values.shape[1] // head_parts
        values = values.reshape(mine, rows, head_parts, c)
        if stream_parts > 1:
            values = jnp.pad(values, ((0, stream_parts * group - mine),) + ((0, 0),) * 3)
        values = values.reshape(stream_parts, group, rows, head_parts, c).transpose(0, 3, 1, 2, 4)
        return lax.all_to_all(values.reshape(blk, group, rows, c), "blk", 0, 0)

    def to_rows(values):
        c = values.shape[3]
        swapped = lax.all_to_all(values, "blk", 0, 0)
        swapped = swapped.reshape(stream_parts, head_parts, group, rows, c).transpose(0, 2, 3, 1, 4)
        swapped = swapped.reshape(stream_parts * group, rows, head_parts * c)
        return swapped[:mine].reshape(count, head_parts * c)

    own_ends = ends
    if stream_parts > 1:
        own_ends = jnp.pad(ends, ((0, stream_parts * group - mine), (0, 0)))
        own_ends = lax.dynamic_slice_in_dim(own_ends, b // head_parts * group, group, 0)

    qkv = to_heads(dot(h1, w_qkv, NN).astype(BF))
    attn = to_rows(self_forward(own_ends, qkv, width))
    x2 = x + dot(attn, w_out, NT)

    n2, r2 = normalize(x2)
    h2 = (n2 * norm_gain[1] + norm_bias[1]).astype(BF)
    cq = dot(h2, w_query, NN).astype(BF).reshape(mine, rows, model)
    texts = of_rank(text_states, t).reshape(mine * text_rows, model)
    ckv = dot(texts, w_mem, NN).astype(BF).reshape(mine, text_rows, 2 * model)
    (cattn,) = cross_call(
        cross_forward_kernel, info, (cq, ckv), [jax.ShapeDtypeStruct(cq.shape, BF)], "cross_forward"
    )
    cattn = cattn.reshape(count, model)
    x3 = x2 + dot(cattn, w_cross_out, NT)

    n3, r3 = normalize(x3)
    h3 = (n3 * norm_gain[2] + norm_bias[2]).astype(BF)
    swap = [(i, i ^ 1) for i in range(tp)]
    partner = t ^ 1
    h3_pair = jnp.concatenate([h3, lax.ppermute(h3, "tp", swap)], axis=0)
    ct = of_rank(cotangent, t).reshape(count, model)
    ct_pair = jnp.concatenate([ct, of_rank(cotangent, partner).reshape(count, model)], axis=0)
    up = dot(h3_pair, w_up, NN)
    act, slope = gelu_parts(up)
    act = act.astype(BF)
    d_up = (dot(ct_pair, w_down, NN) * slope).astype(BF)

    def pair_sum(partial):
        sent = lax.ppermute(partial[count:].astype(BF), "tp", swap)
        return partial[:count] + sent.astype(F32)

    d_h3 = pair_sum(dot(d_up, w_up, NT))
    out = x3 + pair_sum(dot(act, w_down, NT))
    g_up = dot(h3_pair, d_up, TN).astype(BF)
    g_down = dot(ct_pair, act, TN).astype(BF)

    def over_frames(parts):
        joined = jnp.concatenate(parts, axis=1) if len(parts) > 1 else parts[0]
        return lax.psum_scatter(joined, "blk", scatter_dimension=0, tiled=True)

    g_ffn = over_frames([g_up, g_down])
    g_ffn = g_ffn.reshape(share, 2, groups, hidden)
    ffn_total = g_ffn[:, :, 0].astype(F32)
    for j in range(1, groups):
        back = [((i + 2 * j) % tp, i) for i in range(tp)]
        ffn_total += lax.ppermute(g_ffn[:, :, j], "tp", back).astype(F32)
    grad_ffn_up = ffn_total[:, 0]
    grad_ffn_down = ffn_total[:, 1].T

    d_n3, gain3, bias3 = norm_backward(n3, r3, norm_gain[2], d_h3)
    d_x3 = ct.astype(F32) + d_n3

    d_c = d_x3.astype(BF)
    g_cross_out = dot(d_c, cattn, TN).astype(BF)
    d_cattn = dot(d_c, w_cross_out, NN).astype(BF).reshape(mine, rows, model)
    d_cq, d_ckv = cross_call(
        cross_backward_kernel,
        info,
        (cq, ckv, d_cattn),
        [jax.ShapeDtypeStruct(cq.shape, BF), jax.ShapeDtypeStruct(ckv.shape, BF)],
        "cross_backward",
    )
    d_cq = d_cq.reshape(count, model)
    g_query = dot(h2, d_cq, TN).astype(BF)
    d_h2 = dot(d_cq, w_query, NT)
    d_n2, gain2, bias2 = norm_backward(n2, r2, norm_gain[1], d_h2)
    d_x2 = d_x3 + d_n2

    d_ckv = lax.psum_scatter(
        d_ckv.reshape(mine * text_rows, 2 * model), "blk", scatter_dimension=0, tiled=True
    )
    text_part = mine * text_rows // blk
    g_mem = dot(lax.dynamic_slice_in_dim(texts, b * text_part, text_part, 0), d_ckv, TN).astype(BF)
    d_text = dot(d_ckv, w_mem, NT).astype(BF)
    d_text = lax.all_gather(lax.all_gather(d_text, "tp"), "blk")
    grad_text = d_text.transpose(1, 0, 2, 3).reshape(streams, slots, text, model)
    grad_text = grad_text.astype(F32)

    d_a = d_x2.astype(BF)
    g_out = dot(d_a, attn, TN).astype(BF)
    d_attn = to_heads(dot(d_a, w_out, NN).astype(BF))
    d_qkv = to_rows(self_backward(own_ends, qkv, d_attn, width))
    g_qkv = dot(h1, d_qkv, TN).astype(BF)
    d_h1 = dot(d_qkv, w_qkv, NT)
    d_n1, gain1, bias1 = norm_backward(n1, r1, norm_gain[0], d_h1)
    d_x = d_x2 + d_n1

    def over_ranks(values):
        return lax.psum_scatter(values, "tp", scatter_dimension=0).astype(F32)

    g_attn = over_frames([g_out, g_query, g_cross_out, g_mem])
    g_attn = over_ranks(g_attn.reshape(share, 5, tp, local).transpose(2, 1, 0, 3))
    grad_self_out = g_attn[0].T
    grad_cross_query = g_attn[1]
    grad_cross_out = g_attn[2].T
    grad_cross_mem = g_attn[3:]
    g_qkv = over_frames([g_qkv])
    g_qkv = over_ranks(g_qkv.reshape(share, tp, 3 * local).transpose(1, 0, 2))
    grad_self_proj = g_qkv.reshape(share, per, 3, width).transpose(2, 0, 1, 3)
    grad_self_proj = grad_self_proj.reshape(3, share, local)

    norms = lax.psum(jnp.stack([gain1, gain2, gain3, bias1, bias2, bias3]), ("blk", "tp"))
    norms = lax.dynamic_slice_in_dim(norms, b * share, share, 1)

    def to_ranks(values):
        gathered = lax.all_gather(values.astype(BF), "tp", axis=0, tiled=True)
        return gathered.reshape(streams, rows, model).astype(F32)

    return (
        to_ranks(out),
        to_ranks(d_x),
        grad_text,
        norms[:3],
        norms[3:],
        grad_self_proj,
        grad_self_out,
        grad_cross_query,
        grad_cross_mem,
        grad_cross_out,
        grad_ffn_up,
        grad_ffn_down,
    )


def solution(mesh):
    in_specs = (
        P(None, "blk", None),
        P(),
        P(),
        P(),
        P(None, "blk", None),
        P(),
        P(),
        P(None, None, "tp"),
        P("tp", None),
        P(None, "tp"),
        P(None, None, "tp"),
        P("tp", None),
        P(None, "tp"),
        P("tp", None),
    )
    out_specs = (
        P(None, "blk", None),
        P(None, "blk", None),
        P(),
        P(None, "blk"),
        P(None, "blk"),
        P(None, "blk", "tp"),
        P("tp", "blk"),
        P("blk", "tp"),
        P(None, "blk", "tp"),
        P("tp", "blk"),
        P("blk", "tp"),
        P("tp", "blk"),
    )
    return jax.shard_map(shards, mesh=mesh, in_specs=in_specs, out_specs=out_specs, check_vma=False)
```

time: 1750 us -> 860 us (0.49)
  waiting for transfers between devices: 1160 us -> 432 us
  blocking collectives: 0 us -> 134 us
  matrix products: 215 us -> 82.6 us
  local copies, waits for them, and re-layouts: 187 us -> 66.8 us
  other arithmetic: 152 us -> 41 us
  Pallas kernels: 0 us -> 58.5 us
  starting transfers between devices: 2.31 us -> 20.8 us
    psum x5 -> x0, waiting for transfers between devices: 736 us -> none  [the longest x1 361 us: shards(): lax.psum(jnp.einsum('sqf,fd->sqd', active, ffn_down, preferred_element_ty...]
    unnamed x23 -> x13, waiting for transfers between devices: 263 us -> 0.88 us
    dot_general x49 -> x21, matrix products: 210 us -> 82.6 us  [dot(): return lax.dot_general(a, b, (dims, ((), ())), preferred_element_type=F32)]
    reduce_scatter x2 -> x6, waiting for transfers between devices: 78.2 us -> 180 us  [the longest x3 133 us: over_frames(): return lax.psum_scatter(joined, 'blk', scatter_dimension=0, tiled=True)]
    all_to_all x0 -> x3, waiting for transfers between devices: none -> 75.9 us  [the longest x2 38.5 us: to_rows(): swapped = lax.all_to_all(values, 'blk', 0, 0)]
    psum x0 -> x1, blocking collectives: none -> 74.7 us  [shards(): lax.psum(jnp.stack([gain1, gain2, gain3, bias1, bias2, bias3]), ('blk', '...]
    reduce_sum x37 -> x5, other arithmetic: 63.8 us -> 3.95 us  [the longest x3 1.98 us: normalize(): inverse = lax.rsqrt(jnp.mean(centre * centre, axis=-1, keepdims=True) + EPS)]
    another operation x26 -> x5, local copies, waits for them, and re-layouts: 62.3 us -> 2.85 us  [the longest x2 1.8 us: to_heads(): values.reshape(stream_parts, group, rows, head_parts, c)]
  transfers between devices with their start and end apart: 16 -> 21, of which waited for: 16 -> 17; matrix products, arithmetic and copies ran while one was open for 11% -> 19% of each run, Pallas kernels for 0% -> 4%
where the time goes in v1:
time: 860 us; the launch traced here: 851 us
  waiting for transfers between devices  432 us (50%)
  blocking collectives  134 us (16%)
  matrix products  82.6 us (10%)
  local copies, waits for them, and re-layouts  66.8 us (8%)
  Pallas kernels  58.5 us (7%)
  other arithmetic  41 us (5%)
  starting transfers between devices  20.8 us (2%)
  between operations  15.2 us (2%)
    reduce_scatter x3, waiting for transfers between devices, over_frames(): return lax.psum_scatter(joined, 'blk', scatter_dimension=0, tiled=True)  133 us
    dot_general x21, matrix products, dot(): return lax.dot_general(a, b, (dims, ((), ())), preferred_element_type=F32)  82.6 us
    psum x1, blocking collectives, shards(): lax.psum(jnp.stack([gain1, gain2, gain3, bias1, bias2, bias3]), ('blk', '...  74.7 us
    reduce_scatter x2, waiting for transfers between devices, over_ranks(): return lax.psum_scatter(values, 'tp', scatter_dimension=0).astype(F32)  47.3 us
    all_gather x2, waiting for transfers between devices, to_ranks(): gathered = lax.all_gather(values.astype(BF), 'tp', axis=0, tiled=True)  43.5 us
    all_to_all x2, waiting for transfers between devices, to_rows(): swapped = lax.all_to_all(values, 'blk', 0, 0)  38.5 us
    all_to_all x1, waiting for transfers between devices, to_heads(): return lax.all_to_all(values.reshape(blk, group, rows, c), 'blk', 0, 0)  37.4 us
    pallas_call x2, Pallas kernels, cross_call(): pl.pallas_call(functools.partial(kernel, slots=slots), out_shape=outs, gr...  35.2 us
  transfers between devices with their start and end apart: 21, of which 17 were waited for; matrix products, arithmetic and copies ran while one was open for 19% of the time, Pallas kernels for 4%

profile of v1, /device:TPU:0, one launch (start us, length us, event | category | flops | bytes accessed | tf_op | source)
XLA Modules:
  0.0 851.1 jit_solution(6318584839618602041)
XLA Ops:
  11.5 27.1 %all_gather.36 = bf16[4,128,768]{2,1,0:T(8,128)(2,1)S(1)} all-gather(bf16[1,128,768]{2,1,0:T(8,128)(2,1)S(1)} %copy.90), channel_id=1, replica_groups=mesh['blk'=8,'tp'=4] {'tp'}, dimensions={0}, use_global_device_ids=true | all-gather | bytes 983040 | tf_op jit(solution)/shard_map/all_gather | solution.py:324
  39.8 12.1 %all-gather.21.cloned.1.call-done = bf16[20,128,256]{2,1,0:T(8,128)(2,1)} async-done(((bf16[5,128,256]{2,1,0:T(8,128)(2,1)}), bf16[20,128,256]{2,1,0:T(8,128)(2,1)}) %all-gather.21.cloned.1.call-update) | async-done | bytes 1310736 | tf_op jit(solution)/shard_map/all_gather | solution.py:331
  54.4 3.9 copy.99
  65.3 21.2 %collective-permute-done.1 = bf16[128,2048]{0,1:T(8,128)(2,1)S(1)} collective-permute-done((bf16[128,2048]{0,1:T(8,128)(2,1)S(1)}, bf16[128,2048]{0,1:T(8,128)(2,1)S(1)}, u32[]{:S(2)}, u32[]{:S(2)}) %collective-permute-start.1) | collective-permute-done | bytes 524320 | tf_op jit(solution)/shard_map/ppermute | solution.py:341
  88.7 12.1 %all-gather.11.cloned.1.call-done = bf16[1024,3072]{0,1:T(8,128)(2,1)} async-done(((bf16[128,3072]{0,1:T(8,128)(2,1)}), bf16[1024,3072]{0,1:T(8,128)(2,1)}) %all-gather.11.cloned.1.call-update) | async-done | bytes 6291472 | tf_op jit(solution)/shard_map/all_gather | solution.py:325
  100.8 5.1 convolution_convert_fusion.1
  107.9 3.8 all-to-all-start
  112.1 37.4 %all-to-all-done.qkv_ref = bf16[8,5,64,384]{3,2,1,0:T(8,128)(2,1)S(1)} async-done(((bf16[8,5,64,384]{3,2,1,0:T(8,128)(2,1)}), bf16[8,5,64,384]{3,2,1,0:T(8,128)(2,1)S(1)}, u32[]{:S(2)}, u32[]{:S(2)}) %all-to-all-start) | async-done | bytes 1966112 | tf_op jit(solution)/shard_map/all_to_all | solution.py:365
  149.5 7.7 self_forward.1
  157.2 3.5 all-to-all-start.1
  161.0 2.6 constant_dynamic-slice_fusion.4
  163.7 15.5 %all-to-all-done.1 = bf16[8,5,64,128]{3,2,1,0:T(8,128)(2,1)S(1)} async-done(((bf16[8,5,64,128]{3,2,1,0:T(8,128)(2,1)}), bf16[8,5,64,128]{3,2,1,0:T(8,128)(2,1)S(1)}, u32[]{:S(2)}, u32[]{:S(2)}) %all-to-all-start.1) | async-done | bytes 655392 | tf_op jit(solution)/shard_map/all_to_all | solution.py:369
  179.6 16.4 %all-gather.13.cloned.1.call-done = bf16[1024,5120]{0,1:T(8,128)(2,1)} async-done(((bf16[128,5120]{0,1:T(8,128)(2,1)}), bf16[1024,5120]{0,1:T(8,128)(2,1)}) %all-gather.13.cloned.1.call-update) | async-done | bytes 10485776 | tf_op jit(solution)/shard_map/all_gather | solution.py:332
  196.0 2.5 fusion.77
  198.9 2.7 fusion.37
  201.6 5.6 fusion.10
  207.2 14.0 %cross_forward.1 = bf16[5,64,1024]{2,1,0:T(8,128)(2,1)S(1)} custom-call(s32[5,5]{1,0:T(8,128)S(1)} %add_add_fusion.info_ref, bf16[5,64,1024]{2,1,0:T(8,128)(2,1)S(1)} %bitcast.151, bf16[5,128,2048]{2,1,0:T(8,128)(2,1)S(1)} %bitcast.147), custom_call_target="tpu_custom_call" | custom-call | flops 335544320 | bytes 3932160 | tf_op jit(solution)/shard_map/cross_forward/pallas_call | solution.py:242
  221.2 2.7 fusion.78
  228.3 7.7 all-gather.15.cloned.1.call-done
  236.0 2.8 fusion.72
  238.8 3.5 collective-permute-done
  242.2 3.3 multiply_convert_fusion
  245.6 6.7 fusion.5
  252.3 2.9 fusion.14
  256.9 2.9 fusion.13
  260.4 12.6 %collective-permute-done.3 = bf16[320,1024]{1,0:T(8,128)(2,1)S(1)} collective-permute-done((bf16[320,1024]{1,0:T(8,128)(2,1)S(1)}, bf16[320,1024]{1,0:T(8,128)(2,1)S(1)}, u32[]{:S(2)}, u32[]{:S(2)}) %collective-permute-start.3) | collective-permute-done | bytes 655392 | tf_op jit(solution)/shard_map/ppermute | solution.py:407
  273.7 11.8 %collective-permute-done.2 = bf16[320,1024]{1,0:T(8,128)(2,1)S(1)} collective-permute-done((bf16[320,1024]{1,0:T(8,128)(2,1)S(1)}, bf16[320,1024]{1,0:T(8,128)(2,1)S(1)}, u32[]{:S(2)}, u32[]{:S(2)}) %collective-permute-start.2) | collective-permute-done | bytes 655392 | tf_op jit(solution)/shard_map/ppermute | solution.py:407
  287.0 3.0 fusion.40
  290.0 21.2 %cross_backward.1 = (bf16[5,64,1024]{2,1,0:T(8,128)(2,1)S(1)}, bf16[5,128,2048]{2,1,0:T(8,128)(2,1)}) custom-call(s32[5,5]{1,0:T(8,128)S(1)} %add_add_fusion.info_ref, bf16[5,64,1024]{2,1,0:T(8,128)(2,1)S(1)} %bitcast.152, bf16[5,128,2048]{2,1,0:T(8,128)(2,1)} %bitcast.148, bf16[5,64,1024]{2,1,0:T(8,128)(2,1)S(1)} %bitcast.153), custom_call_target="tpu_custom_call" | custom-call | flops 335544320 | bytes 7208960 | tf_op jit(solution)/shard_map/cross_backward/pallas_call | solution.py:242
  312.5 3.0 multiply_reduce_fusion.1
  315.9 2.6 fusion.45
  318.8 14.1 %all_to_all.20.grad_ref = bf16[8,5,64,128]{3,2,1,0:T(8,128)(2,1)S(1)} all-to-all(bf16[8,5,64,128]{3,2,1,0:T(8,128)(2,1)S(1)} %bitcast.175), channel_id=1, replica_groups=mesh['blk'=8,'tp'=4] {'blk'}, dimensions={0} | all-to-all | bytes 1310720 | tf_op jit(solution)/shard_map/all_to_all | solution.py:365
  332.9 15.6 %self_backward.1 = bf16[8,5,64,384]{3,2,1,0:T(8,128)(2,1)} custom-call(s32[5,2]{1,0:T(8,128)S(1)} %reduce_window_sum.11.ends_ref, bf16[8,5,64,384]{3,2,1,0:T(8,128)(2,1)S(1)} %copy-done.6, bf16[8,5,64,128]{3,2,1,0:T(8,128)(2,1)S(1)} %all_to_all.20.grad_ref), custom_call_target="tpu_custom_call" | custom-call | flops 1677721600 | bytes 4587520 | tf_op jit(solution)/shard_map/self_backward/pallas_call | solution.py:148
  348.5 4.3 all-to-all-start.3
  355.2 23.0 %all-to-all-done.3 = bf16[8,5,64,384]{3,2,1,0:T(8,128)(2,1)} async-done(((bf16[8,5,64,384]{3,2,1,0:T(8,128)(2,1)}), bf16[8,5,64,384]{3,2,1,0:T(8,128)(2,1)}, u32[]{:S(2)}, u32[]{:S(2)}) %all-to-all-start.3) | async-done | bytes 1966112 | tf_op jit(solution)/shard_map/all_to_all | solution.py:369
  378.1 2.7 copy.101
  382.5 5.4 convolution_convert_fusion
  388.0 4.0 convolution_convert_fusion.5
  391.9 4.3 copy.107
  396.2 4.3 convolution_convert_fusion.6
  400.5 4.2 copy.106
  404.7 2.6 convolution_convert_fusion.7
  407.3 3.9 copy.105
  411.3 2.5 convolution_convert_fusion.4
  414.4 5.2 pad_maximum_fusion
  420.7 6.9 convolution_convert_fusion.2
  427.6 5.1 convolution_convert_fusion.3
  432.7 7.9 pad_maximum_fusion.1
  441.9 6.1 multiply_reduce_fusion.2
  449.7 3.0 fusion.48
  452.7 17.9 %all-gather.1 = bf16[320,1024]{1,0:T(8,128)(2,1)} all-gather(bf16[80,1024]{1,0:T(8,128)(2,1)S(1)} %fusion.48), channel_id=3, replica_groups=mesh['blk'=8,'tp'=4] {'tp'}, dimensions={0}, use_global_device_ids=true | all-gather | bytes 819200 | tf_op jit(solution)/shard_map/all_gather | solution.py:453
  473.1 61.9 %reduce-scatter.13.cloned.1.call-done = bf16[128,5120]{1,0:T(8,128)(2,1)} async-done(((bf16[1024,5120]{1,0:T(8,128)(2,1)}), bf16[128,5120]{1,0:T(8,128)(2,1)}) %reduce-scatter.13.cloned.1.call-update) | async-done | bytes 1310736 | tf_op jit(solution)/shard_map/reduce_scatter | solution.py:417
  535.0 2.8 reshape.233
  539.2 71.0 %reduce-scatter.17.cloned.1.call-done = bf16[128,4096]{1,0:T(8,128)(2,1)} async-done(((bf16[1024,4096]{1,0:T(8,128)(2,1)}), bf16[128,4096]{1,0:T(8,128)(2,1)}) %reduce-scatter.17.cloned.1.call-update) | async-done | bytes 1048592 | tf_op jit(solution)/shard_map/reduce_scatter | solution.py:417
  613.8 2.5 collective-permute-start.4
  616.4 74.7 %psum.7 = f32[6,1024]{1,0:T(8,128)S(1)} all-reduce(f32[6,1024]{1,0:T(8,128)S(1)} %stack.44), channel_id=1, replica_groups=mesh['blk'=8,'tp'=4] {'blk','tp'}, use_global_device_ids=true, to_apply=%region_20.21 | all-reduce | flops 6144 | bytes 49152 | tf_op jit(solution)/shard_map/psum | solution.py:480
  691.7 5.0 convert.17
  696.6 43.5 %all-gather.19.cloned.1.call-done = bf16[1280,1024]{1,0:T(8,128)(2,1)} async-done(((bf16[320,1024]{1,0:T(8,128)(2,1)}), bf16[1280,1024]{1,0:T(8,128)(2,1)}) %all-gather.19.cloned.1.call-update) | async-done | bytes 2621456 | tf_op jit(solution)/shard_map/all_gather | solution.py:484
  740.1 4.7 convert.18
  747.1 34.8 %all-gather.23.cloned.1.call-done = bf16[32,80,1024]{2,1,0:T(8,128)(2,1)} async-done(((bf16[4,80,1024]{2,1,0:T(8,128)(2,1)}), bf16[32,80,1024]{2,1,0:T(8,128)(2,1)}) %all-gather.23.cloned.1.call-update) | async-done | bytes 5242896 | tf_op jit(solution)/shard_map/all_gather | solution.py:453
  781.9 3.8 convert_bitcast_fusion
  785.7 5.2 copy.102
  790.9 16.5 %reduce-scatter.11.cloned.1.call-done = bf16[1,128,768]{1,2,0:T(8,128)(2,1)} async-done(((bf16[4,128,768]{1,2,0:T(8,128)(2,1)}), bf16[1,128,768]{1,2,0:T(8,128)(2,1)}) %reduce-scatter.11.cloned.1.call-update) | async-done | bytes 196624 | tf_op jit(solution)/shard_map/reduce_scatter | solution.py:467
  809.4 30.8 %reduce-scatter.15.cloned.1.call-done = bf16[1,5,128,256]{3,2,1,0:T(8,128)(2,1)} async-done(((bf16[4,5,128,256]{3,2,1,0:T(8,128)(2,1)}), bf16[1,5,128,256]{3,2,1,0:T(8,128)(2,1)}) %reduce-scatter.15.cloned.1.call-update) | async-done | bytes 327696 | tf_op jit(solution)/shard_map/reduce_scatter | solution.py:467
  (194 shorter events, 56.2 us)
Async XLA Ops:
  7.2 3.9 copy-start
  7.2 44.7 %all-gather.21.cloned.1.call-start = ((), (), s32[]{:S(2)}) async-start(), calls=%async_computation.21 | async-start | bytes 1638400 | tf_op jit(solution)/shard_map/all_gather | solution.py:331
  11.0 89.7 %all-gather.11.cloned.1.call-start = ((), (), s32[]{:S(2)}) async-start(), calls=%async_computation.10 | async-start | bytes 7077888 | tf_op jit(solution)/shard_map/all_gather | solution.py:325
  39.8 156.3 %all-gather.13.cloned.1.call-start = ((), (), s32[]{:S(2)}) async-start(), calls=%async_computation.11 | async-start | bytes 11796480 | tf_op jit(solution)/shard_map/all_gather | solution.py:332
  54.4 181.6 %all-gather.15.cloned.1.call-start = ((), (), s32[]{:S(2)}) async-start(), calls=%async_computation.12 | async-start | bytes 4718592 | tf_op jit(solution)/shard_map/all_gather | solution.py:344
  60.4 28.3 %copy-start.33 = (f32[3,1024]{1,0:T(4,128)S(1)}, f32[3,1024]{1,0:T(4,128)}, u32[]{:S(2)}) copy-start(f32[3,1024]{1,0:T(4,128)} %param.20) | copy-start | bytes 36868
  60.4 28.3 %copy-start.34 = (f32[3,1024]{1,0:T(4,128)S(1)}, f32[3,1024]{1,0:T(4,128)}, u32[]{:S(2)}) copy-start(f32[3,1024]{1,0:T(4,128)} %param.19) | copy-start | bytes 36868
  60.4 26.1 %collective-permute-start.1 = (bf16[128,2048]{0,1:T(8,128)(2,1)S(1)}, bf16[128,2048]{0,1:T(8,128)(2,1)S(1)}, u32[]{:S(2)}, u32[]{:S(2)}) collective-permute-start(bf16[128,2048]{0,1:T(8,128)(2,1)S(1)} %pad_maximum_fusion.14), channel_id=1, source_target_pairs={{0,2},{1,3},{2,0},{3,1},{4,6},{5,7},{6,4},{7,5},{8,10},{9,11},{10,... | collective-permute-start | bytes 1572872 | tf_op jit(solution)/shard_map/ppermute | solution.py:341
  86.5 0.8 copy-start.30
  88.6 17.3 %copy-start.14 = (f32[5,64,1024]{2,1,0:T(8,128)}, f32[5,64,1024]{2,1,0:T(8,128)S(1)}, u32[]{:S(2)}) copy-start(f32[5,64,1024]{2,1,0:T(8,128)S(1)} %dynamic-slice_convert_fusion) | copy-start | bytes 3932164
  107.9 3.8 copy-start.35
  107.9 3.8 copy-start.36
  107.9 41.6 %all-to-all-start = ((bf16[8,5,64,384]{3,2,1,0:T(8,128)(2,1)}), bf16[8,5,64,384]{3,2,1,0:T(8,128)(2,1)S(1)}, u32[]{:S(2)}, u32[]{:S(2)}) async-start(bf16[8,5,64,384]{3,2,1,0:T(8,128)(2,1)} %bitcast.157), calls=%async_computation | async-start | bytes 3932160 | tf_op jit(solution)/shard_map/all_to_all | solution.py:365
  149.5 7.7 copy-start.5
  157.2 22.0 %all-to-all-start.1 = ((bf16[8,5,64,128]{3,2,1,0:T(8,128)(2,1)}), bf16[8,5,64,128]{3,2,1,0:T(8,128)(2,1)S(1)}, u32[]{:S(2)}, u32[]{:S(2)}) async-start(bf16[8,5,64,128]{3,2,1,0:T(8,128)(2,1)} %self_forward.1), calls=%async_computation.1 | async-start | bytes 1310720 | tf_op jit(solution)/shard_map/all_to_all | solution.py:369
  160.8 35.3 %copy-start.15 = (f32[5,64,1024]{2,1,0:T(8,128)S(1)}, f32[5,64,1024]{2,1,0:T(8,128)}, u32[]{:S(2)}) copy-start(f32[5,64,1024]{2,1,0:T(8,128)} %copy-done.14) | copy-start | bytes 3932164
  160.8 250.5 %reduce-scatter.7.cloned.1.call-start = ((), (), s32[]{:S(2)}) async-start(), calls=%async_computation.15 | async-start | bytes 2949120 | tf_op jit(solution)/shard_map/reduce_scatter | solution.py:447
  179.6 19.0 %copy-start.21 = (bf16[1,5,64,8,128]{4,3,2,1,0:T(8,128)(2,1)}, bf16[1,5,64,8,128]{4,3,2,1,0:T(8,128)(2,1)S(1)}, u32[]{:S(2)}) copy-start(bf16[1,5,64,8,128]{4,3,2,1,0:T(8,128)(2,1)S(1)} %copy.93) | copy-start | bytes 1966084
  198.6 22.6 %copy-start.17 = (f32[320,1024]{1,0:T(8,128)}, f32[320,1024]{1,0:T(8,128)S(1)}, u32[]{:S(2)}) copy-start(f32[320,1024]{1,0:T(8,128)S(1)} %get-tuple-element.86) | copy-start | bytes 3932164
  198.9 2.7 copy-start.24
  201.6 5.6 copy-start.3
  207.2 16.7 %copy-start.2 = (bf16[640,2048]{1,0:T(8,128)(2,1)}, bf16[640,2048]{1,0:T(8,128)(2,1)S(1)}, u32[]{:S(2)}) copy-start(bf16[640,2048]{1,0:T(8,128)(2,1)S(1)} %fusion.10) | copy-start | bytes 7864324
  223.9 1.1 copy-start.7
  225.3 17.0 %copy-start.26 = (bf16[320,1024]{1,0:T(8,128)(2,1)}, bf16[320,1024]{1,0:T(8,128)(2,1)S(1)}, u32[]{:S(2)}) copy-start(bf16[320,1024]{1,0:T(8,128)(2,1)S(1)} %add_convert_fusion.2) | copy-start | bytes 1966084
  225.3 17.0 %collective-permute-start = (bf16[320,1024]{1,0:T(8,128)(2,1)S(1)}, bf16[320,1024]{1,0:T(8,128)(2,1)S(1)}, u32[]{:S(2)}, u32[]{:S(2)}) collective-permute-start(bf16[320,1024]{1,0:T(8,128)(2,1)S(1)} %add_convert_fusion.2), channel_id=1, source_target_pairs={{0,1},{1,0},{2,3},{3,2},{4,5},{5,4},{6,7},{7,6},{8,9},{9,8},{10,11... | collective-permute-start | bytes 1966088 | tf_op jit(solution)/shard_map/ppermute | solution.py:398
  228.3 17.3 %copy-start.28 = (bf16[5,64,1024]{2,1,0:T(8,128)(2,1)}, bf16[5,64,1024]{2,1,0:T(8,128)(2,1)S(1)}, u32[]{:S(2)}) copy-start(bf16[5,64,1024]{2,1,0:T(8,128)(2,1)S(1)} %get-tuple-element.67) | copy-start | bytes 1966084
  236.0 6.3 copy-start.20
  242.2 3.3 copy-start.37
  242.2 3.4 copy-start.32
  245.6 11.3 %copy-start.41 = (bf16[640,2048]{1,0:T(8,128)(2,1)}, bf16[640,2048]{1,0:T(8,128)(2,1)S(1)}, u32[]{:S(2)}) copy-start(bf16[640,2048]{1,0:T(8,128)(2,1)S(1)} %get-tuple-element.89) | copy-start | bytes 7864324
  252.3 2.9 copy-start.39
  255.3 17.7 %collective-permute-start.3 = (bf16[320,1024]{1,0:T(8,128)(2,1)S(1)}, bf16[320,1024]{1,0:T(8,128)(2,1)S(1)}, u32[]{:S(2)}, u32[]{:S(2)}) collective-permute-start(bf16[320,1024]{1,0:T(8,128)(2,1)S(1)} %slice.193), channel_id=1, source_target_pairs={{0,1},{1,0},{2,3},{3,2},{4,5},{5,4},{6,7},{7,6},{8,9},{9,8},{10,11... | collective-permute-start | bytes 1966088 | tf_op jit(solution)/shard_map/ppermute | solution.py:407
  259.7 13.3 %copy-start.8 = (f32[320,1024]{1,0:T(8,128)S(1)}, f32[320,1024]{1,0:T(8,128)}, u32[]{:S(2)}) copy-start(f32[320,1024]{1,0:T(8,128)} %copy-done.7) | copy-start | bytes 3932164
  259.9 25.7 %collective-permute-start.2 = (bf16[320,1024]{1,0:T(8,128)(2,1)S(1)}, bf16[320,1024]{1,0:T(8,128)(2,1)S(1)}, u32[]{:S(2)}, u32[]{:S(2)}) collective-permute-start(bf16[320,1024]{1,0:T(8,128)(2,1)S(1)} %slice.194), channel_id=1, source_target_pairs={{0,1},{1,0},{2,3},{3,2},{4,5},{5,4},{6,7},{7,6},{8,9},{9,8},{10,11... | collective-permute-start | bytes 1966088 | tf_op jit(solution)/shard_map/ppermute | solution.py:407
  287.0 3.0 copy-start.9
  287.0 3.0 copy-start.4
  311.1 1.3 copy-start.18
  312.5 3.0 copy-start.10
  312.5 3.0 copy-start.19
  318.5 14.4 %copy-start.6 = (bf16[8,5,64,384]{3,2,1,0:T(8,128)(2,1)S(1)}, bf16[8,5,64,384]{3,2,1,0:T(8,128)(2,1)}, u32[]{:S(2)}) copy-start(bf16[8,5,64,384]{3,2,1,0:T(8,128)(2,1)} %copy-done.5) | copy-start | bytes 5898244
  348.5 29.6 %all-to-all-start.3 = ((bf16[8,5,64,384]{3,2,1,0:T(8,128)(2,1)}), bf16[8,5,64,384]{3,2,1,0:T(8,128)(2,1)}, u32[]{:S(2)}, u32[]{:S(2)}) async-start(bf16[8,5,64,384]{3,2,1,0:T(8,128)(2,1)} %self_backward.1), calls=%async_computation.3 | async-start | bytes 3932160 | tf_op jit(solution)/shard_map/all_to_all | solution.py:369
  352.9 117.8 %reduce-scatter.9.cloned.1.call-start = ((), (), s32[]{:S(2)}) async-start(), calls=%async_computation.16 | async-start | bytes 7077888 | tf_op jit(solution)/shard_map/reduce_scatter | solution.py:417
  380.8 1.7 copy-start.25
  381.2 1.3 copy-start.23
  387.9 147.1 %reduce-scatter.13.cloned.1.call-start = ((), (), s32[]{:S(2)}) async-start(), calls=%async_computation.18 | async-start | bytes 11796480 | tf_op jit(solution)/shard_map/reduce_scatter | solution.py:417
  400.5 4.2 copy-start.22
  411.3 2.5 copy-start.11
  411.3 2.5 copy-start.12
  411.3 3.2 copy-start.13
  419.6 1.1 copy-start.29
  419.6 8.0 copy-start.27
  419.6 190.5 %reduce-scatter.17.cloned.1.call-start = ((), (), s32[]{:S(2)}) async-start(), calls=%async_computation.20 | async-start | bytes 9437184 | tf_op jit(solution)/shard_map/reduce_scatter | solution.py:417
  420.7 6.9 copy-start.38
  420.7 6.9 copy-start.40
  440.6 1.3 copy-start.16
  440.6 251.1 %all-gather.17.cloned.1.call-start = ((), (), s32[]{:S(2)}) async-start(), calls=%async_computation.13 | async-start | bytes 3276800 | tf_op jit(solution)/shard_map/all_gather | solution.py:484
  441.4 298.8 %all-gather.19.cloned.1.call-start = ((), (), s32[]{:S(2)}) async-start(), calls=%async_computation.14 | async-start | bytes 3276800 | tf_op jit(solution)/shard_map/all_gather | solution.py:484
  448.0 1.6 copy-start.31
  449.4 332.6 %all-gather.23.cloned.1.call-start = ((), (), s32[]{:S(2)}) async-start(), calls=%async_computation.22 | async-start | bytes 5898240 | tf_op jit(solution)/shard_map/all_gather | solution.py:453
  470.6 336.8 %reduce-scatter.11.cloned.1.call-start = ((), (), s32[]{:S(2)}) async-start(), calls=%async_computation.17 | async-start | bytes 983040 | tf_op jit(solution)/shard_map/reduce_scatter | solution.py:467
  473.1 367.1 %reduce-scatter.15.cloned.1.call-start = ((), (), s32[]{:S(2)}) async-start(), calls=%async_computation.19 | async-start | bytes 1638400 | tf_op jit(solution)/shard_map/reduce_scatter | solution.py:467
  613.8 131.0 %collective-permute-start.4 = (bf16[128,2,1024]{2,0,1:T(8,128)(2,1)S(1)}, bf16[128,2,1024]{2,0,1:T(8,128)(2,1)S(1)}, u32[]{:S(2)}, u32[]{:S(2)}) collective-permute-start(bf16[128,2,1024]{2,0,1:T(8,128)(2,1)S(1)} %bitcast.190), channel_id=1, source_target_pairs={{2,0},{3,1},{0,2},{1,3},{6,4},{7,5},{4,6},{5,7},{10,8},{11,9},{8,1... | collective-permute-start | bytes 1572872 | tf_op jit(solution)/shard_map/ppermute | solution.py:424
  807.4 36.8 %copy-start.1 = (bf16[3,1024,256]{2,1,0:T(8,128)(2,1)S(1)}, bf16[3,1024,256]{2,1,0:T(8,128)(2,1)}, u32[]{:S(2)}) copy-start(bf16[3,1024,256]{2,1,0:T(8,128)(2,1)} %param.21) | copy-start | bytes 4718596
Sparse Core Ops, SparseCore 0:
  11.2 40.7 all-gather.20
  54.4 46.3 all-gather.10
  102.7 93.3 all-gather.12
  198.3 37.5 all-gather.14
  311.3 43.6 reduce-scatter.6
  388.1 60.8 reduce-scatter.8
  453.4 81.5 reduce-scatter.12
  538.9 71.2 reduce-scatter.16
  611.8 71.5 all-gather.16
  685.3 54.7 all-gather.18
  742.0 39.8 all-gather.22
  784.1 23.2 reduce-scatter.10
  809.7 30.4 reduce-scatter.14

commit v2 on v1

v2 whole, which is shorter than its diff:
```python
import functools

import jax
import jax.numpy as jnp
from jax import lax
from jax.experimental import pallas as pl
from jax.experimental.pallas import tpu as pltpu
from jax.sharding import PartitionSpec as P

HEAD_DIM = 64
SCALE = 0.125
MASKED = -1e30
EPS = 1e-05
LANES = 128
BF = jnp.bfloat16
F32 = jnp.float32
MIB = 1 << 20

NN = ((1,), (0,))
NT = ((1,), (1,))
TN = ((0,), (0,))


def dot(a, b, dims):
    return lax.dot_general(a, b, (dims, ((), ())), preferred_element_type=F32)


def whole_spec(array):
    zeros = (0,) * len(array.shape)
    return pl.BlockSpec(tuple(array.shape), lambda *_: zeros)


def call(kernel, name, grid, ins, outs, scalars=(), scratch=(), deps=(), flops=0, exps=0):
    count = len(ins)

    def body(*refs):
        kept = len(scalars) + count
        kernel(*refs[:kept], *refs[kept + len(deps) :])

    specs = [whole_spec(a) if s is None else s for a, s in ins]
    specs += [pl.BlockSpec(memory_space=pl.ANY)] * len(deps)
    moved = sum(a.size * a.dtype.itemsize for a, _ in (*ins, *outs))
    return pl.pallas_call(
        body,
        out_shape=[o for o, _ in outs],
        grid_spec=pltpu.PrefetchScalarGridSpec(
            num_scalar_prefetch=len(scalars),
            grid=grid,
            in_specs=specs,
            out_specs=[whole_spec(o) if s is None else s for o, s in outs],
            scratch_shapes=list(scratch),
        ),
        compiler_params=pltpu.CompilerParams(vmem_limit_bytes=56 * MIB),
        cost_estimate=pl.CostEstimate(flops=flops, bytes_accessed=moved, transcendentals=exps),
        name=name,
    )(*scalars, *[a for a, _ in ins], *deps)


def struct(shape, dtype=BF):
    return jax.ShapeDtypeStruct(tuple(shape), dtype)


def assemble(whole_ref, near_ref, far_ref, device, parts=1):
    chips, ranks, share, cols = near_ref.shape
    c = cols // parts
    core = device % 2
    for chip in range(chips):
        for ref, k in ((near_ref, core), (far_ref, 1 - core)):
            rows = pl.ds(pl.multiple_of((2 * chip + k) * share, share), share)
            for p in range(parts):
                for r in range(ranks):
                    to = (p * ranks + r) * c
                    whole_ref[rows, to : to + c] = ref[chip, r, :, p * c : (p + 1) * c]


def columns(pair, size, place):
    return [
        (w, pl.BlockSpec(w.shape[:3] + (size,), lambda *_: (0, 0, 0, place))) for w in pair
    ]


def normalize(values):
    centre = values - jnp.mean(values, axis=-1, keepdims=True)
    inverse = lax.rsqrt(jnp.mean(centre * centre, axis=-1, keepdims=True) + EPS)
    return centre * inverse, inverse


def normed(values, gain, bias):
    return (normalize(values)[0] * gain + bias).astype(BF)


def norm_backward(values, gain, upstream):
    normal, inverse = normalize(values)
    g = upstream * gain
    mean_g = jnp.mean(g, axis=-1, keepdims=True)
    mean_gn = jnp.mean(g * normal, axis=-1, keepdims=True)
    d_values = inverse * (g - mean_g - normal * mean_gn)
    gain_sum = jnp.sum(upstream * normal, axis=0, keepdims=True)
    return d_values, gain_sum, jnp.sum(upstream, axis=0, keepdims=True)


def head_masks(width):
    lane = lax.broadcasted_iota(jnp.int32, (1, width), 1) // HEAD_DIM
    return [lane == h for h in range(width // HEAD_DIM)]


def pick(mask, values):
    return jnp.where(mask, values, jnp.zeros_like(values))


def stacked_heads(values):
    return jnp.concatenate([pick(m, values) for m in head_masks(values.shape[1])], axis=0)


def merged_heads(values, rows):
    total = values[:rows]
    for h, mask in enumerate(head_masks(values.shape[1])):
        if h:
            total = jnp.where(mask, values[h * rows : (h + 1) * rows], total)
    return total


def softmax(scores, allowed):
    scores = jnp.where(allowed, scores, MASKED)
    weights = jnp.exp(scores - jnp.max(scores, axis=1, keepdims=True))
    return weights * (1.0 / jnp.sum(weights, axis=1, keepdims=True))


def qkv_kernel(x_ref, norm_ref, w_ref, out_ref, h_ref):
    width = out_ref.shape[3] // 3
    x = x_ref[...].reshape(-1, x_ref.shape[-1]).astype(F32)
    h = normed(x, norm_ref[0:1], norm_ref[1:2])
    h_ref[...] = h
    for k in range(3):
        result = dot(h, w_ref[k], NN).astype(BF)
        for p in range(out_ref.shape[1]):
            out_ref[0, p, :, k * width : (k + 1) * width] = result[:, p * width : (p + 1) * width]


def qkv_pieces(frames, norm, weights, slices, parts, width, deps=()):
    streams, rows, model = frames.shape
    group = streams // slices
    out = struct((slices, parts, group * rows, 3 * width))
    return call(
        qkv_kernel,
        "qkv",
        (slices,),
        [
            (frames, pl.BlockSpec((group, rows, model), lambda i: (i, 0, 0))),
            (norm, None),
            (weights, None),
        ],
        [
            (out, pl.BlockSpec((1,) + out.shape[1:], lambda i: (i, 0, 0, 0))),
            (
                struct((streams * rows, model)),
                pl.BlockSpec((group * rows, model), lambda i: (i, 0)),
            ),
        ],
        deps=deps,
        flops=2 * streams * rows * weights.size,
    )


def qkv_grad_kernel(grad_ref, w_ref, out_ref, merged_ref):
    parts, width = grad_ref.shape[1], grad_ref.shape[3] // 3
    local = parts * width
    for p in range(parts):
        for k in range(3):
            to = k * local + p * width
            merged_ref[:, to : to + width] = grad_ref[0, p, :, k * width : (k + 1) * width]
    total = 0.0
    for k in range(3):
        total += dot(merged_ref[:, k * local : (k + 1) * local], w_ref[k], NT)
    out_ref[0] = total.astype(BF)


def last_kernel(parts_ref, x_ref, dx2_ref, norm_ref, dx_ref, sums_ref):
    d_h1 = parts_ref[0].astype(F32)
    for r in range(1, parts_ref.shape[0]):
        d_h1 += parts_ref[r].astype(F32)
    d_v, gain, bias = norm_backward(x_ref[...].astype(F32), norm_ref[0:1], d_h1)
    sums_ref[0:1] = gain
    sums_ref[1:2] = bias
    d_x = (dx2_ref[...] + d_v).astype(BF)
    for r in range(dx_ref.shape[0]):
        dx_ref[r] = d_x


def causal_probs(ends_ref, stream, slots, q, k, first):
    block = q.shape[0]
    rows = first + lax.broadcasted_iota(jnp.int32, (block, 1), 0)
    begin = jnp.zeros((block, 1), jnp.int32)
    for c in range(slots):
        end = ends_ref[stream, c]
        begin = jnp.where(rows >= end, jnp.maximum(begin, end), begin)
    cols = lax.broadcasted_iota(jnp.int32, (block, k.shape[0]), 1)
    return softmax(dot(q, k, NT), (cols <= rows) & (cols >= begin))


def self_forward_kernel(ends_ref, qkv_ref, out_ref, *, slots, width, block):
    stream = pl.program_id(0)
    parts, _, rows, _ = qkv_ref.shape
    length = parts * rows
    qkv = qkv_ref[...].reshape(length, 3 * width)
    q = qkv[:, :width] * jnp.asarray(SCALE, BF)
    k = qkv[:, width : 2 * width]
    v = qkv[:, 2 * width :]
    masks = head_masks(width)
    q_of = [pick(m, q) for m in masks]
    v_of = [pick(m, v) for m in masks]
    per = block // rows
    for first in range(0, length, block):
        top = first + block
        total = jnp.zeros((block, width), F32)
        for h in range(len(masks)):
            probs = causal_probs(ends_ref, stream, slots, q_of[h][first:top], k[:top], first)
            total += dot(probs.astype(BF), v_of[h][:top], NN)
        at = first // rows
        out_ref[at : at + per, 0] = total.astype(BF).reshape(per, rows, width)


def self_backward_kernel(ends_ref, qkv_ref, grad_ref, out_ref, dk_ref, dv_ref, *, slots, width, block):
    stream = pl.program_id(0)
    parts, _, rows, _ = qkv_ref.shape
    length = parts * rows
    qkv = qkv_ref[...].reshape(length, 3 * width)
    q = qkv[:, :width] * jnp.asarray(SCALE, BF)
    k = qkv[:, width : 2 * width]
    v = qkv[:, 2 * width :]
    grad = grad_ref[...].reshape(length, width)
    masks = head_masks(width)
    q_of = [pick(m, q) for m in masks]
    k_of = [pick(m, k) for m in masks]
    g_of = [pick(m, grad) for m in masks]
    dk_ref[...] = jnp.zeros_like(dk_ref)
    dv_ref[...] = jnp.zeros_like(dv_ref)
    per = block // rows
    for first in range(0, length, block):
        top = first + block
        dq = jnp.zeros((block, width), F32)
        for h in range(len(masks)):
            q_part = q_of[h][first:top]
            g_part = g_of[h][first:top]
            probs = causal_probs(ends_ref, stream, slots, q_part, k[:top], first)
            d_probs = dot(g_part, v[:top], NT)
            delta = jnp.sum(probs * d_probs, axis=1, keepdims=True)
            d_scores = (probs * (d_probs - delta)).astype(BF)
            dq += dot(d_scores, k_of[h][:top], NN)
            dk_ref[:top] += dot(d_scores, q_part, TN)
            dv_ref[:top] += dot(probs.astype(BF), g_part, TN)
        at = first // rows
        out_ref[at : at + per, 0, :, :width] = (dq * SCALE).astype(BF).reshape(per, rows, width)
    out_ref[:, 0, :, width : 2 * width] = dk_ref[...].astype(BF).reshape(parts, rows, width)
    out_ref[:, 0, :, 2 * width :] = dv_ref[...].astype(BF).reshape(parts, rows, width)


def self_attention(ends, arrays, width, kernel, out_width, scratch, name, deps=()):
    parts, streams, rows, _ = arrays[0].shape
    length = parts * rows
    block = min(length, rows * max(1, 256 // rows))
    work = streams * (width // HEAD_DIM) * length * length

    def spec(c):
        return pl.BlockSpec((parts, 1, rows, c), lambda s, *_: (0, s, 0, 0))

    out = struct((parts, streams, rows, out_width))
    return call(
        functools.partial(kernel, slots=ends.shape[1], width=width, block=block),
        name,
        (streams,),
        [(a, spec(a.shape[3])) for a in arrays],
        [(out, spec(out_width))],
        scalars=(ends,),
        scratch=[pltpu.VMEM((length, width), F32)] * scratch,
        deps=deps,
        flops=4 * len(arrays) * work * HEAD_DIM,
        exps=work,
    )[0]


def first_kernel(device_ref, x_ref, norm_ref, near_ref, far_ref, *refs):
    pieces, (x2_ref, h2_ref, cq_ref, attn_out_ref, w_ref) = refs[:-5], refs[-5:]
    model = x2_ref.shape[1]
    assemble(w_ref, near_ref, far_ref, device_ref[0], 2)
    for j, ref in enumerate(pieces):
        piece = jnp.concatenate([ref[p] for p in range(ref.shape[0])], axis=1)
        local = piece.shape[1]
        to = pl.multiple_of((device_ref[1] ^ j) * local, local)
        attn_out_ref[:, pl.ds(to, local)] = piece
    attn = attn_out_ref[...]
    x2 = x_ref[...].astype(F32) + dot(attn, w_ref[:, :model], NT)
    x2_ref[...] = x2
    h2 = normed(x2, norm_ref[0:1], norm_ref[1:2])
    h2_ref[...] = h2
    cq_ref[...] = dot(h2, w_ref[:, model:], NN).astype(BF)


def memory_kernel(device_ref, text_ref, near_ref, far_ref, out_ref, w_ref):
    assemble(w_ref, near_ref, far_ref, device_ref[0])
    out_ref[...] = dot(text_ref[...], w_ref[...], NN).astype(BF)


def text_grad_kernel(device_ref, rows_ref, near_ref, far_ref, out_ref, w_ref):
    assemble(w_ref, near_ref, far_ref, device_ref[0], 2)
    out_ref[...] = dot(rows_ref[...], w_ref[...], NT).astype(BF)


def cross_allowed(info_ref, stream, slots, rows, keys):
    text = keys // slots
    pos = info_ref[stream, 2 * slots] + lax.broadcasted_iota(jnp.int32, (rows, 1), 0)
    clip = jnp.zeros((rows, 1), jnp.int32)
    for c in range(slots):
        clip += jnp.where(pos >= info_ref[stream, c], 1, 0)
    begin = clip * text
    count = jnp.zeros((rows, 1), jnp.int32)
    for c in range(slots):
        count = jnp.where(clip == c, info_ref[stream, slots + c], count)
    key = lax.broadcasted_iota(jnp.int32, (rows, keys), 1)
    return (key >= begin) & (key < begin + count)


CROSS_LANES = 256


def second_kernel(
    info_ref, x2_ref, cq_ref, kv_ref, norm_ref, near_ref, far_ref, *refs, slots, rows
):
    cattn_ref, x3_ref, h3_ref, wo_ref = refs
    stream = pl.program_id(0)
    model = x2_ref.shape[1]
    keys = kv_ref.shape[1]
    mine = pl.ds(pl.multiple_of(stream * rows, rows), rows)
    once = cross_allowed(info_ref, stream, slots, rows, keys)
    allowed = jnp.concatenate([once] * (CROSS_LANES // HEAD_DIM), axis=0)
    for at in range(0, model, CROSS_LANES):
        cols = slice(at, at + CROSS_LANES)
        q = stacked_heads(cq_ref[mine, cols] * jnp.asarray(SCALE, BF))
        probs = softmax(dot(q, kv_ref[0, :, cols], NT), allowed)
        result = dot(probs.astype(BF), kv_ref[0, :, model + at : model + at + CROSS_LANES], NN)
        cattn_ref[mine, cols] = merged_heads(result, rows).astype(BF)

    @pl.when(stream == pl.num_programs(0) - 1)
    def _():
        assemble(wo_ref, near_ref, far_ref, info_ref[0, 2 * slots + 1])
        x3 = x2_ref[...] + dot(cattn_ref[...], wo_ref[...], NT)
        x3_ref[...] = x3
        h3_ref[...] = normed(x3, norm_ref[0:1], norm_ref[1:2])


def third_kernel(
    info_ref,
    dh_ref,
    received_ref,
    x3_ref,
    ct_ref,
    x2_ref,
    cq_ref,
    kv_ref,
    gain_ref,
    near1_ref,
    far1_ref,
    near2_ref,
    far2_ref,
    dc_ref,
    dcq_ref,
    dx2_ref,
    da_ref,
    dattn_ref,
    dkv_ref,
    sums_ref,
    dx3_ref,
    dcattn_ref,
    w_first_ref,
    w_cross_ref,
    *,
    slots,
    rows,
):
    device = info_ref[0, 2 * slots + 1]
    stream = pl.program_id(0)
    model = x2_ref.shape[1]
    keys = kv_ref.shape[1]

    @pl.when(stream == 0)
    def _():
        d_h3 = dh_ref[...] + received_ref[...].astype(F32)
        d_v, gain, bias = norm_backward(x3_ref[...], gain_ref[2:3], d_h3)
        sums_ref[1:2] = gain
        sums_ref[3:4] = bias
        d_x3 = ct_ref[...].astype(F32) + d_v
        dx3_ref[...] = d_x3
        d_c = d_x3.astype(BF)
        dc_ref[...] = d_c
        assemble(w_cross_ref, near2_ref, far2_ref, device)
        dcattn_ref[...] = dot(d_c, w_cross_ref[...], NN).astype(BF)

    mine = pl.ds(pl.multiple_of(stream * rows, rows), rows)
    once = cross_allowed(info_ref, stream, slots, rows, keys)
    allowed = jnp.concatenate([once] * (CROSS_LANES // HEAD_DIM), axis=0)
    for at in range(0, model, CROSS_LANES):
        cols = slice(at, at + CROSS_LANES)
        k = kv_ref[0, :, cols]
        v = kv_ref[0, :, model + at : model + at + CROSS_LANES]
        q = stacked_heads(cq_ref[mine, cols] * jnp.asarray(SCALE, BF))
        grad = stacked_heads(dcattn_ref[mine, cols])
        probs = softmax(dot(q, k, NT), allowed)
        d_probs = dot(grad, v, NT)
        delta = jnp.sum(probs * d_probs, axis=1, keepdims=True)
        d_scores = (probs * (d_probs - delta)).astype(BF)
        dcq_ref[mine, cols] = (merged_heads(dot(d_scores, k, NN), rows) * SCALE).astype(BF)
        d_k = dot(d_scores, q, TN).astype(BF)
        d_v = dot(probs.astype(BF), grad, TN).astype(BF)
        dkv_ref[0, :, cols] = d_k
        dkv_ref[0, :, model + at : model + at + CROSS_LANES] = d_v

    @pl.when(stream == pl.num_programs(0) - 1)
    def _():
        assemble(w_first_ref, near1_ref, far1_ref, device, 2)
        d_h2 = dot(dcq_ref[...], w_first_ref[:, model:], NT)
        d_v, gain, bias = norm_backward(x2_ref[...], gain_ref[1:2], d_h2)
        sums_ref[0:1] = gain
        sums_ref[2:3] = bias
        d_x2 = dx3_ref[...] + d_v
        dx2_ref[...] = d_x2
        d_a = d_x2.astype(BF)
        da_ref[...] = d_a
        d_attn = dot(d_a, w_first_ref[:, :model], NN).astype(BF)
        ranks, parts, _, width = dattn_ref.shape
        for p in range(ranks * parts):
            to = (p // parts) ^ info_ref[0, 2 * slots + 2]
            dattn_ref[to, p % parts] = d_attn[:, p * width : (p + 1) * width]


def ffn_kernel(h_ref, ct_ref, *refs, groups, tiles):
    act_ref, dup_ref, dh_ref, out_ref, dh_acc, out_acc = refs[2 * groups :]
    step = pl.program_id(0)

    @pl.when(step == 0)
    def _():
        dh_acc[...] = jnp.zeros_like(dh_acc)
        out_acc[...] = jnp.zeros_like(out_acc)

    for g in range(groups):

        @pl.when(step // tiles == g)
        def _(g=g):
            w_up, w_down = refs[2 * g][...], refs[2 * g + 1][...]
            into, out_of = (NN, NT) if g else (NT, NN)
            up = dot(h_ref[...], w_up, NN)
            d_act = dot(ct_ref[...], w_down, into)
            cdf = 0.5 * (1.0 + lax.erf(up * (0.5**0.5)))
            slope = cdf + up * jnp.exp(-0.5 * up * up) * 0.3989422804014327
            act = (up * cdf).astype(BF)
            d_up = (d_act * slope).astype(BF)
            act_ref[...] = act
            dup_ref[...] = d_up
            dh_acc[...] += dot(d_up, w_up, NT)
            out_acc[...] += dot(act, w_down, out_of)

    @pl.when(step == groups * tiles - 1)
    def _():
        dh_ref[...] = dh_acc[...].astype(dh_ref.dtype)
        out_ref[...] = out_acc[...].astype(out_ref.dtype)


def feed_forward(h, ct, own, others, hidden, dtype, deps=()):
    count, model = h.shape
    groups = 1 + len(others)
    tile = min(hidden, 512)
    tiles = hidden // tile

    def place(g):
        return lambda i: jnp.clip(i - g * tiles, 0, tiles - 1)

    ins = [(h, None), (ct, None)]
    ins.append((own[0], pl.BlockSpec((model, tile), lambda i: (0, place(0)(i)))))
    ins.append((own[1], pl.BlockSpec((tile, model), lambda i: (place(0)(i), 0))))
    for g, w in enumerate(others, 1):
        for first in (0, tiles):
            spec = pl.BlockSpec((model, tile), lambda i, g=g, f=first: (0, f + place(g)(i)))
            ins.append((w, spec))
    wide = struct((count, groups * hidden))
    narrow = struct((count, model), dtype)
    column = pl.BlockSpec((count, tile), lambda i: (0, i))
    return call(
        functools.partial(ffn_kernel, groups=groups, tiles=tiles),
        "feed_forward",
        (groups * tiles,),
        ins,
        [(wide, column), (wide, column), (narrow, None), (narrow, None)],
        scratch=[pltpu.VMEM((count, model), F32)] * 2,
        deps=deps,
        flops=8 * count * model * groups * hidden,
        exps=2 * count * groups * hidden,
    )


def weight_grad_kernel(index_ref, *refs, sums, chips, plus, apart):
    outs = refs[-chips:] if apart else [refs[-1].at[j] for j in range(chips)]
    plus_ref = refs[-chips - 1 if apart else -2]
    at = 0
    for p, terms in enumerate(sums):
        total = 0.0
        for _ in range(terms):
            left = jnp.concatenate([r[...] for r in refs[at : at + chips]], axis=1)
            total += dot(left, refs[at + chips][...], TN)
            at += chips + 1
        share = total.shape[0] // chips
        for j in range(chips):
            block = total[j * share : (j + 1) * share]
            if plus:
                block += plus_ref[j, p].astype(F32)
            outs[j][p] = block.astype(BF)


def weight_grad_blocks(index, sums, share, plus=None, apart=False, deps=()):
    model = sums[0][0][0].shape[1]
    cols = sums[0][0][1][2]
    chips = model // (2 * share)
    if share % LANES:
        parts = []
        for terms in sums:
            total = 0.0
            for left, (right, first, _) in terms:
                left = left.reshape(-1, 2 * chips, share)[:, index]
                right = right[:, first : first + cols]
                total += dot(left.reshape(-1, chips * share), right, TN)
            parts.append(total.reshape(chips, share, cols))
        blocks = jnp.stack(parts, axis=1)
        blocks = (blocks if plus is None else blocks + plus.astype(F32)).astype(BF)
        return [blocks[j] for j in range(chips)] if apart else blocks
    tile = 512 if cols % 512 == 0 else cols
    ins = []
    flops = 0
    for terms in sums:
        for left, (right, first, _) in terms:
            for j in range(chips):
                ins.append((left, pl.BlockSpec((left.shape[0], share), lambda i, w, j=j: (0, w[j]))))
            spec = pl.BlockSpec(
                (right.shape[0], tile), lambda i, w, first=first: (0, first // tile + i)
            )
            ins.append((right, spec))
            flops += right.shape[0] * model * cols
    every = struct((chips, len(sums), share, cols))
    every_spec = pl.BlockSpec((chips, len(sums), share, tile), lambda i, w: (0, 0, 0, i))
    one_spec = pl.BlockSpec((len(sums), share, tile), lambda i, w: (0, 0, i))
    outs = [(every, every_spec)]
    if plus is not None:
        ins.append((plus, every_spec))
    if apart:
        outs = [(struct(every.shape[1:]), one_spec)] * chips
    result = call(
        functools.partial(
            weight_grad_kernel,
            sums=[len(terms) for terms in sums],
            chips=chips,
            plus=plus is not None,
            apart=apart,
        ),
        "weight_grad",
        (cols // tile,),
        ins,
        outs,
        scalars=(index,),
        deps=deps,
        flops=flops,
    )
    return result if apart else result[0]


def tie_kernel(*refs):
    pass


def tied(value, *first):
    anywhere = pl.BlockSpec(memory_space=pl.ANY)
    return pl.pallas_call(
        tie_kernel,
        out_shape=struct(value.shape, value.dtype),
        in_specs=[anywhere] * (1 + len(first)),
        out_specs=anywhere,
        input_output_aliases={0: 0},
        cost_estimate=pl.CostEstimate(flops=0, bytes_accessed=0, transcendentals=0),
        name="tied",
    )(value, *first)


def text_kernel(in_ref, out_ref):
    part = in_ref.shape[2]
    for i in range(in_ref.shape[0]):
        out_ref[0, i * part : (i + 1) * part] = in_ref[i, 0].astype(F32)


def shards(
    frames,
    text_states,
    clip_lengths,
    text_lengths,
    cotangent,
    norm_gain,
    norm_bias,
    self_proj,
    self_out,
    cross_query,
    cross_mem,
    cross_out,
    ffn_up,
    ffn_down,
):
    streams, rows, model = frames.shape
    slots, text = text_states.shape[1:3]
    text_rows = slots * text
    blk, tp = lax.axis_size("blk"), lax.axis_size("tp")
    b, t = lax.axis_index("blk"), lax.axis_index("tp")
    mine = streams // tp
    count = mine * rows
    core, chips = b % 2, blk // 2
    local = self_out.shape[0]
    per = min(blk // tp, local // HEAD_DIM)
    width = local // per
    slices = blk // per
    group = -(-streams // slices)
    share = model // blk
    hidden = ffn_up.shape[1]
    groups = tp // 2
    device = jnp.stack([b, t]).astype(jnp.int32)
    plane = [[2 * c + k for c in range(chips)] for k in range(2)]
    chip = b // 2
    all_chips = jnp.arange(chips, dtype=jnp.int32)
    near_chips = chip ^ jnp.arange(chips, dtype=jnp.int32)

    def swapped(size, j):
        return [(i, i ^ j) for i in range(size)]

    def of_rank(values, rank):
        return lax.dynamic_slice_in_dim(values, rank * mine, mine, 0)

    def norm_rows(i):
        return jnp.stack([norm_gain[i], norm_bias[i]])

    def at(values, i):
        return lax.dynamic_index_in_dim(values, i, 0, keepdims=False)

    def from_ranks(values):
        return [values[0]] + [
            lax.ppermute(values[j], "tp", swapped(tp, j)) for j in range(1, tp)
        ]

    def over_chips(blocks):
        return lax.all_to_all(blocks, "blk", 0, 0, axis_index_groups=plane)

    def other_core(values):
        return lax.ppermute(values, "blk", swapped(blk, 1))

    def spread(w):
        near = over_chips(jnp.broadcast_to(w, (chips,) + w.shape))
        return near, other_core(near)

    def weight_grads(sums, order, apart, deps=(), later=()):
        sums = [
            [(left, r if isinstance(r, tuple) else (r, 0, r.shape[1])) for left, r in terms]
            for terms in sums
        ]
        send = weight_grad_blocks(2 * order + 1 - core, sums, share, deps=deps)
        return weight_grad_blocks(
            2 * order + core, sums, share, other_core(send), apart=apart, deps=later
        )

    def from_chips(blocks):
        return [blocks[0]] + [
            lax.ppermute(blocks[j], "blk", swapped(blk, 2 * j)) for j in range(1, chips)
        ]

    def added(values):
        total = values[0].astype(F32)
        for v in values[1:]:
            total += v.astype(F32)
        return total

    def over_ranks(total):
        parts, _, c = total.shape
        split = total.astype(BF).reshape(parts, share, tp, c // tp).transpose(2, 0, 1, 3)
        return added(from_ranks([at(split, t ^ j) for j in range(tp)]))

    def share_rows(w):
        return lax.dynamic_slice_in_dim(w, b * share, share, w.ndim - 2)

    def share_cols(w):
        return lax.dynamic_slice_in_dim(w, b * share, share, 1).T

    mem = share_rows(cross_mem)
    shared = [mem[0], mem[1], share_cols(self_out), share_rows(cross_query), share_cols(cross_out)]
    shared = jnp.concatenate(shared, axis=1)
    piece = jnp.concatenate([share_rows(ffn_up), share_cols(ffn_down)], axis=1)

    padded = frames
    if slices * group > streams:
        padded = jnp.pad(frames, ((0, slices * group - streams), (0, 0), (0, 0)))
    pieces, h_all = qkv_pieces(
        padded, norm_rows(0), self_proj, slices, per, width, deps=(shared, piece)
    )
    qkv = lax.all_to_all(pieces.reshape(blk, group, rows, 3 * width), "blk", 0, 0)
    all_ends = jnp.cumsum(clip_lengths, axis=1).astype(jnp.int32)
    ends = of_rank(all_ends, t)
    own_ends = jnp.pad(all_ends, ((0, slices * group - streams), (0, 0)))
    own_ends = lax.dynamic_slice_in_dim(own_ends, b // per * group, group, 0)
    shared = lax.all_gather(shared, "tp")
    attn_own = self_attention(
        own_ends, [qkv], width, self_forward_kernel, width, 0, "self_forward"
    )
    even = slices == tp and group == mine

    attn_rows = lax.all_to_all(attn_own, "blk", 0, 0)
    if even:
        attn = attn_rows.reshape(tp, per, count, width)
    else:
        attn = attn_rows.reshape(slices, per, group, rows, width).transpose(0, 2, 1, 3, 4)
        attn = attn.reshape(slices * group, per, rows, width)[:streams]
        attn = attn.reshape(tp, mine, per, rows, width).transpose(0, 2, 1, 3, 4)
        attn = attn.reshape(tp, per, count, width)
    attn = from_ranks([at(attn, t ^ j) for j in range(tp)])

    weights = spread(tied(shared, *attn))
    w_mem = columns(weights, 2 * local, 0)
    w_first = columns(weights, 2 * local, 1)
    w_cross_out = columns(weights, local, 4)
    piece = tied(piece, *attn)
    pieces_of = [lax.ppermute(piece, "tp", swapped(tp, 2 * j)) for j in range(1, groups)]
    ffn_others = [
        lax.all_gather(tied(p, weights[0]), "blk", axis=0, tiled=True) for p in pieces_of
    ]

    info = jnp.concatenate(
        [
            ends,
            of_rank(text_lengths, t),
            jnp.full((mine, 1), b * rows, jnp.int32),
            jnp.full((mine, 1), b, jnp.int32),
            jnp.full((mine, 1), t, jnp.int32),
        ],
        axis=1,
    )
    x = of_rank(frames, t).reshape(count, model)
    flat = struct((count, model))
    wide = struct((count, model), F32)
    x2, h2, cq, attn = call(
        first_kernel,
        "to_cross",
        (1,),
        [
            (x, None),
            (norm_rows(1), None),
            *w_first,
            *[(a, None) for a in attn],
        ],
        [(wide, None), (flat, None), (flat, None), (flat, None)],
        scalars=(device,),
        scratch=[pltpu.VMEM((model, 2 * model), BF)],
        deps=pieces_of,
        flops=4 * count * model * model,
    )
    texts = of_rank(text_states, t).reshape(mine * text_rows, model)
    tile = model // 2
    (ckv,) = call(
        memory_kernel,
        "memory",
        (4,),
        [
            (texts, None),
            *[
                (
                    w,
                    pl.BlockSpec(
                        (chips, tp // 2, share, local), lambda i, _: (0, i % 2, 0, i // 2)
                    ),
                )
                for w in weights
            ],
        ],
        [
            (
                struct((mine * text_rows, 2 * model)),
                pl.BlockSpec((mine * text_rows, tile), lambda i, _: (0, i)),
            )
        ],
        scalars=(device,),
        scratch=[pltpu.VMEM((model, tile), BF)],
        deps=(cq,),
        flops=4 * texts.shape[0] * model * model,
    )
    ckv = ckv.reshape(mine, text_rows, 2 * model)
    kv_spec = pl.BlockSpec((1, text_rows, 2 * model), lambda s, *_: (s, 0, 0))
    cross_work = count * (model // HEAD_DIM) * text_rows
    cattn, x3, h3 = call(
        functools.partial(second_kernel, slots=slots, rows=rows),
        "cross_forward",
        (mine,),
        [
            (x2, None),
            (cq, None),
            (ckv, kv_spec),
            (norm_rows(2), None),
            *w_cross_out,
        ],
        [(flat, None), (wide, None), (flat, None)],
        scalars=(info,),
        scratch=[pltpu.VMEM((model, model), BF)],
        flops=2 * count * model * model + 4 * cross_work * HEAD_DIM,
        exps=cross_work,
    )

    swap = swapped(tp, 1)
    h3_other = lax.ppermute(h3, "tp", swap)
    ct = of_rank(cotangent, t).reshape(count, model)
    ct_other = of_rank(cotangent, t ^ 1).reshape(count, model)
    own_weights = (ffn_up, ffn_down)
    act_other, d_up_other, d_h3_other, out_other = feed_forward(
        h3_other, ct_other, own_weights, ffn_others, hidden, BF
    )
    d_h3_got = lax.ppermute(d_h3_other, "tp", swap)
    act, d_up, d_h3, out = feed_forward(
        h3, ct, own_weights, ffn_others, hidden, F32, deps=(out_other,)
    )
    out_got = lax.ppermute(tied(out_other, d_h3_got), "tp", swap)
    out = x3 + out + out_got.astype(F32)

    ffn_blocks = weight_grads(
        [[(h3, d_up), (h3_other, d_up_other)], [(ct, act), (ct_other, act_other)]],
        all_chips,
        False,
        deps=(d_h3_got,),
    )
    ffn_got = over_chips(ffn_blocks)
    g_ffn = jnp.sum(ffn_got.astype(F32), axis=0)
    split = g_ffn.reshape(2, share, groups, hidden)

    d_c, d_cq, d_x2, d_a, d_attn, d_ckv, early = call(
        functools.partial(third_kernel, slots=slots, rows=rows),
        "cross_backward",
        (mine,),
        [
            (d_h3, None),
            (d_h3_got, None),
            (x3, None),
            (ct, None),
            (x2, None),
            (cq, None),
            (ckv, kv_spec),
            (norm_gain, None),
            *w_first,
            *w_cross_out,
        ],
        [
            (flat, None),
            (flat, None),
            (wide, None),
            (flat, None),
            (struct((tp, per, count, width)), None),
            (struct(ckv.shape), kv_spec),
            (struct((4, model), F32), None),
        ],
        scalars=(info,),
        scratch=[
            pltpu.VMEM((count, model), F32),
            pltpu.VMEM((count, model), BF),
            pltpu.VMEM((model, 2 * model), BF),
            pltpu.VMEM((model, model), BF),
        ],
        deps=(ffn_blocks,),
        flops=6 * count * model * model + 10 * cross_work * HEAD_DIM,
        exps=cross_work,
    )

    d_attn = from_ranks([d_attn[j] for j in range(tp)])
    attn_blocks = weight_grads(
        [[(d_a, attn)], [(h2, d_cq)], [(d_c, cattn)]], near_chips, True, deps=(d_attn[-1],)
    )

    d_attn = jnp.stack(d_attn)[jnp.arange(tp) ^ t]
    if not even:
        d_attn = d_attn.reshape(tp, per, mine, rows, width).transpose(0, 2, 1, 3, 4)
        d_attn = d_attn.reshape(streams, per, rows, width)
        d_attn = jnp.pad(d_attn, ((0, slices * group - streams), (0, 0), (0, 0), (0, 0)))
        d_attn = d_attn.reshape(slices, group, per, rows, width).transpose(0, 2, 1, 3, 4)
    d_attn = d_attn.reshape(blk, group, rows, width)
    d_attn = lax.all_to_all(tied(d_attn, ffn_got), "blk", 0, 0)
    d_qkv_own = self_attention(
        own_ends,
        [qkv, d_attn],
        width,
        self_backward_kernel,
        3 * width,
        2,
        "self_backward",
        deps=(out_got, attn_blocks[0]),
    )
    out_all = lax.all_gather(out.astype(BF), "tp", axis=0, tiled=True)

    part = mine * text_rows // blk
    d_ckv = d_ckv.reshape(chips, 2, part, 2 * model)
    received = other_core(lax.dynamic_index_in_dim(d_ckv, 1 - core, 1, keepdims=False))
    d_ckv = lax.dynamic_index_in_dim(d_ckv, core, 1, keepdims=False).astype(F32)
    d_ckv = tied((d_ckv + received.astype(F32)).astype(BF), d_attn)
    d_ckv = jnp.sum(over_chips(d_ckv).astype(F32), axis=0).astype(BF)

    d_qkv = lax.all_to_all(tied(d_qkv_own, d_ckv), "blk", 0, 0)
    texts = lax.dynamic_slice_in_dim(texts, b * part, part, 0)
    (d_text,) = call(
        text_grad_kernel,
        "text_grad",
        (1,),
        [(d_ckv, None), *w_mem],
        [(struct((part, model)), None)],
        scalars=(device,),
        scratch=[pltpu.VMEM((model, 2 * model), BF)],
        deps=(d_qkv_own,),
        flops=4 * part * model * model,
    )
    d_text = jnp.stack(from_ranks([d_text] * tp))[jnp.arange(tp) ^ t]

    d_qkv = d_qkv.reshape(slices, per, group * rows, 3 * width)
    padded_rows = slices * group * rows
    parts, d_qkv = call(
        qkv_grad_kernel,
        "qkv_grad",
        (slices,),
        [
            (d_qkv, pl.BlockSpec((1,) + d_qkv.shape[1:], lambda i: (i, 0, 0, 0))),
            (self_proj, None),
        ],
        [
            (
                struct((slices, group * rows, model)),
                pl.BlockSpec((1, group * rows, model), lambda i: (i, 0, 0)),
            ),
            (
                struct((padded_rows, 3 * local)),
                pl.BlockSpec((group * rows, 3 * local), lambda i: (i, 0)),
            ),
        ],
        deps=(d_text,),
        flops=6 * padded_rows * model * local,
    )
    parts_own = parts.reshape(padded_rows, model)[: streams * rows].reshape(tp, count, model)
    parts = lax.all_to_all(parts_own, "tp", 0, 0)
    qkv_blocks = weight_grads(
        [[(h_all, d_qkv)]], near_chips, True, deps=(parts_own,)
    )
    qkv_got = from_chips(qkv_blocks)
    mem_blocks = weight_grads(
        [[(texts, (d_ckv, 0, model))], [(texts, (d_ckv, model, model))]],
        near_chips,
        True,
        deps=(parts_own,),
    )
    mem_got = from_chips(mem_blocks)
    attn_got = from_chips([tied(w, d_qkv) for w in attn_blocks])

    d_x, late = call(
        last_kernel,
        "to_frames",
        (1,),
        [(parts, None), (x, None), (d_x2, None), (norm_rows(0), None)],
        [(struct((tp, count, model)), None), (struct((2, model), F32), None)],
        deps=(*attn_got[1:], qkv_blocks[0], mem_blocks[0]),
        flops=20 * count * model,
    )
    grad_frames = lax.all_to_all(d_x, "tp", 0, 0).reshape(streams, rows, model).astype(F32)

    ffn_total = split[:, :, 0]
    ffn_back = [
        lax.ppermute(tied(split[:, :, j].astype(BF), d_x), "tp", swapped(tp, 2 * j)) for j in range(1, groups)
    ]
    for back in ffn_back:
        ffn_total += back.astype(F32)
    grad_ffn_up = ffn_total[0]
    grad_ffn_down = ffn_total[1].T
    g_attn_own = over_ranks(tied(added(attn_got), d_x))
    grad_cross_mem = over_ranks(added(mem_got))
    grad_self_out = g_attn_own[0].T
    grad_cross_query = g_attn_own[1]
    grad_cross_out = g_attn_own[2].T
    (g_qkv,) = added(qkv_got)
    grad_self_proj = g_qkv.reshape(share, 3, local).transpose(1, 0, 2)

    d_text = lax.all_gather(d_text, "blk")
    if part % 16:
        d_text = d_text.transpose(1, 0, 2, 3)
        grad_text = d_text.reshape(streams, slots, text, model).astype(F32)
    else:
        (grad_text,) = call(
            text_kernel,
            "text_out",
            (tp,),
            [(d_text, pl.BlockSpec((blk, 1, part, model), lambda i: (0, i, 0, 0)))],
            [
                (
                    struct((tp, mine * text_rows, model), F32),
                    pl.BlockSpec((1, mine * text_rows, model), lambda i: (i, 0, 0)),
                )
            ],
        )
        grad_text = grad_text.reshape(streams, slots, text, model)

    sums = jnp.concatenate([early, late], axis=0)
    for axis, size in (("blk", blk), ("tp", tp)):
        step = 1
        while step < size:
            sums = sums + lax.ppermute(sums, axis, swapped(size, step))
            step *= 2
    sums = lax.dynamic_slice_in_dim(sums, b * share, share, 1)
    grad_gain = jnp.stack([sums[4], sums[0], sums[1]])
    grad_bias = jnp.stack([sums[5], sums[2], sums[3]])

    out_frames = out_all.reshape(streams, rows, model).astype(F32)

    return (
        out_frames,
        grad_frames,
        grad_text,
        grad_gain,
        grad_bias,
        grad_self_proj,
        grad_self_out,
        grad_cross_query,
        grad_cross_mem,
        grad_cross_out,
        grad_ffn_up,
        grad_ffn_down,
    )


def solution(mesh):
    in_specs = (
        P(None, "blk", None),
        P(),
        P(),
        P(),
        P(None, "blk", None),
        P(),
        P(),
        P(None, None, "tp"),
        P("tp", None),
        P(None, "tp"),
        P(None, None, "tp"),
        P("tp", None),
        P(None, "tp"),
        P("tp", None),
    )
    out_specs = (
        P(None, "blk", None),
        P(None, "blk", None),
        P(),
        P(None, "blk"),
        P(None, "blk"),
        P(None, "blk", "tp"),
        P("tp", "blk"),
        P("blk", "tp"),
        P(None, "blk", "tp"),
        P("tp", "blk"),
        P("blk", "tp"),
        P("tp", "blk"),
    )
    return jax.shard_map(shards, mesh=mesh, in_specs=in_specs, out_specs=out_specs, check_vma=False)
```

time: 860 us -> 664 us (0.77)
  waiting for transfers between devices: 432 us -> 220 us
  Pallas kernels: 58.5 us -> 176 us
  matrix products: 82.6 us -> 0 us
  blocking collectives: 134 us -> 61.7 us
  starting transfers between devices: 20.8 us -> 80.6 us
    reduce_scatter x6 -> x0, waiting for transfers between devices: 180 us -> none  [the longest x3 133 us: over_frames(): return lax.psum_scatter(joined, 'blk', scatter_dimension=0, tiled=True)]
    all_gather x7 -> x4, waiting for transfers between devices: 127 us -> 0.03 us  [the longest x1 0.02 us: shards(): out_all = lax.all_gather(out.astype(BF), 'tp', axis=0, tiled=True)]
    ppermute x5 -> x40, waiting for transfers between devices: 49 us -> 174 us  [the longest x15 63.7 us: from_ranks(): lax.ppermute(values[j], 'tp', swapped(tp, j))]
    pallas_call x4 -> x34, Pallas kernels: 58.5 us -> 176 us  [the longest x21 176 us: call(): pl.pallas_call(body, out_shape=[o for o, _ in outs], grid_spec=pltpu.Pref...]
    dot_general x21 -> x0, matrix products: 82.6 us -> none  [dot(): return lax.dot_general(a, b, (dims, ((), ())), preferred_element_type=F32)]
    psum x1 -> x0, blocking collectives: 74.7 us -> none  [shards(): lax.psum(jnp.stack([gain1, gain2, gain3, bias1, bias2, bias3]), ('blk', '...]
    all_to_all x1, blocking collectives: 14.1 us -> 61.7 us  [over_chips(): return lax.all_to_all(blocks, 'blk', 0, 0, axis_index_groups=plane)]
    all_gather x2 -> x0, blocking collectives: 45 us -> none  [the longest x1 27.1 us: shards(): lax.all_gather(first, 'tp').transpose(1, 0, 2)]
  transfers between devices with their start and end apart: 21 -> 52, of which waited for: 17 -> 23; matrix products, arithmetic and copies ran while one was open for 19% -> 12% of each run, Pallas kernels for 4% -> 20%
where the time goes in v2:
time: 664 us; the launch traced here: 657 us
  waiting for transfers between devices  220 us (33%)
  Pallas kernels  176 us (27%)
  starting transfers between devices  80.6 us (12%)
  local copies, waits for them, and re-layouts  62.2 us (9%)
  blocking collectives  61.7 us (9%)
  other arithmetic  41.1 us (6%)
  between operations  14.8 us (2%)
    pallas_call x21, Pallas kernels, call(): pl.pallas_call(body, out_shape=[o for o, _ in outs], grid_spec=pltpu.Pref...  176 us
    ppermute x15, waiting for transfers between devices, from_ranks(): lax.ppermute(values[j], 'tp', swapped(tp, j))  63.7 us
    all_to_all x1, blocking collectives, over_chips(): return lax.all_to_all(blocks, 'blk', 0, 0, axis_index_groups=plane)  61.7 us
    ppermute x9, waiting for transfers between devices, from_chips(): lax.ppermute(blocks[j], 'blk', swapped(blk, 2 * j))  41.2 us
    unnamed x80, local copies, waits for them, and re-layouts  27.7 us
    all_to_all x1, waiting for transfers between devices, shards(): lax.all_to_all(pieces.reshape(blk, group, rows, 3 * width), 'blk', 0, 0)  23.6 us
    ppermute x5, waiting for transfers between devices, shards(): sums = sums + lax.ppermute(sums, axis, swapped(size, step))  22.6 us
    ppermute x15, starting transfers between devices, from_ranks(): lax.ppermute(values[j], 'tp', swapped(tp, j))  22.3 us
  transfers between devices with their start and end apart: 52, of which 23 were waited for; matrix products, arithmetic and copies ran while one was open for 12% of the time, Pallas kernels for 20%

profile of v2, /device:TPU:0, one launch (start us, length us, event | category | flops | bytes accessed | tf_op | source)
XLA Modules:
  0.0 656.7 jit_solution(7041549862133516084)
XLA Ops:
  14.6 6.8 %qkv.1 = (bf16[4,2,320,384]{3,2,1,0:T(8,128)(2,1)}, bf16[1280,1024]{1,0:T(8,128)(2,1)}) custom-call(bf16[20,64,1024]{2,1,0:T(8,128)(2,1)} %refs_0_.1, f32[2,1024]{1,0:T(2,128)} %pad_maximum_fusion.5.refs_1_.refs_3_, bf16[3,1024,256]{2,1,0:T(8,128)(2,1)} %refs_1_.1, bf16[128,1280]{1,0:T(8,128)(2,1)} %copy-done.23, ...), custom_call_target="tpu_custom_call" | custom-call | flops 2013265920 | bytes 8790016 | tf_op jit(solution)/shard_map/qkv/pallas_call | solution.py:43
  21.4 5.3 all-to-all-start
  28.3 23.6 %all-to-all-done.refs_1_ = bf16[8,5,64,384]{3,2,1,0:T(8,128)(2,1)S(1)} async-done(((bf16[8,5,64,384]{3,2,1,0:T(8,128)(2,1)}), bf16[8,5,64,384]{3,2,1,0:T(8,128)(2,1)S(1)}, u32[]{:S(2)}, u32[]{:S(2)}) %all-to-all-start) | async-done | bytes 1966112 | tf_op jit(solution)/shard_map/all_to_all | solution.py:703
  53.3 8.6 %self_forward.1 = bf16[8,5,64,128]{3,2,1,0:T(8,128)(2,1)} custom-call(s32[5,2]{1,0:T(8,128)} %get-tuple-element.169.refs_0_, bf16[8,5,64,384]{3,2,1,0:T(8,128)(2,1)} %copy-done.4), custom_call_target="tpu_custom_call" | custom-call | flops 671088640 | bytes 2621440 | tf_op jit(solution)/shard_map/self_forward/pallas_call | solution.py:43
  61.9 3.5 all-to-all-start.1
  65.5 11.1 %all-to-all-done.1 = bf16[8,5,64,128]{3,2,1,0:T(8,128)(2,1)S(1)} async-done(((bf16[8,5,64,128]{3,2,1,0:T(8,128)(2,1)}), bf16[8,5,64,128]{3,2,1,0:T(8,128)(2,1)S(1)}, u32[]{:S(2)}, u32[]{:S(2)}) %all-to-all-start.1) | async-done | bytes 655392 | tf_op jit(solution)/shard_map/all_to_all | solution.py:714
  78.8 2.6 collective-permute-start.1
  83.5 7.8 %collective-permute-done.1.refs_3_.refs_7_ = bf16[2,320,128]{2,1,0:T(8,128)(2,1)S(1)} collective-permute-done((bf16[2,320,128]{2,1,0:T(8,128)(2,1)S(1)}, bf16[2,320,128]{2,1,0:T(8,128)(2,1)S(1)}, u32[]{:S(2)}, u32[]{:S(2)}) %collective-permute-start.1) | collective-permute-done | bytes 163872 | tf_op jit(solution)/shard_map/ppermute | solution.py:647
  93.9 61.7 %all_to_all.45.refs_3_.refs_2_.refs_5_.refs_1_.refs_9_.refs_11_ = bf16[4,4,128,1280]{3,2,1,0:T(8,128)(2,1)} all-to-all(bf16[4,4,128,1280]{3,2,1,0:T(8,128)(2,1)S(1)} %broadcast_in_dim.17), channel_id=1, replica_groups={{0,8,16,24},{4,12,20,28},{1,9,17,25},{5,13,21,29},{2,10,18,26},{6,14,22..., dimensions={0} | all-to-all | bytes 10485760 | tf_op jit(solution)/shard_map/all_to_all | solution.py:651
  155.6 5.0 collective-permute-start.4
  163.8 20.8 %collective-permute-done.4.refs_9_.refs_0_ = bf16[128,2048]{1,0:T(8,128)(2,1)S(1)} collective-permute-done((bf16[128,2048]{1,0:T(8,128)(2,1)}, bf16[128,2048]{1,0:T(8,128)(2,1)S(1)}, u32[]{:S(2)}, u32[]{:S(2)}) %collective-permute-start.4) | collective-permute-done | bytes 524320 | tf_op jit(solution)/shard_map/ppermute | solution.py:729
  185.4 6.5 to_cross.1
  193.5 2.5 constant_dynamic-slice_fusion.13
  196.0 7.6 %memory.1 = bf16[640,2048]{1,0:T(8,128)(2,1)} custom-call(s32[2]{0:T(128)} %pad_add_fusion.refs_0_, bf16[640,1024]{1,0:T(8,128)(2,1)} %bitcast.140, bf16[4,4,128,1280]{3,2,1,0:T(8,128)(2,1)} %all_to_all.45.refs_3_.refs_2_.refs_5_.refs_1_.refs_9_.refs_11_, bf16[4,4,128,1280]{3,2,1,0:T(8,128)(2,1)} %collective-permute-done.3.refs_4_.refs_3_.refs_6_.refs_10_.refs_12_, ...), custom_call_target="tpu_custom_call" | custom-call | flops 2684354560 | bytes 14417920 | tf_op jit(solution)/shard_map/memory/pallas_call | solution.py:43
  203.5 12.0 %cross_forward.1 = (bf16[320,1024]{1,0:T(8,128)(2,1)}, f32[320,1024]{1,0:T(8,128)}, bf16[320,1024]{1,0:T(8,128)(2,1)}) custom-call(s32[5,7]{1,0:T(8,128)} %concatenate.12.refs_0_, f32[320,1024]{1,0:T(8,128)} %get-tuple-element.53.refs_1_.refs_5_, bf16[320,1024]{1,0:T(8,128)(2,1)} %get-tuple-element.54.refs_4_.refs_2_.refs_6_, ...), custom_call_target="tpu_custom_call" | custom-call | flops 838860800 | bytes 17702912 | tf_op jit(solution)/shard_map/cross_forward/pallas_call | solution.py:43
  216.8 15.6 %collective-permute-done.5.refs_0_.refs_6_.refs_7_.refs_8_.refs_9_ = bf16[320,1024]{1,0:T(8,128)(2,1)S(1)} collective-permute-done((bf16[320,1024]{1,0:T(8,128)(2,1)}, bf16[320,1024]{1,0:T(8,128)(2,1)S(1)}, u32[]{:S(2)}, u32[]{:S(2)}) %collective-permute-start.5) | collective-permute-done | bytes 655392 | tf_op jit(solution)/shard_map/ppermute | solution.py:814
  233.2 11.6 %feed_forward.2 = (bf16[320,2048]{1,0:T(8,128)(2,1)}, bf16[320,2048]{1,0:T(8,128)(2,1)}, bf16[320,1024]{1,0:T(8,128)(2,1)}, bf16[320,1024]{1,0:T(8,128)(2,1)}) custom-call(bf16[320,1024]{1,0:T(8,128)(2,1)} %copy-done.2, bf16[320,1024]{1,0:T(8,128)(2,1)} %bitcast.125, bf16[1024,1024]{1,0:T(8,128)(2,1)} %refs_2_.5, bf16[1024,1024]{1,0:T(8,128)(2,1)} %refs_3_.3, ...), custom_call_target="tpu_custom_call" | custom-call | flops 5368709120 | bytes 17825792 | tf_op jit(solution)/shard_map/feed_forward/pallas_call | solution.py:43
  245.6 12.1 %feed_forward.3 = (bf16[320,2048]{1,0:T(8,128)(2,1)}, bf16[320,2048]{1,0:T(8,128)(2,1)}, f32[320,1024]{1,0:T(8,128)}, f32[320,1024]{1,0:T(8,128)}) custom-call(bf16[320,1024]{1,0:T(8,128)(2,1)} %get-tuple-element.56.refs_0_.refs_1_.refs_2_.refs_3_.refs_4_, bf16[320,1024]{1,0:T(8,128)(2,1)} %bitcast.115, bf16[1024,1024]{1,0:T(8,128)(2,1)} %refs_2_.5, ...), custom_call_target="tpu_custom_call" | custom-call | flops 5368709120 | bytes 19136512 | tf_op jit(solution)/shard_map/feed_forward/pallas_call | solution.py:43
  257.7 3.1 collective-permute-done.6.refs_1_.refs_21_.refs_2_
  261.6 9.2 %weight_grad.8 = bf16[4,2,128,2048]{3,2,1,0:T(8,128)(2,1)} custom-call(s32[4]{0:T(128)} %add_subtract_fusion.1.refs_0_, bf16[320,1024]{1,0:T(8,128)(2,1)} %get-tuple-element.56.refs_0_.refs_1_.refs_2_.refs_3_.refs_4_, bf16[320,1024]{1,0:T(8,128)(2,1)} %get-tuple-element.56.refs_0_.refs_1_.refs_2_.refs_3_.refs_4_, ...), custom_call_target="tpu_custom_call" | custom-call | flops 2684354560 | bytes 19922944 | tf_op jit(solution)/shard_map/weight_grad/pallas_call | solution.py:43
  271.5 6.8 %collective-permute-done.8.refs_21_ = bf16[4,2,128,2048]{3,2,1,0:T(8,128)(2,1)S(1)} collective-permute-done((bf16[4,2,128,2048]{3,2,1,0:T(8,128)(2,1)}, bf16[4,2,128,2048]{3,2,1,0:T(8,128)(2,1)S(1)}, u32[]{:S(2)}, u32[]{:S(2)}) %collective-permute-start.8) | collective-permute-done | bytes 4194336 | tf_op jit(solution)/shard_map/ppermute | solution.py:654
  280.3 10.1 %weight_grad.9.refs_13_ = bf16[4,2,128,2048]{3,2,1,0:T(8,128)(2,1)} custom-call(s32[4]{0:T(128)} %fusion.9.refs_0_, bf16[320,1024]{1,0:T(8,128)(2,1)} %get-tuple-element.56.refs_0_.refs_1_.refs_2_.refs_3_.refs_4_, bf16[320,1024]{1,0:T(8,128)(2,1)} %get-tuple-element.56.refs_0_.refs_1_.refs_2_.refs_3_.refs_4_, ...), custom_call_target="tpu_custom_call" | custom-call | flops 2684354560 | bytes 24117248 | tf_op jit(solution)/shard_map/weight_grad/pallas_call | solution.py:43
  290.4 4.9 all-to-all-start.3
  296.3 22.9 %cross_backward.1 = (bf16[320,1024]{1,0:T(8,128)(2,1)}, bf16[320,1024]{1,0:T(8,128)(2,1)}, f32[320,1024]{1,0:T(8,128)}, bf16[320,1024]{1,0:T(8,128)(2,1)}, bf16[...) custom-call(s32[5,7]{1,0:T(8,128)} %concatenate.12.refs_0_, ...), custom_call_target="tpu_custom_call" | custom-call | flops 2432696320 | bytes 36073472 | tf_op jit(solution)/shard_map/cross_backward/pallas_call | solution.py:43
  322.1 6.2 collective-permute-done.11.refs_16_
  329.0 5.7 weight_grad.10
  339.2 3.0 collective-permute-start.9
  342.2 6.5 collective-permute-done.9
  348.8 11.6 %collective-permute-done.10 = bf16[2,320,128]{2,1,0:T(8,128)(2,1)S(1)} collective-permute-done((bf16[2,320,128]{2,1,0:T(8,128)(2,1)S(1)}, bf16[2,320,128]{2,1,0:T(8,128)(2,1)S(1)}, u32[]{:S(2)}, u32[]{:S(2)}) %collective-permute-start.10) | collective-permute-done | bytes 163872 | tf_op jit(solution)/shard_map/ppermute | solution.py:647
  362.9 3.8 all-to-all-start.4
  366.7 2.9 fusion.refs_0_
  369.6 8.3 %all-to-all-done.4.refs_2_.refs_1_ = bf16[8,5,64,128]{3,2,1,0:T(8,128)(2,1)S(1)} async-done(((bf16[8,5,64,128]{3,2,1,0:T(8,128)(2,1)}), bf16[8,5,64,128]{3,2,1,0:T(8,128)(2,1)S(1)}, u32[]{:S(2)}, u32[]{:S(2)}) %all-to-all-start.4) | async-done | bytes 655392 | tf_op jit(solution)/shard_map/all_to_all | solution.py:887
  378.7 3.5 all-to-all-start.5
  382.8 6.1 weight_grad.11
  388.9 16.5 %self_backward.1.refs_4_ = bf16[8,5,64,384]{3,2,1,0:T(8,128)(2,1)} custom-call(s32[5,2]{1,0:T(8,128)} %get-tuple-element.169.refs_0_, bf16[8,5,64,384]{3,2,1,0:T(8,128)(2,1)} %copy-done.4, bf16[8,5,64,128]{3,2,1,0:T(8,128)(2,1)} %copy-done.5, bf16[320,1024]{1,0:T(8,128)(2,1)} %copy-done.13, bf16[3,128,1024]{2,1,0:T(8,128)(2,1)} %get-tuple-element.72.refs_4_.refs_0_), custom_call_target="tpu_custom_call" | custom-call | flops 1342177280 | bytes 4587520 | tf_op jit(solution)/shard_map/self_backward/pallas_call | solution.py:43
  405.4 3.0 copy.155.refs_0_
  409.4 4.2 all-to-all-start.6
  413.6 5.3 text_grad.1
  419.0 4.4 collective-permute-start.16
  423.4 3.6 collective-permute-done.14
  427.0 7.2 %collective-permute-done.15 = bf16[80,1024]{1,0:T(8,128)(2,1)S(1)} collective-permute-done((bf16[80,1024]{1,0:T(8,128)(2,1)}, bf16[80,1024]{1,0:T(8,128)(2,1)S(1)}, u32[]{:S(2)}, u32[]{:S(2)}) %collective-permute-start.15) | collective-permute-done | bytes 163872 | tf_op jit(solution)/shard_map/ppermute | solution.py:647
  440.1 5.9 qkv_grad.1
  446.0 3.7 all-to-all-start.7
  451.3 3.7 weight_grad.14
  454.9 4.8 weight_grad.12
  463.7 4.8 weight_grad.13
  468.6 4.0 weight_grad.15
  472.5 22.7 %collective-permute-done.19.refs_6_ = bf16[3,128,1024]{2,1,0:T(8,128)(2,1)S(1)} collective-permute-done((bf16[3,128,1024]{2,1,0:T(8,128)(2,1)}, bf16[3,128,1024]{2,1,0:T(8,128)(2,1)S(1)}, u32[]{:S(2)}, u32[]{:S(2)}) %collective-permute-start.19) | collective-permute-done | bytes 786464 | tf_op jit(solution)/shard_map/ppermute | solution.py:672
  495.2 16.1 %collective-permute-done.18.refs_5_ = bf16[3,128,1024]{2,1,0:T(8,128)(2,1)} collective-permute-done((bf16[3,128,1024]{2,1,0:T(8,128)(2,1)}, bf16[3,128,1024]{2,1,0:T(8,128)(2,1)}, u32[]{:S(2)}, u32[]{:S(2)}) %collective-permute-start.18) | collective-permute-done | bytes 786464 | tf_op jit(solution)/shard_map/ppermute | solution.py:672
  512.8 5.1 to_frames.1
  517.9 4.9 all-to-all-start.8
  522.8 4.8 convert.10
  531.0 4.5 convert_reduce_fusion
  535.5 2.9 copy.105
  543.0 2.5 copy.125
  547.6 3.3 convert_add_fusion.1.refs_0_
  554.9 2.4 add_convert_fusion.1
  575.0 16.8 %collective-permute-done.37 = bf16[2,128,256]{2,1,0:T(8,128)(2,1)} collective-permute-done((bf16[2,128,256]{2,1,0:T(8,128)(2,1)}, bf16[2,128,256]{2,1,0:T(8,128)(2,1)}, u32[]{:S(2)}, u32[]{:S(2)}) %collective-permute-start.37) | collective-permute-done | bytes 131104 | tf_op jit(solution)/shard_map/ppermute | solution.py:647
  595.9 2.4 convert_element_type.131
  603.6 2.4 collective-permute-start.30
  606.1 2.4 collective-permute-start.32
  608.5 22.1 %collective-permute-done.26 = f32[6,1024]{1,0:T(8,128)S(1)} collective-permute-done((f32[6,1024]{1,0:T(8,128)S(1)}, f32[6,1024]{1,0:T(8,128)S(1)}, u32[]{:S(2)}, u32[]{:S(2)}) %collective-permute-start.26) | collective-permute-done | bytes 24608 | tf_op jit(solution)/shard_map/ppermute | solution.py:1010
  639.7 7.0 %text_out.1 = f32[4,640,1024]{2,1,0:T(8,128)} custom-call(bf16[8,4,80,1024]{3,2,1,0:T(8,128)(2,1)} %bitcast.146), custom_call_target="tpu_custom_call" | custom-call | bytes 15728640 | tf_op jit(solution)/shard_map/text_out/pallas_call | solution.py:43
  646.7 3.0 convert.12
  (227 shorter events, 106.3 us)
Async XLA Ops:
  7.2 185.5 %copy-start = (s32[20,2]{0,1:T(2,128)S(1)}, s32[20,2]{0,1:T(2,128)}, u32[]{:S(2)}) copy-start(s32[20,2]{0,1:T(2,128)} %param.17) | copy-start | bytes 484
  7.2 4.1 copy-start.25
  7.2 4.1 copy-start.27
  21.4 6.1 copy-start.28
  21.4 30.5 %all-to-all-start = ((bf16[8,5,64,384]{3,2,1,0:T(8,128)(2,1)}), bf16[8,5,64,384]{3,2,1,0:T(8,128)(2,1)S(1)}, u32[]{:S(2)}, u32[]{:S(2)}) async-start(bf16[8,5,64,384]{3,2,1,0:T(8,128)(2,1)} %bitcast.152), calls=%async_computation | async-start | bytes 3932160 | tf_op jit(solution)/shard_map/all_to_all | solution.py:703
  26.7 55.0 %all-gather.11.cloned.1.call-start = ((), (), s32[]{:S(2)}) async-start(), calls=%async_computation.11 | async-start | bytes 1638400 | tf_op jit(solution)/shard_map/all_gather | solution.py:708
  61.9 14.6 %all-to-all-start.1 = ((bf16[8,5,64,128]{3,2,1,0:T(8,128)(2,1)}), bf16[8,5,64,128]{3,2,1,0:T(8,128)(2,1)S(1)}, u32[]{:S(2)}, u32[]{:S(2)}) async-start(bf16[8,5,64,128]{3,2,1,0:T(8,128)(2,1)} %self_forward.1), calls=%async_computation.1 | async-start | bytes 1310720 | tf_op jit(solution)/shard_map/all_to_all | solution.py:714
  77.2 6.2 collective-permute-start
  78.8 12.5 %collective-permute-start.1 = (bf16[2,320,128]{2,1,0:T(8,128)(2,1)S(1)}, bf16[2,320,128]{2,1,0:T(8,128)(2,1)S(1)}, u32[]{:S(2)}, u32[]{:S(2)}) collective-permute-start(bf16[2,320,128]{2,1,0:T(8,128)(2,1)S(1)} %get-tuple-element.153), channel_id=1, source_target_pairs={{0,2},{1,3},{2,0},{3,1},{4,6},{5,7},{6,4},{7,5},{8,10},{9,11},{10,... | collective-permute-start | bytes 491528 | tf_op jit(solution)/shard_map/ppermute | solution.py:647
  81.4 9.9 %collective-permute-start.2 = (bf16[2,320,128]{2,1,0:T(8,128)(2,1)S(1)}, bf16[2,320,128]{2,1,0:T(8,128)(2,1)S(1)}, u32[]{:S(2)}, u32[]{:S(2)}) collective-permute-start(bf16[2,320,128]{2,1,0:T(8,128)(2,1)S(1)} %get-tuple-element.152), channel_id=1, source_target_pairs={{0,3},{1,2},{2,1},{3,0},{4,7},{5,6},{6,5},{7,4},{8,11},{9,10},{10,... | collective-permute-start | bytes 491528 | tf_op jit(solution)/shard_map/ppermute | solution.py:647
  83.5 7.8 %copy-start.16 = (bf16[2,320,128]{2,1,0:T(8,128)(2,1)}, bf16[2,320,128]{2,1,0:T(8,128)(2,1)S(1)}, u32[]{:S(2)}) copy-start(bf16[2,320,128]{2,1,0:T(8,128)(2,1)S(1)} %collective-permute-done.refs_2_.refs_6_) | copy-start | bytes 491524
  155.6 29.0 %collective-permute-start.3 = (bf16[4,4,128,1280]{3,2,1,0:T(8,128)(2,1)}, bf16[4,4,128,1280]{3,2,1,0:T(8,128)(2,1)}, u32[]{:S(2)}, u32[]{:S(2)}) collective-permute-start(bf16[4,4,128,1280]{3,2,1,0:T(8,128)(2,1)} %all_to_all.45.refs_3_.refs_2_.refs_5_.refs_1_.refs_9_.refs_11_), channel_id=1, source_target_pairs={{0,4},{4,0},{8,12},{12,8},{16,20},{20,16},{24,28},{28,24},{1,5},{5... | collective-permute-start | bytes 15728648 | tf_op jit(solution)/shard_map/ppermute | solution.py:654
  155.6 29.0 %collective-permute-start.4 = (bf16[128,2048]{1,0:T(8,128)(2,1)}, bf16[128,2048]{1,0:T(8,128)(2,1)S(1)}, u32[]{:S(2)}, u32[]{:S(2)}) collective-permute-start(bf16[128,2048]{1,0:T(8,128)(2,1)} %tied.14), channel_id=1, source_target_pairs={{0,2},{1,3},{2,0},{3,1},{4,6},{5,7},{6,4},{7,5},{8,10},{9,11},{10,... | collective-permute-start | bytes 1572872 | tf_op jit(solution)/shard_map/ppermute | solution.py:729
  191.9 40.4 %all-gather.7.cloned.1.call-start = ((), (), s32[]{:S(2)}) async-start(), calls=%async_computation.9 | async-start | bytes 4718592 | tf_op jit(solution)/shard_map/all_gather | solution.py:731
  203.5 12.0 %copy-start.21 = (bf16[20,64,1024]{2,1,0:T(8,128)(2,1)S(1)}, bf16[20,64,1024]{2,1,0:T(8,128)(2,1)}, u32[]{:S(2)}) copy-start(bf16[20,64,1024]{2,1,0:T(8,128)(2,1)} %param.18) | copy-start | bytes 7864324
  215.5 16.8 %collective-permute-start.5 = (bf16[320,1024]{1,0:T(8,128)(2,1)}, bf16[320,1024]{1,0:T(8,128)(2,1)S(1)}, u32[]{:S(2)}, u32[]{:S(2)}) collective-permute-start(bf16[320,1024]{1,0:T(8,128)(2,1)} %get-tuple-element.56.refs_0_.refs_1_.refs_2_.refs_3_.refs_4_), channel_id=1, source_target_pairs={{0,1},{1,0},{2,3},{3,2},{4,5},{5,4},{6,7},{7,6},{8,9},{9,8},{10,11... | collective-permute-start | bytes 1966088 | tf_op jit(solution)/shard_map/ppermute | solution.py:814
  244.8 16.0 %collective-permute-start.6 = (bf16[320,1024]{1,0:T(8,128)(2,1)}, bf16[320,1024]{1,0:T(8,128)(2,1)S(1)}, u32[]{:S(2)}, u32[]{:S(2)}) collective-permute-start(bf16[320,1024]{1,0:T(8,128)(2,1)} %get-tuple-element.59), channel_id=1, source_target_pairs={{0,1},{1,0},{2,3},{3,2},{4,5},{5,4},{6,7},{7,6},{8,9},{9,8},{10,11... | collective-permute-start | bytes 1966088 | tf_op jit(solution)/shard_map/ppermute | solution.py:821
  270.9 7.4 %collective-permute-start.8 = (bf16[4,2,128,2048]{3,2,1,0:T(8,128)(2,1)}, bf16[4,2,128,2048]{3,2,1,0:T(8,128)(2,1)S(1)}, u32[]{:S(2)}, u32[]{:S(2)}) collective-permute-start(bf16[4,2,128,2048]{3,2,1,0:T(8,128)(2,1)} %weight_grad.8), channel_id=1, source_target_pairs={{0,4},{4,0},{8,12},{12,8},{16,20},{20,16},{24,28},{28,24},{1,5},{5... | collective-permute-start | bytes 12582920 | tf_op jit(solution)/shard_map/ppermute | solution.py:654
  290.4 72.5 %all-to-all-start.3 = ((bf16[4,2,128,2048]{3,2,1,0:T(8,128)(2,1)}), bf16[4,2,128,2048]{3,2,1,0:T(8,128)(2,1)}, u32[]{:S(2)}, u32[]{:S(2)}) async-start(bf16[4,2,128,2048]{3,2,1,0:T(8,128)(2,1)} %weight_grad.9.refs_13_), calls=%async_computation.3 | async-start | bytes 8388608 | tf_op jit(solution)/shard_map/all_to_all | solution.py:651
  295.4 227.4 %all-gather.9.cloned.1.call-start = ((), (), s32[]{:S(2)}) async-start(), calls=%async_computation.10 | async-start | bytes 3276800 | tf_op jit(solution)/shard_map/all_gather | solution.py:898
  295.6 39.1 %collective-permute-start.7 = (bf16[320,1024]{1,0:T(8,128)(2,1)}, bf16[320,1024]{1,0:T(8,128)(2,1)S(1)}, u32[]{:S(2)}, u32[]{:S(2)}) collective-permute-start(bf16[320,1024]{1,0:T(8,128)(2,1)} %tied.16), channel_id=1, source_target_pairs={{0,1},{1,0},{2,3},{3,2},{4,5},{5,4},{6,7},{7,6},{8,9},{9,8},{10,11... | collective-permute-start | bytes 1966088 | tf_op jit(solution)/shard_map/ppermute | solution.py:825
  320.4 7.9 %collective-permute-start.11 = (bf16[2,320,128]{2,1,0:T(8,128)(2,1)S(1)}, bf16[2,320,128]{2,1,0:T(8,128)(2,1)S(1)}, u32[]{:S(2)}, u32[]{:S(2)}) collective-permute-start(bf16[2,320,128]{2,1,0:T(8,128)(2,1)S(1)} %get-tuple-element.149), channel_id=1, source_target_pairs={{0,3},{1,2},{2,1},{3,0},{4,7},{5,6},{6,5},{7,4},{8,11},{9,10},{10,... | collective-permute-start | bytes 491528 | tf_op jit(solution)/shard_map/ppermute | solution.py:647
  329.0 6.6 %copy-start.7 = (f32[320,1024]{1,0:T(8,128)S(1)}, f32[320,1024]{1,0:T(8,128)}, u32[]{:S(2)}) copy-start(f32[320,1024]{1,0:T(8,128)} %get-tuple-element.55.refs_3_) | copy-start | bytes 3932164
  329.0 6.6 %copy-start.19 = (f32[320,1024]{1,0:T(8,128)S(1)}, f32[320,1024]{1,0:T(8,128)}, u32[]{:S(2)}) copy-start(f32[320,1024]{1,0:T(8,128)} %get-tuple-element.58) | copy-start | bytes 3932164
  334.7 48.1 %collective-permute-start.12 = (bf16[4,3,128,1024]{3,2,1,0:T(8,128)(2,1)}, bf16[4,3,128,1024]{3,2,1,0:T(8,128)(2,1)}, u32[]{:S(2)}, u32[]{:S(2)}) collective-permute-start(bf16[4,3,128,1024]{3,2,1,0:T(8,128)(2,1)} %weight_grad.10), channel_id=1, source_target_pairs={{0,4},{4,0},{8,12},{12,8},{16,20},{20,16},{24,28},{28,24},{1,5},{5... | collective-permute-start | bytes 9437192 | tf_op jit(solution)/shard_map/ppermute | solution.py:654
  338.7 28.0 %collective-permute-start.13 = (bf16[4,80,2048]{2,1,0:T(8,128)(2,1)}, bf16[4,80,2048]{2,1,0:T(8,128)(2,1)}, u32[]{:S(2)}, u32[]{:S(2)}) collective-permute-start(bf16[4,80,2048]{2,1,0:T(8,128)(2,1)} %dynamic-slice_bitcast_fusion), channel_id=1, source_target_pairs={{0,4},{4,0},{8,12},{12,8},{16,20},{20,16},{24,28},{28,24},{1,5},{5... | collective-permute-start | bytes 3932168 | tf_op jit(solution)/shard_map/ppermute | solution.py:654
  339.2 9.6 %collective-permute-start.9 = (bf16[2,320,128]{2,1,0:T(8,128)(2,1)S(1)}, bf16[2,320,128]{2,1,0:T(8,128)(2,1)S(1)}, u32[]{:S(2)}, u32[]{:S(2)}) collective-permute-start(bf16[2,320,128]{2,1,0:T(8,128)(2,1)S(1)} %get-tuple-element.151), channel_id=1, source_target_pairs={{0,1},{1,0},{2,3},{3,2},{4,5},{5,4},{6,7},{7,6},{8,9},{9,8},{10,11... | collective-permute-start | bytes 491528 | tf_op jit(solution)/shard_map/ppermute | solution.py:647
  342.2 18.2 %collective-permute-start.10 = (bf16[2,320,128]{2,1,0:T(8,128)(2,1)S(1)}, bf16[2,320,128]{2,1,0:T(8,128)(2,1)S(1)}, u32[]{:S(2)}, u32[]{:S(2)}) collective-permute-start(bf16[2,320,128]{2,1,0:T(8,128)(2,1)S(1)} %get-tuple-element.150), channel_id=1, source_target_pairs={{0,2},{1,3},{2,0},{3,1},{4,6},{5,7},{6,4},{7,5},{8,10},{9,11},{10,... | collective-permute-start | bytes 491528 | tf_op jit(solution)/shard_map/ppermute | solution.py:647
  362.9 15.0 %all-to-all-start.4 = ((bf16[8,5,64,128]{3,2,1,0:T(8,128)(2,1)}), bf16[8,5,64,128]{3,2,1,0:T(8,128)(2,1)S(1)}, u32[]{:S(2)}, u32[]{:S(2)}) async-start(bf16[8,5,64,128]{3,2,1,0:T(8,128)(2,1)} %tied.17), calls=%async_computation.4 | async-start | bytes 1310720 | tf_op jit(solution)/shard_map/all_to_all | solution.py:887
  378.7 29.7 %all-to-all-start.5 = ((bf16[4,80,2048]{2,1,0:T(8,128)(2,1)}), bf16[4,80,2048]{2,1,0:T(8,128)(2,1)S(1)}, u32[]{:S(2)}, u32[]{:S(2)}) async-start(bf16[4,80,2048]{2,1,0:T(8,128)(2,1)} %tied.18), calls=%async_computation.5 | async-start | bytes 2621440 | tf_op jit(solution)/shard_map/all_to_all | solution.py:651
  409.4 29.4 %all-to-all-start.6 = ((bf16[8,5,64,384]{3,2,1,0:T(8,128)(2,1)}), bf16[8,5,64,384]{3,2,1,0:T(8,128)(2,1)S(1)}, u32[]{:S(2)}, u32[]{:S(2)}) async-start(bf16[8,5,64,384]{3,2,1,0:T(8,128)(2,1)} %tied.19), calls=%async_computation.6 | async-start | bytes 3932160 | tf_op jit(solution)/shard_map/all_to_all | solution.py:907
  413.6 226.1 %all-gather.13.cloned.1.call-start = ((), (), s32[]{:S(2)}) async-start(), calls=%async_computation.12 | async-start | bytes 5898240 | tf_op jit(solution)/shard_map/all_gather | solution.py:987
  419.0 8.0 %collective-permute-start.14 = (bf16[80,1024]{1,0:T(8,128)(2,1)}, bf16[80,1024]{1,0:T(8,128)(2,1)S(1)}, u32[]{:S(2)}, u32[]{:S(2)}) collective-permute-start(bf16[80,1024]{1,0:T(8,128)(2,1)} %text_grad.1), channel_id=1, source_target_pairs={{0,1},{1,0},{2,3},{3,2},{4,5},{5,4},{6,7},{7,6},{8,9},{9,8},{10,11... | collective-permute-start | bytes 491528 | tf_op jit(solution)/shard_map/ppermute | solution.py:647
  419.0 15.2 %collective-permute-start.15 = (bf16[80,1024]{1,0:T(8,128)(2,1)}, bf16[80,1024]{1,0:T(8,128)(2,1)S(1)}, u32[]{:S(2)}, u32[]{:S(2)}) collective-permute-start(bf16[80,1024]{1,0:T(8,128)(2,1)} %text_grad.1), channel_id=1, source_target_pairs={{0,2},{1,3},{2,0},{3,1},{4,6},{5,7},{6,4},{7,5},{8,10},{9,11},{10,... | collective-permute-start | bytes 491528 | tf_op jit(solution)/shard_map/ppermute | solution.py:647
  419.0 15.2 %collective-permute-start.16 = (bf16[80,1024]{1,0:T(8,128)(2,1)}, bf16[80,1024]{1,0:T(8,128)(2,1)S(1)}, u32[]{:S(2)}, u32[]{:S(2)}) collective-permute-start(bf16[80,1024]{1,0:T(8,128)(2,1)} %text_grad.1), channel_id=1, source_target_pairs={{0,3},{1,2},{2,1},{3,0},{4,7},{5,6},{6,5},{7,4},{8,11},{9,10},{10,... | collective-permute-start | bytes 491528 | tf_op jit(solution)/shard_map/ppermute | solution.py:647
  446.0 65.3 %all-to-all-start.7 = ((bf16[4,320,1024]{2,1,0:T(8,128)(2,1)}), bf16[4,320,1024]{2,1,0:T(8,128)(2,1)S(1)}, u32[]{:S(2)}, u32[]{:S(2)}) async-start(bf16[4,320,1024]{2,1,0:T(8,128)(2,1)} %get-tuple-element.74.refs_6_.refs_11_), calls=%async_computation.7 | async-start | bytes 5242880 | tf_op jit(solution)/shard_map/all_to_all | solution.py:946
  454.9 13.6 %collective-permute-start.21 = (bf16[4,2,128,1024]{3,2,1,0:T(8,128)(2,1)}, bf16[4,2,128,1024]{3,2,1,0:T(8,128)(2,1)}, u32[]{:S(2)}, u32[]{:S(2)}) collective-permute-start(bf16[4,2,128,1024]{3,2,1,0:T(8,128)(2,1)} %weight_grad.14), channel_id=1, source_target_pairs={{0,4},{4,0},{8,12},{12,8},{16,20},{20,16},{24,28},{28,24},{1,5},{5... | collective-permute-start | bytes 6291464 | tf_op jit(solution)/shard_map/ppermute | solution.py:654
  459.7 4.0 collective-permute-start.20
  460.2 35.0 %collective-permute-start.19 = (bf16[3,128,1024]{2,1,0:T(8,128)(2,1)}, bf16[3,128,1024]{2,1,0:T(8,128)(2,1)S(1)}, u32[]{:S(2)}, u32[]{:S(2)}) collective-permute-start(bf16[3,128,1024]{2,1,0:T(8,128)(2,1)} %tied.22), channel_id=1, source_target_pairs={{0,24},{4,28},{8,16},{12,20},{16,8},{20,12},{24,0},{28,4},{1,25},{... | collective-permute-start | bytes 2359304 | tf_op jit(solution)/shard_map/ppermute | solution.py:672
  461.8 49.5 %collective-permute-start.18 = (bf16[3,128,1024]{2,1,0:T(8,128)(2,1)}, bf16[3,128,1024]{2,1,0:T(8,128)(2,1)}, u32[]{:S(2)}, u32[]{:S(2)}) collective-permute-start(bf16[3,128,1024]{2,1,0:T(8,128)(2,1)} %tied.21), channel_id=1, source_target_pairs={{0,16},{4,20},{8,24},{12,28},{16,0},{20,4},{24,8},{28,12},{1,17},{... | collective-permute-start | bytes 2359304 | tf_op jit(solution)/shard_map/ppermute | solution.py:672
  462.4 48.9 %collective-permute-start.17 = (bf16[3,128,1024]{2,1,0:T(8,128)(2,1)}, bf16[3,128,1024]{2,1,0:T(8,128)(2,1)}, u32[]{:S(2)}, u32[]{:S(2)}) collective-permute-start(bf16[3,128,1024]{2,1,0:T(8,128)(2,1)} %tied.20), channel_id=1, source_target_pairs={{0,8},{4,12},{8,0},{12,4},{16,24},{20,28},{24,16},{28,20},{1,9},{5... | collective-permute-start | bytes 2359304 | tf_op jit(solution)/shard_map/ppermute | solution.py:672
  495.2 16.1 %copy-start.10 = (bf16[3,128,1024]{2,1,0:T(8,128)(2,1)}, bf16[3,128,1024]{2,1,0:T(8,128)(2,1)S(1)}, u32[]{:S(2)}) copy-start(bf16[3,128,1024]{2,1,0:T(8,128)(2,1)S(1)} %collective-permute-done.19.refs_6_) | copy-start | bytes 2359300
  517.9 128.8 %all-to-all-start.8 = ((bf16[4,320,1024]{2,1,0:T(8,128)(2,1)}), bf16[4,320,1024]{2,1,0:T(8,128)(2,1)S(1)}, u32[]{:S(2)}, u32[]{:S(2)}) async-start(bf16[4,320,1024]{2,1,0:T(8,128)(2,1)} %get-tuple-element.83.refs_1_), calls=%async_computation.8 | async-start | bytes 5242880 | tf_op jit(solution)/shard_map/all_to_all | solution.py:969
  527.5 23.4 %collective-permute-start.33 = (bf16[2,128,1024]{2,1,0:T(8,128)(2,1)}, bf16[2,128,1024]{2,1,0:T(8,128)(2,1)}, u32[]{:S(2)}, u32[]{:S(2)}) collective-permute-start(bf16[2,128,1024]{2,1,0:T(8,128)(2,1)} %get-tuple-element.89), channel_id=1, source_target_pairs={{0,8},{4,12},{8,0},{12,4},{16,24},{20,28},{24,16},{28,20},{1,9},{5... | collective-permute-start | bytes 1572872 | tf_op jit(solution)/shard_map/ppermute | solution.py:672
  529.0 23.6 %collective-permute-start.34 = (bf16[2,128,1024]{2,1,0:T(8,128)(2,1)}, bf16[2,128,1024]{2,1,0:T(8,128)(2,1)}, u32[]{:S(2)}, u32[]{:S(2)}) collective-permute-start(bf16[2,128,1024]{2,1,0:T(8,128)(2,1)} %get-tuple-element.90), channel_id=1, source_target_pairs={{0,16},{4,20},{8,24},{12,28},{16,0},{20,4},{24,8},{28,12},{1,17},{... | collective-permute-start | bytes 1572872 | tf_op jit(solution)/shard_map/ppermute | solution.py:672
  529.5 25.3 %collective-permute-start.35 = (bf16[2,128,1024]{2,1,0:T(8,128)(2,1)}, bf16[2,128,1024]{2,1,0:T(8,128)(2,1)}, u32[]{:S(2)}, u32[]{:S(2)}) collective-permute-start(bf16[2,128,1024]{2,1,0:T(8,128)(2,1)} %get-tuple-element.91), channel_id=1, source_target_pairs={{0,24},{4,28},{8,16},{12,20},{16,8},{20,12},{24,0},{28,4},{1,25},{... | collective-permute-start | bytes 1572872 | tf_op jit(solution)/shard_map/ppermute | solution.py:672
  545.5 22.7 %collective-permute-start.27 = (bf16[1,128,768]{2,1,0:T(8,128)(2,1)}, bf16[1,128,768]{2,1,0:T(8,128)(2,1)}, u32[]{:S(2)}, u32[]{:S(2)}) collective-permute-start(bf16[1,128,768]{2,1,0:T(8,128)(2,1)} %get-tuple-element.86), channel_id=1, source_target_pairs={{0,8},{4,12},{8,0},{12,4},{16,24},{20,28},{24,16},{28,20},{1,9},{5... | collective-permute-start | bytes 589832 | tf_op jit(solution)/shard_map/ppermute | solution.py:672
  547.0 3.9 copy-start.26
  547.0 7.9 %copy-start.14 = (bf16[2,128,1024]{2,1,0:T(8,128)(2,1)S(1)}, bf16[2,128,1024]{2,1,0:T(8,128)(2,1)}, u32[]{:S(2)}) copy-start(bf16[2,128,1024]{2,1,0:T(8,128)(2,1)} %get-tuple-element.82.refs_8_) | copy-start | bytes 1572868
  547.0 21.3 %collective-permute-start.28 = (bf16[1,128,768]{2,1,0:T(8,128)(2,1)}, bf16[1,128,768]{2,1,0:T(8,128)(2,1)}, u32[]{:S(2)}, u32[]{:S(2)}) collective-permute-start(bf16[1,128,768]{2,1,0:T(8,128)(2,1)} %get-tuple-element.87), channel_id=1, source_target_pairs={{0,16},{4,20},{8,24},{12,28},{16,0},{20,4},{24,8},{28,12},{1,17},{... | collective-permute-start | bytes 589832 | tf_op jit(solution)/shard_map/ppermute | solution.py:672
  550.9 18.9 %collective-permute-start.29 = (bf16[1,128,768]{2,1,0:T(8,128)(2,1)}, bf16[1,128,768]{2,1,0:T(8,128)(2,1)}, u32[]{:S(2)}, u32[]{:S(2)}) collective-permute-start(bf16[1,128,768]{2,1,0:T(8,128)(2,1)} %get-tuple-element.88), channel_id=1, source_target_pairs={{0,24},{4,28},{8,16},{12,20},{16,8},{20,12},{24,0},{28,4},{1,25},{... | collective-permute-start | bytes 589832 | tf_op jit(solution)/shard_map/ppermute | solution.py:672
  552.5 6.2 collective-permute-start.22
  558.7 11.0 %copy-start.20 = (bf16[1,128,768]{2,1,0:T(8,128)(2,1)S(1)}, bf16[1,128,768]{2,1,0:T(8,128)(2,1)}, u32[]{:S(2)}) copy-start(bf16[1,128,768]{2,1,0:T(8,128)(2,1)} %get-tuple-element.81.refs_7_) | copy-start | bytes 589828
  558.8 6.5 collective-permute-start.23
  561.9 13.1 %collective-permute-start.36 = (bf16[2,128,256]{2,1,0:T(8,128)(2,1)}, bf16[2,128,256]{2,1,0:T(8,128)(2,1)S(1)}, u32[]{:S(2)}, u32[]{:S(2)}) collective-permute-start(bf16[2,128,256]{2,1,0:T(8,128)(2,1)} %bitcast.114), channel_id=1, source_target_pairs={{0,1},{1,0},{2,3},{3,2},{4,5},{5,4},{6,7},{7,6},{8,9},{9,8},{10,11... | collective-permute-start | bytes 393224 | tf_op jit(solution)/shard_map/ppermute | solution.py:647
  565.3 26.5 %collective-permute-start.37 = (bf16[2,128,256]{2,1,0:T(8,128)(2,1)}, bf16[2,128,256]{2,1,0:T(8,128)(2,1)}, u32[]{:S(2)}, u32[]{:S(2)}) collective-permute-start(bf16[2,128,256]{2,1,0:T(8,128)(2,1)} %bitcast.113), channel_id=1, source_target_pairs={{0,2},{1,3},{2,0},{3,1},{4,6},{5,7},{6,4},{7,5},{8,10},{9,11},{10,... | collective-permute-start | bytes 393224 | tf_op jit(solution)/shard_map/ppermute | solution.py:647
  568.2 23.5 %collective-permute-start.38 = (bf16[2,128,256]{2,1,0:T(8,128)(2,1)}, bf16[2,128,256]{2,1,0:T(8,128)(2,1)}, u32[]{:S(2)}, u32[]{:S(2)}) collective-permute-start(bf16[2,128,256]{2,1,0:T(8,128)(2,1)} %bitcast.112), channel_id=1, source_target_pairs={{0,3},{1,2},{2,1},{3,0},{4,7},{5,6},{6,5},{7,4},{8,11},{9,10},{10,... | collective-permute-start | bytes 393224 | tf_op jit(solution)/shard_map/ppermute | solution.py:647
  568.3 4.3 collective-permute-start.24
  573.9 26.3 %collective-permute-start.25 = (f32[6,1024]{1,0:T(8,128)}, f32[6,1024]{1,0:T(8,128)}, u32[]{:S(2)}, u32[]{:S(2)}) collective-permute-start(f32[6,1024]{1,0:T(8,128)} %add.189), channel_id=1, source_target_pairs={{0,1},{1,0},{2,3},{3,2},{4,5},{5,4},{6,7},{7,6},{8,9},{9,8},{10,11... | collective-permute-start | bytes 73736 | tf_op jit(solution)/shard_map/ppermute | solution.py:1010
  593.6 42.7 %collective-permute-start.39 = (bf16[2,128,1024]{2,1,0:T(8,128)(2,1)}, bf16[2,128,1024]{2,1,0:T(8,128)(2,1)}, u32[]{:S(2)}, u32[]{:S(2)}) collective-permute-start(bf16[2,128,1024]{2,1,0:T(8,128)(2,1)} %tied.25), channel_id=1, source_target_pairs={{0,2},{1,3},{2,0},{3,1},{4,6},{5,7},{6,4},{7,5},{8,10},{9,11},{10,... | collective-permute-start | bytes 1572872 | tf_op jit(solution)/shard_map/ppermute | solution.py:973
  601.1 29.5 %collective-permute-start.26 = (f32[6,1024]{1,0:T(8,128)S(1)}, f32[6,1024]{1,0:T(8,128)S(1)}, u32[]{:S(2)}, u32[]{:S(2)}) collective-permute-start(f32[6,1024]{1,0:T(8,128)S(1)} %add.190), channel_id=1, source_target_pairs={{0,2},{1,3},{2,0},{3,1},{4,6},{5,7},{6,4},{7,5},{8,10},{9,11},{10,... | collective-permute-start | bytes 73736 | tf_op jit(solution)/shard_map/ppermute | solution.py:1010
  603.6 28.3 %collective-permute-start.30 = (bf16[3,128,256]{2,1,0:T(8,128)(2,1)S(1)}, bf16[3,128,256]{2,1,0:T(8,128)(2,1)S(1)}, u32[]{:S(2)}, u32[]{:S(2)}) collective-permute-start(bf16[3,128,256]{2,1,0:T(8,128)(2,1)S(1)} %bitcast.158), channel_id=1, source_target_pairs={{0,1},{1,0},{2,3},{3,2},{4,5},{5,4},{6,7},{7,6},{8,9},{9,8},{10,11... | collective-permute-start | bytes 589832 | tf_op jit(solution)/shard_map/ppermute | solution.py:647
  606.0 28.0 %collective-permute-start.31 = (bf16[3,128,256]{2,1,0:T(8,128)(2,1)S(1)}, bf16[3,128,256]{2,1,0:T(8,128)(2,1)S(1)}, u32[]{:S(2)}, u32[]{:S(2)}) collective-permute-start(bf16[3,128,256]{2,1,0:T(8,128)(2,1)S(1)} %bitcast.159), channel_id=1, source_target_pairs={{0,2},{1,3},{2,0},{3,1},{4,6},{5,7},{6,4},{7,5},{8,10},{9,11},{10,... | collective-permute-start | bytes 589832 | tf_op jit(solution)/shard_map/ppermute | solution.py:647
  606.1 27.9 %collective-permute-start.32 = (bf16[3,128,256]{2,1,0:T(8,128)(2,1)S(1)}, bf16[3,128,256]{2,1,0:T(8,128)(2,1)S(1)}, u32[]{:S(2)}, u32[]{:S(2)}) collective-permute-start(bf16[3,128,256]{2,1,0:T(8,128)(2,1)S(1)} %bitcast.160), channel_id=1, source_target_pairs={{0,3},{1,2},{2,1},{3,0},{4,7},{5,6},{6,5},{7,4},{8,11},{9,10},{10,... | collective-permute-start | bytes 589832 | tf_op jit(solution)/shard_map/ppermute | solution.py:647
  (17 other events, 24.8 us)
Sparse Core Ops, SparseCore 0:
  29.7 34.4 all-gather.10
  195.2 34.4 all-gather.6
  336.9 58.4 all-gather.8
  436.7 73.0 all-gather.12

commit v3 on v2

--- a/solution.py
+++ b/solution.py
@@ -175,13 +175,23 @@
     out_ref[0] = total.astype(BF)
 
 
-def last_kernel(parts_ref, x_ref, dx2_ref, norm_ref, dx_ref, sums_ref):
+def first_norm_kernel(parts_ref, x_ref, sums_ref):
+    d_h1 = parts_ref[0].astype(F32)
+    normal, _ = normalize(x_ref[0].astype(F32))
+    sums = [jnp.sum(d_h1 * normal, axis=0, keepdims=True), jnp.sum(d_h1, axis=0, keepdims=True)]
+
+    @pl.when(pl.program_id(0) == 0)
+    def _():
+        sums_ref[...] = jnp.zeros_like(sums_ref)
+
+    sums_ref[...] += jnp.concatenate(sums, axis=0)
+
+
+def last_kernel(parts_ref, x_ref, dx2_ref, norm_ref, dx_ref):
     d_h1 = parts_ref[0].astype(F32)
     for r in range(1, parts_ref.shape[0]):
         d_h1 += parts_ref[r].astype(F32)
-    d_v, gain, bias = norm_backward(x_ref[...].astype(F32), norm_ref[0:1], d_h1)
-    sums_ref[0:1] = gain
-    sums_ref[1:2] = bias
+    d_v, _, _ = norm_backward(x_ref[...].astype(F32), norm_ref[0:1], d_h1)
     d_x = (dx2_ref[...] + d_v).astype(BF)
     for r in range(dx_ref.shape[0]):
         dx_ref[r] = d_x
@@ -210,12 +220,19 @@
     q_of = [pick(m, q) for m in masks]
     v_of = [pick(m, v) for m in masks]
     per = block // rows
-    for first in range(0, length, block):
-        top = first + block
-        total = jnp.zeros((block, width), F32)
-        for h in range(len(masks)):
-            probs = causal_probs(ends_ref, stream, slots, q_of[h][first:top], k[:top], first)
-            total += dot(probs.astype(BF), v_of[h][:top], NN)
+    firsts = range(0, length, block)
+    pairs = [(h, first) for first in firsts for h in range(len(masks))]
+    probs = [
+        causal_probs(
+            ends_ref, stream, slots, q_of[h][first : first + block], k[: first + block], first
+        ).astype(BF)
+        for h, first in pairs
+    ]
+    results = [
+        dot(p, v_of[h][: first + block], NN) for p, (h, first) in zip(probs, pairs)
+    ]
+    for first in firsts:
+        total = sum(r for r, (_, f) in zip(results, pairs) if f == first)
         at = first // rows
         out_ref[at : at + per, 0] = total.astype(BF).reshape(per, rows, width)
 
@@ -333,12 +350,14 @@
     mine = pl.ds(pl.multiple_of(stream * rows, rows), rows)
     once = cross_allowed(info_ref, stream, slots, rows, keys)
     allowed = jnp.concatenate([once] * (CROSS_LANES // HEAD_DIM), axis=0)
-    for at in range(0, model, CROSS_LANES):
-        cols = slice(at, at + CROSS_LANES)
-        q = stacked_heads(cq_ref[mine, cols] * jnp.asarray(SCALE, BF))
-        probs = softmax(dot(q, kv_ref[0, :, cols], NT), allowed)
-        result = dot(probs.astype(BF), kv_ref[0, :, model + at : model + at + CROSS_LANES], NN)
-        cattn_ref[mine, cols] = merged_heads(result, rows).astype(BF)
+    every = [slice(at, at + CROSS_LANES) for at in range(0, model, CROSS_LANES)]
+    q = [stacked_heads(cq_ref[mine, c] * jnp.asarray(SCALE, BF)) for c in every]
+    scores = [dot(a, kv_ref[0, :, c], NT) for a, c in zip(q, every)]
+    probs = [softmax(a, allowed).astype(BF) for a in scores]
+    values = [kv_ref[0, :, model + c.start : model + c.stop] for c in every]
+    results = [dot(a, v, NN) for a, v in zip(probs, values)]
+    for c, a in zip(every, results):
+        cattn_ref[mine, c] = merged_heads(a, rows).astype(BF)
 
     @pl.when(stream == pl.num_programs(0) - 1)
     def _():
@@ -384,7 +403,7 @@
 
     @pl.when(stream == 0)
     def _():
-        d_h3 = dh_ref[...] + received_ref[...].astype(F32)
+        d_h3 = dh_ref[...] + received_ref[0].astype(F32)
         d_v, gain, bias = norm_backward(x3_ref[...], gain_ref[2:3], d_h3)
         sums_ref[1:2] = gain
         sums_ref[3:4] = bias
@@ -398,21 +417,23 @@
     mine = pl.ds(pl.multiple_of(stream * rows, rows), rows)
     once = cross_allowed(info_ref, stream, slots, rows, keys)
     allowed = jnp.concatenate([once] * (CROSS_LANES // HEAD_DIM), axis=0)
-    for at in range(0, model, CROSS_LANES):
-        cols = slice(at, at + CROSS_LANES)
-        k = kv_ref[0, :, cols]
-        v = kv_ref[0, :, model + at : model + at + CROSS_LANES]
-        q = stacked_heads(cq_ref[mine, cols] * jnp.asarray(SCALE, BF))
-        grad = stacked_heads(dcattn_ref[mine, cols])
-        probs = softmax(dot(q, k, NT), allowed)
-        d_probs = dot(grad, v, NT)
-        delta = jnp.sum(probs * d_probs, axis=1, keepdims=True)
-        d_scores = (probs * (d_probs - delta)).astype(BF)
-        dcq_ref[mine, cols] = (merged_heads(dot(d_scores, k, NN), rows) * SCALE).astype(BF)
-        d_k = dot(d_scores, q, TN).astype(BF)
-        d_v = dot(probs.astype(BF), grad, TN).astype(BF)
-        dkv_ref[0, :, cols] = d_k
-        dkv_ref[0, :, model + at : model + at + CROSS_LANES] = d_v
+    every = [slice(at, at + CROSS_LANES) for at in range(0, model, CROSS_LANES)]
+    k = [kv_ref[0, :, c] for c in every]
+    v = [kv_ref[0, :, model + c.start : model + c.stop] for c in every]
+    q = [stacked_heads(cq_ref[mine, c] * jnp.asarray(SCALE, BF)) for c in every]
+    grad = [stacked_heads(dcattn_ref[mine, c]) for c in every]
+    scores = [dot(a, b, NT) for a, b in zip(q, k)]
+    d_probs = [dot(a, b, NT) for a, b in zip(grad, v)]
+    probs = [softmax(a, allowed) for a in scores]
+    delta = [jnp.sum(a * b, axis=1, keepdims=True) for a, b in zip(probs, d_probs)]
+    d_scores = [(a * (b - c)).astype(BF) for a, b, c in zip(probs, d_probs, delta)]
+    d_q = [dot(a, b, NN) for a, b in zip(d_scores, k)]
+    d_k = [dot(a, b, TN) for a, b in zip(d_scores, q)]
+    d_v = [dot(a.astype(BF), b, TN) for a, b in zip(probs, grad)]
+    for i, c in enumerate(every):
+        dcq_ref[mine, c] = (merged_heads(d_q[i], rows) * SCALE).astype(BF)
+        dkv_ref[0, :, c] = d_k[i].astype(BF)
+        dkv_ref[0, :, model + c.start : model + c.stop] = d_v[i].astype(BF)
 
     @pl.when(stream == pl.num_programs(0) - 1)
     def _():
@@ -433,7 +454,8 @@
 
 
 def ffn_kernel(h_ref, ct_ref, *refs, groups, tiles):
-    act_ref, dup_ref, dh_ref, out_ref, dh_acc, out_acc = refs[2 * groups :]
+    (act_ref, dup_ref), results = refs[2 * groups : 2 * groups + 2], refs[2 * groups + 2 : -2]
+    dh_acc, out_acc = refs[-2:]
     step = pl.program_id(0)
 
     @pl.when(step == 0)
@@ -460,11 +482,15 @@
 
     @pl.when(step == groups * tiles - 1)
     def _():
-        dh_ref[...] = dh_acc[...].astype(dh_ref.dtype)
-        out_ref[...] = out_acc[...].astype(out_ref.dtype)
-
-
-def feed_forward(h, ct, own, others, hidden, dtype, deps=()):
+        if len(results) == 2:
+            results[0][...] = dh_acc[...]
+            results[1][...] = out_acc[...]
+        else:
+            results[0][0] = dh_acc[...].astype(BF)
+            results[0][1] = out_acc[...].astype(BF)
+
+
+def feed_forward(h, ct, own, others, hidden, paired, deps=()):
     count, model = h.shape
     groups = 1 + len(others)
     tile = min(hidden, 512)
@@ -481,14 +507,16 @@
             spec = pl.BlockSpec((model, tile), lambda i, g=g, f=first: (0, f + place(g)(i)))
             ins.append((w, spec))
     wide = struct((count, groups * hidden))
-    narrow = struct((count, model), dtype)
+    results = [(struct((count, model), F32), None)] * 2
+    if paired:
+        results = [(struct((2, count, model)), None)]
     column = pl.BlockSpec((count, tile), lambda i: (0, i))
     return call(
         functools.partial(ffn_kernel, groups=groups, tiles=tiles),
         "feed_forward",
         (groups * tiles,),
         ins,
-        [(wide, column), (wide, column), (narrow, None), (narrow, None)],
+        [(wide, column), (wide, column), *results],
         scratch=[pltpu.VMEM((count, model), F32)] * 2,
         deps=deps,
         flops=8 * count * model * groups * hidden,
@@ -498,7 +526,6 @@
 
 def weight_grad_kernel(index_ref, *refs, sums, chips, plus, apart):
     outs = refs[-chips:] if apart else [refs[-1].at[j] for j in range(chips)]
-    plus_ref = refs[-chips - 1 if apart else -2]
     at = 0
     for p, terms in enumerate(sums):
         total = 0.0
@@ -510,7 +537,7 @@
         for j in range(chips):
             block = total[j * share : (j + 1) * share]
             if plus:
-                block += plus_ref[j, p].astype(F32)
+                block += refs[sum(sums) * (chips + 1) + j][p].astype(F32)
             outs[j][p] = block.astype(BF)
 
 
@@ -528,7 +555,9 @@
                 total += dot(left.reshape(-1, chips * share), right, TN)
             parts.append(total.reshape(chips, share, cols))
         blocks = jnp.stack(parts, axis=1)
-        blocks = (blocks if plus is None else blocks + plus.astype(F32)).astype(BF)
+        if plus is not None:
+            blocks += jnp.stack(plus).astype(F32)
+        blocks = blocks.astype(BF)
         return [blocks[j] for j in range(chips)] if apart else blocks
     tile = 512 if cols % 512 == 0 else cols
     ins = []
@@ -547,7 +576,7 @@
     one_spec = pl.BlockSpec((len(sums), share, tile), lambda i, w: (0, 0, i))
     outs = [(every, every_spec)]
     if plus is not None:
-        ins.append((plus, every_spec))
+        ins += [(p, one_spec) for p in plus]
     if apart:
         outs = [(struct(every.shape[1:]), one_spec)] * chips
     result = call(
@@ -567,6 +596,16 @@
         flops=flops,
     )
     return result if apart else result[0]
+
+
+def ffn_sum_kernel(in_ref, own_ref, *others):
+    total = in_ref[0].astype(F32)
+    for c in range(1, in_ref.shape[0]):
+        total += in_ref[c].astype(F32)
+    hidden = own_ref.shape[2]
+    own_ref[...] = total[:, :, :hidden]
+    for j, ref in enumerate(others, 1):
+        ref[...] = total[:, :, j * hidden : (j + 1) * hidden].astype(BF)
 
 
 def tie_kernel(*refs):
@@ -662,9 +701,10 @@
             [(left, r if isinstance(r, tuple) else (r, 0, r.shape[1])) for left, r in terms]
             for terms in sums
         ]
-        send = weight_grad_blocks(2 * order + 1 - core, sums, share, deps=deps)
+        send = weight_grad_blocks(2 * order + 1 - core, sums, share, apart=True, deps=deps)
+        received = [other_core(v) for v in send]
         return weight_grad_blocks(
-            2 * order + core, sums, share, other_core(send), apart=apart, deps=later
+            2 * order + core, sums, share, received, apart=apart, deps=later
         )
 
     def from_chips(blocks):
@@ -678,10 +718,11 @@
             total += v.astype(F32)
         return total
 
-    def over_ranks(total):
+    def over_ranks(total, *first):
         parts, _, c = total.shape
         split = total.astype(BF).reshape(parts, share, tp, c // tp).transpose(2, 0, 1, 3)
-        return added(from_ranks([at(split, t ^ j) for j in range(tp)]))
+        mine_of, *got = from_ranks([at(split, t ^ j) for j in range(tp)])
+        return added([mine_of] + [tied(g, *first) for g in got])
 
     def share_rows(w):
         return lax.dynamic_slice_in_dim(w, b * share, share, w.ndim - 2)
@@ -706,12 +747,14 @@
     own_ends = jnp.pad(all_ends, ((0, slices * group - streams), (0, 0)))
     own_ends = lax.dynamic_slice_in_dim(own_ends, b // per * group, group, 0)
     shared = lax.all_gather(shared, "tp")
+    memory_weights = spread(tied(shared[:, :, : 2 * local], qkv))
+    w_mem = columns(memory_weights, 2 * local, 0)
     attn_own = self_attention(
         own_ends, [qkv], width, self_forward_kernel, width, 0, "self_forward"
     )
     even = slices == tp and group == mine
 
-    attn_rows = lax.all_to_all(attn_own, "blk", 0, 0)
+    attn_rows = lax.all_to_all(tied(attn_own, memory_weights[0]), "blk", 0, 0)
     if even:
         attn = attn_rows.reshape(tp, per, count, width)
     else:
@@ -721,10 +764,9 @@
         attn = attn.reshape(tp, per, count, width)
     attn = from_ranks([at(attn, t ^ j) for j in range(tp)])
 
-    weights = spread(tied(shared, *attn))
-    w_mem = columns(weights, 2 * local, 0)
-    w_first = columns(weights, 2 * local, 1)
-    w_cross_out = columns(weights, local, 4)
+    weights = spread(tied(shared[:, :, 2 * local :], *attn))
+    w_first = columns(weights, 2 * local, 0)
+    w_cross_out = columns(weights, local, 2)
     piece = tied(piece, *attn)
     pieces_of = [lax.ppermute(piece, "tp", swapped(tp, 2 * j)) for j in range(1, groups)]
     ffn_others = [
@@ -744,22 +786,6 @@
     x = of_rank(frames, t).reshape(count, model)
     flat = struct((count, model))
     wide = struct((count, model), F32)
-    x2, h2, cq, attn = call(
-        first_kernel,
-        "to_cross",
-        (1,),
-        [
-            (x, None),
-            (norm_rows(1), None),
-            *w_first,
-            *[(a, None) for a in attn],
-        ],
-        [(wide, None), (flat, None), (flat, None), (flat, None)],
-        scalars=(device,),
-        scratch=[pltpu.VMEM((model, 2 * model), BF)],
-        deps=pieces_of,
-        flops=4 * count * model * model,
-    )
     texts = of_rank(text_states, t).reshape(mine * text_rows, model)
     tile = model // 2
     (ckv,) = call(
@@ -775,7 +801,7 @@
                         (chips, tp // 2, share, local), lambda i, _: (0, i % 2, 0, i // 2)
                     ),
                 )
-                for w in weights
+                for w in memory_weights
             ],
         ],
         [
@@ -786,8 +812,23 @@
         ],
         scalars=(device,),
         scratch=[pltpu.VMEM((model, tile), BF)],
-        deps=(cq,),
         flops=4 * texts.shape[0] * model * model,
+    )
+    x2, h2, cq, attn = call(
+        first_kernel,
+        "to_cross",
+        (1,),
+        [
+            (x, None),
+            (norm_rows(1), None),
+            *w_first,
+            *[(a, None) for a in attn],
+        ],
+        [(wide, None), (flat, None), (flat, None), (flat, None)],
+        scalars=(device,),
+        scratch=[pltpu.VMEM((model, 2 * model), BF)],
+        deps=(ckv,),
+        flops=4 * count * model * model,
     )
     ckv = ckv.reshape(mine, text_rows, 2 * model)
     kv_spec = pl.BlockSpec((1, text_rows, 2 * model), lambda s, *_: (s, 0, 0))
@@ -815,25 +856,27 @@
     ct = of_rank(cotangent, t).reshape(count, model)
     ct_other = of_rank(cotangent, t ^ 1).reshape(count, model)
     own_weights = (ffn_up, ffn_down)
-    act_other, d_up_other, d_h3_other, out_other = feed_forward(
-        h3_other, ct_other, own_weights, ffn_others, hidden, BF
-    )
-    d_h3_got = lax.ppermute(d_h3_other, "tp", swap)
-    act, d_up, d_h3, out = feed_forward(
-        h3, ct, own_weights, ffn_others, hidden, F32, deps=(out_other,)
-    )
-    out_got = lax.ppermute(tied(out_other, d_h3_got), "tp", swap)
-    out = x3 + out + out_got.astype(F32)
+    act, d_up, d_h3, out = feed_forward(h3, ct, own_weights, ffn_others, hidden, False)
+    act_other, d_up_other, pair = feed_forward(
+        h3_other, ct_other, own_weights, ffn_others, hidden, True, deps=(out,)
+    )
+    pair_got = lax.ppermute(pair, "tp", swap)
+    out = x3 + out + pair_got[1].astype(F32)
 
     ffn_blocks = weight_grads(
         [[(h3, d_up), (h3_other, d_up_other)], [(ct, act), (ct_other, act_other)]],
         all_chips,
         False,
-        deps=(d_h3_got,),
     )
     ffn_got = over_chips(ffn_blocks)
-    g_ffn = jnp.sum(ffn_got.astype(F32), axis=0)
-    split = g_ffn.reshape(2, share, groups, hidden)
+    ffn_total, *ffn_sent = call(
+        ffn_sum_kernel,
+        "ffn_sum",
+        (1,),
+        [(ffn_got, None)],
+        [(struct((2, share, hidden), F32), None)]
+        + [(struct((2, share, hidden)), None)] * (groups - 1),
+    )
 
     d_c, d_cq, d_x2, d_a, d_attn, d_ckv, early = call(
         functools.partial(third_kernel, slots=slots, rows=rows),
@@ -841,7 +884,7 @@
         (mine,),
         [
             (d_h3, None),
-            (d_h3_got, None),
+            (pair_got, pl.BlockSpec((1, count, model), lambda s, _: (0, 0, 0))),
             (x3, None),
             (ct, None),
             (x2, None),
@@ -872,11 +915,9 @@
         exps=cross_work,
     )
 
+
     d_attn = from_ranks([d_attn[j] for j in range(tp)])
-    attn_blocks = weight_grads(
-        [[(d_a, attn)], [(h2, d_cq)], [(d_c, cattn)]], near_chips, True, deps=(d_attn[-1],)
-    )
-
+    out_all = lax.all_gather(tied(out.astype(BF), *d_attn[1:]), "tp", axis=0, tiled=True)
     d_attn = jnp.stack(d_attn)[jnp.arange(tp) ^ t]
     if not even:
         d_attn = d_attn.reshape(tp, per, mine, rows, width).transpose(0, 2, 1, 3, 4)
@@ -893,9 +934,7 @@
         3 * width,
         2,
         "self_backward",
-        deps=(out_got, attn_blocks[0]),
-    )
-    out_all = lax.all_gather(out.astype(BF), "tp", axis=0, tiled=True)
+    )
 
     part = mine * text_rows // blk
     d_ckv = d_ckv.reshape(chips, 2, part, 2 * model)
@@ -906,7 +945,7 @@
 
     d_qkv = lax.all_to_all(tied(d_qkv_own, d_ckv), "blk", 0, 0)
     texts = lax.dynamic_slice_in_dim(texts, b * part, part, 0)
-    (d_text,) = call(
+    (d_text_own,) = call(
         text_grad_kernel,
         "text_grad",
         (1,),
@@ -917,8 +956,23 @@
         deps=(d_qkv_own,),
         flops=4 * part * model * model,
     )
-    d_text = jnp.stack(from_ranks([d_text] * tp))[jnp.arange(tp) ^ t]
-
+    text_got = from_ranks([d_text_own] * tp)
+
+    ffn_back = [
+        lax.ppermute(tied(v, out_all), "tp", swapped(tp, 2 * j)) for j, v in enumerate(ffn_sent, 1)
+    ]
+    attn_blocks = weight_grads(
+        [
+            [(d_a, attn)],
+            [(h2, d_cq)],
+            [(d_c, cattn)],
+            [(texts, (d_ckv, 0, model))],
+            [(texts, (d_ckv, model, model))],
+        ],
+        near_chips,
+        True,
+        deps=(d_text_own,),
+    )
     d_qkv = d_qkv.reshape(slices, per, group * rows, 3 * width)
     padded_rows = slices * group * rows
     parts, d_qkv = call(
@@ -939,52 +993,43 @@
                 pl.BlockSpec((group * rows, 3 * local), lambda i: (i, 0)),
             ),
         ],
-        deps=(d_text,),
+        deps=(attn_blocks[0], *ffn_back),
         flops=6 * padded_rows * model * local,
     )
     parts_own = parts.reshape(padded_rows, model)[: streams * rows].reshape(tp, count, model)
     parts = lax.all_to_all(parts_own, "tp", 0, 0)
-    qkv_blocks = weight_grads(
-        [[(h_all, d_qkv)]], near_chips, True, deps=(parts_own,)
-    )
+    attn_got = from_chips(attn_blocks)
+    qkv_blocks = weight_grads([[(h_all, d_qkv)]], near_chips, True, deps=(parts_own,), later=tuple(attn_got[1:3]))
     qkv_got = from_chips(qkv_blocks)
-    mem_blocks = weight_grads(
-        [[(texts, (d_ckv, 0, model))], [(texts, (d_ckv, model, model))]],
-        near_chips,
-        True,
-        deps=(parts_own,),
-    )
-    mem_got = from_chips(mem_blocks)
-    attn_got = from_chips([tied(w, d_qkv) for w in attn_blocks])
-
-    d_x, late = call(
+    d_text = jnp.stack([text_got[0]] + [tied(g, qkv_blocks[0]) for g in text_got[1:]])
+    d_text = d_text[jnp.arange(tp) ^ t]
+
+    out_frames = out_all.reshape(streams, rows, model).astype(F32)
+
+    (g_qkv,) = added(qkv_got)
+    grad_self_proj = g_qkv.reshape(share, 3, local).transpose(1, 0, 2)
+
+    (late,) = call(
+        first_norm_kernel,
+        "first_norm",
+        (tp,),
+        [
+            (parts_own, pl.BlockSpec((1, count, model), lambda i: (i, 0, 0))),
+            (frames.reshape(tp, count, model), pl.BlockSpec((1, count, model), lambda i: (i, 0, 0))),
+        ],
+        [(struct((2, model), F32), None)],
+        flops=10 * streams * rows * model,
+    )
+    (d_x,) = call(
         last_kernel,
         "to_frames",
         (1,),
         [(parts, None), (x, None), (d_x2, None), (norm_rows(0), None)],
-        [(struct((tp, count, model)), None), (struct((2, model), F32), None)],
-        deps=(*attn_got[1:], qkv_blocks[0], mem_blocks[0]),
+        [(struct((tp, count, model)), None)],
+        deps=(*attn_got[1:], qkv_blocks[0]),
         flops=20 * count * model,
     )
-    grad_frames = lax.all_to_all(d_x, "tp", 0, 0).reshape(streams, rows, model).astype(F32)
-
-    ffn_total = split[:, :, 0]
-    ffn_back = [
-        lax.ppermute(tied(split[:, :, j].astype(BF), d_x), "tp", swapped(tp, 2 * j)) for j in range(1, groups)
-    ]
-    for back in ffn_back:
-        ffn_total += back.astype(F32)
-    grad_ffn_up = ffn_total[0]
-    grad_ffn_down = ffn_total[1].T
-    g_attn_own = over_ranks(tied(added(attn_got), d_x))
-    grad_cross_mem = over_ranks(added(mem_got))
-    grad_self_out = g_attn_own[0].T
-    grad_cross_query = g_attn_own[1]
-    grad_cross_out = g_attn_own[2].T
-    (g_qkv,) = added(qkv_got)
-    grad_self_proj = g_qkv.reshape(share, 3, local).transpose(1, 0, 2)
-
-    d_text = lax.all_gather(d_text, "blk")
+    d_text = lax.all_gather(tied(d_text, d_x), "blk")
     if part % 16:
         d_text = d_text.transpose(1, 0, 2, 3)
         grad_text = d_text.reshape(streams, slots, text, model).astype(F32)
@@ -1002,19 +1047,25 @@
             ],
         )
         grad_text = grad_text.reshape(streams, slots, text, model)
-
-    sums = jnp.concatenate([early, late], axis=0)
-    for axis, size in (("blk", blk), ("tp", tp)):
-        step = 1
-        while step < size:
-            sums = sums + lax.ppermute(sums, axis, swapped(size, step))
-            step *= 2
+    grad_frames = tied(lax.all_to_all(d_x, "tp", 0, 0), grad_text)
+    grad_frames = grad_frames.reshape(streams, rows, model).astype(F32)
+
+    sums = tied(jnp.concatenate([early, late], axis=0), d_x)
+    for step in (1 << i for i in range(blk.bit_length() - 1)):
+        sums = sums + lax.ppermute(sums, "blk", swapped(blk, step))
     sums = lax.dynamic_slice_in_dim(sums, b * share, share, 1)
+    sums = added(from_ranks([sums] * tp))
     grad_gain = jnp.stack([sums[4], sums[0], sums[1]])
     grad_bias = jnp.stack([sums[5], sums[2], sums[3]])
-
-    out_frames = out_all.reshape(streams, rows, model).astype(F32)
-
+    g_attn_own = over_ranks(added(attn_got), grad_frames)
+    grad_cross_mem = g_attn_own[3:]
+    for back in ffn_back:
+        ffn_total += back.astype(F32)
+    grad_ffn_up = ffn_total[0]
+    grad_ffn_down = ffn_total[1].T
+    grad_self_out = g_attn_own[0].T
+    grad_cross_query = g_attn_own[1]
+    grad_cross_out = g_attn_own[2].T
     return (
         out_frames,
         grad_frames,

time: 664 us -> 606 us (0.913)
  blocking collectives: 61.7 us -> 0 us
  local copies, waits for them, and re-layouts: 62.2 us -> 71.4 us
  other arithmetic: 41.1 us -> 34.4 us
    all_to_all x1 -> x0, blocking collectives: 61.7 us -> none  [over_chips(): return lax.all_to_all(blocks, 'blk', 0, 0, axis_index_groups=plane)]
    all_to_all x2 -> x4, waiting for transfers between devices: 0.01 us -> 27.4 us  [over_chips(): return lax.all_to_all(blocks, 'blk', 0, 0, axis_index_groups=plane)]
    all_to_all x1, waiting for transfers between devices: 23.6 us -> 3.41 us  [shards(): lax.all_to_all(pieces.reshape(blk, group, rows, 3 * width), 'blk', 0, 0)]
    all_gather x1, waiting for transfers between devices: 0.01 us -> 20 us  [shards(): shared = lax.all_gather(shared, 'tp')]
    ppermute x15, waiting for transfers between devices: 63.7 us -> 47.1 us  [from_ranks(): lax.ppermute(values[j], 'tp', swapped(tp, j))]
    ppermute x1, waiting for transfers between devices: 15.6 us -> 3.38 us  [shards(): h3_other = lax.ppermute(h3, 'tp', swap)]
    all_to_all x2 -> x4, starting transfers between devices: 8.45 us -> 17 us  [over_chips(): return lax.all_to_all(blocks, 'blk', 0, 0, axis_index_groups=plane)]
    unnamed x80 -> x115, local copies, waits for them, and re-layouts: 27.7 us -> 31.7 us
  transfers between devices with their start and end apart: 52 -> 57, of which waited for: 23 -> 29; matrix products, arithmetic and copies ran while one was open for 12% -> 12% of each run, Pallas kernels for 20% -> 23%
where the time goes in v3:
time: 606 us; the launch traced here: 599 us
  waiting for transfers between devices  224 us (37%)
  Pallas kernels  172 us (28%)
  starting transfers between devices  82.7 us (14%)
  local copies, waits for them, and re-layouts  71.4 us (12%)
  other arithmetic  34.4 us (6%)
  between operations  14.6 us (2%)
    pallas_call x21, Pallas kernels, call(): pl.pallas_call(body, out_shape=[o for o, _ in outs], grid_spec=pltpu.Pref...  172 us
    ppermute x15, waiting for transfers between devices, from_ranks(): lax.ppermute(values[j], 'tp', swapped(tp, j))  47.1 us
    ppermute x6, waiting for transfers between devices, from_chips(): lax.ppermute(blocks[j], 'blk', swapped(blk, 2 * j))  43.2 us
    unnamed x115, local copies, waits for them, and re-layouts  31.7 us
    all_to_all x4, waiting for transfers between devices, over_chips(): return lax.all_to_all(blocks, 'blk', 0, 0, axis_index_groups=plane)  27.4 us
    ppermute x1, waiting for transfers between devices, shards(): lax.ppermute(piece, 'tp', swapped(tp, 2 * j))  25 us
    ppermute x15, starting transfers between devices, from_ranks(): lax.ppermute(values[j], 'tp', swapped(tp, j))  24.4 us
    all_gather x1, waiting for transfers between devices, shards(): shared = lax.all_gather(shared, 'tp')  20 us
  transfers between devices with their start and end apart: 57, of which 29 were waited for; matrix products, arithmetic and copies ran while one was open for 12% of the time, Pallas kernels for 23%

profile of v3, /device:TPU:0, one launch (start us, length us, event | category | flops | bytes accessed | tf_op | source)
XLA Modules:
  0.0 598.7 jit_solution(7216777903548390309)
XLA Ops:
  15.3 6.8 %qkv.1 = (bf16[4,2,320,384]{3,2,1,0:T(8,128)(2,1)}, bf16[1280,1024]{1,0:T(8,128)(2,1)}) custom-call(bf16[20,64,1024]{2,1,0:T(8,128)(2,1)} %refs_0_.1, f32[2,1024]{1,0:T(2,128)} %pad_maximum_fusion.5.refs_1_.refs_3_, bf16[3,1024,256]{2,1,0:T(8,128)(2,1)} %refs_1_.1, bf16[128,1280]{1,0:T(8,128)(2,1)} %copy-done.39, ...), custom_call_target="tpu_custom_call" | custom-call | flops 2013265920 | bytes 8790016 | tf_op jit(solution)/shard_map/qkv/pallas_call | solution.py:43
  22.1 5.2 all-to-all-start
  27.3 20.0 %all-gather.11.cloned.1.call-done = bf16[512,1280]{1,0:T(8,128)(2,1)} async-done(((bf16[128,1280]{1,0:T(8,128)(2,1)}), bf16[512,1280]{1,0:T(8,128)(2,1)}) %all-gather.11.cloned.1.call-update) | async-done | bytes 1310736 | tf_op jit(solution)/shard_map/all_gather | solution.py:749
  49.1 3.4 all-to-all-done.refs_1_
  53.8 2.6 broadcast_in_dim.20
  56.4 3.7 all-to-all-start.1
  61.0 7.5 %self_forward.1.refs_0_ = bf16[8,5,64,128]{3,2,1,0:T(8,128)(2,1)} custom-call(s32[5,2]{1,0:T(8,128)} %get-tuple-element.167.refs_0_, bf16[8,5,64,384]{3,2,1,0:T(8,128)(2,1)} %copy-done.9), custom_call_target="tpu_custom_call" | custom-call | flops 671088640 | bytes 2621440 | tf_op jit(solution)/shard_map/self_forward/pallas_call | solution.py:43
  68.5 15.8 %all-to-all-done.1.refs_1_.refs_2_ = bf16[4,4,128,512]{3,2,1,0:T(8,128)(2,1)S(1)} async-done(((bf16[4,4,128,512]{3,2,1,0:T(8,128)(2,1)}), bf16[4,4,128,512]{3,2,1,0:T(8,128)(2,1)S(1)}, u32[]{:S(2)}, u32[]{:S(2)}) %all-to-all-start.1) | async-done | bytes 2097184 | tf_op jit(solution)/shard_map/all_to_all | solution.py:690
  85.6 3.7 all-to-all-start.2
  89.3 11.1 %all-to-all-done.2 = bf16[8,5,64,128]{3,2,1,0:T(8,128)(2,1)S(1)} async-done(((bf16[8,5,64,128]{3,2,1,0:T(8,128)(2,1)}), bf16[8,5,64,128]{3,2,1,0:T(8,128)(2,1)S(1)}, u32[]{:S(2)}, u32[]{:S(2)}) %all-to-all-start.2) | async-done | bytes 655392 | tf_op jit(solution)/shard_map/all_to_all | solution.py:757
  101.1 3.6 collective-permute-start.2
  106.4 3.2 collective-permute-done.2.refs_4_.refs_8_
  109.6 6.1 %collective-permute-done.1.refs_3_.refs_7_ = bf16[2,320,128]{2,1,0:T(8,128)(2,1)S(1)} collective-permute-done((bf16[2,320,128]{2,1,0:T(8,128)(2,1)S(1)}, bf16[2,320,128]{2,1,0:T(8,128)(2,1)S(1)}, u32[]{:S(2)}, u32[]{:S(2)}) %collective-permute-start.1) | collective-permute-done | bytes 163872 | tf_op jit(solution)/shard_map/ppermute | solution.py:686
  116.4 3.1 broadcast_in_dim.21
  119.5 4.9 all-to-all-start.3
  124.5 25.0 %collective-permute-done.5.refs_0_ = bf16[128,2048]{1,0:T(8,128)(2,1)} collective-permute-done((bf16[128,2048]{1,0:T(8,128)(2,1)}, bf16[128,2048]{1,0:T(8,128)(2,1)}, u32[]{:S(2)}, u32[]{:S(2)}) %collective-permute-start.5) | collective-permute-done | bytes 524320 | tf_op jit(solution)/shard_map/ppermute | solution.py:771
  149.5 11.4 %all-to-all-done.3.refs_3_.refs_5_.refs_1_.refs_9_.refs_11_ = bf16[4,4,128,768]{3,2,1,0:T(8,128)(2,1)S(1)} async-done(((bf16[4,4,128,768]{3,2,1,0:T(8,128)(2,1)}), bf16[4,4,128,768]{3,2,1,0:T(8,128)(2,1)S(1)}, u32[]{:S(2)}, u32[]{:S(2)}) %all-to-all-start.3) | async-done | bytes 3145760 | tf_op jit(solution)/shard_map/all_to_all | solution.py:690
  167.3 2.6 constant_dynamic-slice_fusion.9
  171.3 7.7 %memory.1.refs_9_ = bf16[640,2048]{1,0:T(8,128)(2,1)} custom-call(s32[2]{0:T(128)} %pad_add_fusion.refs_0_, bf16[640,1024]{1,0:T(8,128)(2,1)} %bitcast.130, bf16[4,4,128,512]{3,2,1,0:T(8,128)(2,1)} %copy-done.6, bf16[4,4,128,512]{3,2,1,0:T(8,128)(2,1)} %collective-permute-done.4.refs_3_), custom_call_target="tpu_custom_call" | custom-call | flops 2684354560 | bytes 8126464 | tf_op jit(solution)/shard_map/memory/pallas_call | solution.py:43
  180.6 6.8 %to_cross.1 = (f32[320,1024]{1,0:T(8,128)}, bf16[320,1024]{1,0:T(8,128)(2,1)}, bf16[320,1024]{1,0:T(8,128)(2,1)}, bf16[320,1024]{1,0:T(8,128)(2,1)}) custom-call(s32[2]{0:T(128)} %pad_add_fusion.refs_0_, bf16[320,1024]{1,0:T(8,128)(2,1)} %bitcast.119, f32[2,1024]{1,0:T(2,128)} %get-tuple-element.173.refs_2_, bf16[4,4,128,768]{3,2,1,0:T(8,128)(2,1)} %copy-done.2, ...), custom_call_target="tpu_custom_call" | custom-call | flops 1342177280 | bytes 10887168 | tf_op jit(solution)/shard_map/to_cross/pallas_call | solution.py:43
  187.4 10.3 %cross_forward.1 = (bf16[320,1024]{1,0:T(8,128)(2,1)}, f32[320,1024]{1,0:T(8,128)}, bf16[320,1024]{1,0:T(8,128)(2,1)}) custom-call(s32[5,7]{1,0:T(8,128)} %concatenate.12.refs_0_, f32[320,1024]{1,0:T(8,128)} %get-tuple-element.60.refs_1_.refs_5_, bf16[320,1024]{1,0:T(8,128)(2,1)} %get-tuple-element.61.refs_2_.refs_6_, bf16[5,128,2048]{2,1,0:T(8,128)(2,1)} %bitcast.115, ...), custom_call_target="tpu_custom_call" | custom-call | flops 838860800 | bytes 13508608 | tf_op jit(solution)/shard_map/cross_forward/pallas_call | solution.py:43
  199.4 12.1 %feed_forward.2 = (bf16[320,2048]{1,0:T(8,128)(2,1)}, bf16[320,2048]{1,0:T(8,128)(2,1)}, f32[320,1024]{1,0:T(8,128)}, f32[320,1024]{1,0:T(8,128)}) custom-call(bf16[320,1024]{1,0:T(8,128)(2,1)} %get-tuple-element.63.refs_0_.refs_1_.refs_2_.refs_3_.refs_4_, bf16[320,1024]{1,0:T(8,128)(2,1)} %bitcast.94, bf16[1024,1024]{1,0:T(8,128)(2,1)} %refs_2_.5, ...), custom_call_target="tpu_custom_call" | custom-call | flops 5368709120 | bytes 19136512 | tf_op jit(solution)/shard_map/feed_forward/pallas_call | solution.py:43
  211.5 3.4 collective-permute-done.6.refs_0_.refs_6_.refs_7_.refs_8_.refs_9_
  215.8 11.6 %feed_forward.3 = (bf16[320,2048]{1,0:T(8,128)(2,1)}, bf16[320,2048]{1,0:T(8,128)(2,1)}, bf16[2,320,1024]{2,1,0:T(8,128)(2,1)}) custom-call(bf16[320,1024]{1,0:T(8,128)(2,1)} %copy-done.4, bf16[320,1024]{1,0:T(8,128)(2,1)} %bitcast.104, bf16[1024,1024]{1,0:T(8,128)(2,1)} %refs_2_.5, bf16[1024,1024]{1,0:T(8,128)(2,1)} %refs_3_.3, ...), custom_call_target="tpu_custom_call" | custom-call | flops 5368709120 | bytes 17825792 | tf_op jit(solution)/shard_map/feed_forward/pallas_call | solution.py:43
  227.4 9.4 %weight_grad.6 = (bf16[2,128,2048]{2,1,0:T(8,128)(2,1)}, bf16[2,128,2048]{2,1,0:T(8,128)(2,1)}, bf16[2,128,2048]{2,1,0:T(8,128)(2,1)}, bf16[2,128,2048]{2,1,0:T(8,128)(2,1)}) custom-call(s32[4]{0:T(128)} %add_subtract_fusion.1.refs_0_, bf16[320,1024]{1,0:T(8,128)(2,1)} %get-tuple-element.63.refs_0_.refs_1_.refs_2_.refs_3_.refs_4_, ...), custom_call_target="tpu_custom_call" | custom-call | flops 2684354560 | bytes 19922944 | tf_op jit(solution)/shard_map/weight_grad/pallas_call | solution.py:43
  245.2 10.2 %weight_grad.7.refs_13_ = bf16[4,2,128,2048]{3,2,1,0:T(8,128)(2,1)} custom-call(s32[4]{0:T(128)} %fusion.8.refs_0_, bf16[320,1024]{1,0:T(8,128)(2,1)} %get-tuple-element.63.refs_0_.refs_1_.refs_2_.refs_3_.refs_4_, bf16[320,1024]{1,0:T(8,128)(2,1)} %get-tuple-element.63.refs_0_.refs_1_.refs_2_.refs_3_.refs_4_, ...), custom_call_target="tpu_custom_call" | custom-call | flops 2684354560 | bytes 24117248 | tf_op jit(solution)/shard_map/weight_grad/pallas_call | solution.py:43
  255.4 4.8 all-to-all-start.4
  260.3 8.3 %collective-permute-done.7.refs_2_ = bf16[2,320,1024]{2,1,0:T(8,128)(2,1)S(1)} collective-permute-done((bf16[2,320,1024]{2,1,0:T(8,128)(2,1)S(1)}, bf16[2,320,1024]{2,1,0:T(8,128)(2,1)S(1)}, u32[]{:S(2)}, u32[]{:S(2)}) %collective-permute-start.7) | collective-permute-done | bytes 1310752 | tf_op jit(solution)/shard_map/ppermute | solution.py:863
  269.7 17.2 %cross_backward.1 = (bf16[320,1024]{1,0:T(8,128)(2,1)}, bf16[320,1024]{1,0:T(8,128)(2,1)}, f32[320,1024]{1,0:T(8,128)}, bf16[320,1024]{1,0:T(8,128)(2,1)}, bf16[...) custom-call(s32[5,7]{1,0:T(8,128)} %concatenate.12.refs_0_, ...), custom_call_target="tpu_custom_call" | custom-call | flops 2432696320 | bytes 28340224 | tf_op jit(solution)/shard_map/cross_backward/pallas_call | solution.py:43
  288.2 2.3 collective-permute-start.14
  292.6 2.7 dynamic-slice_bitcast_fusion
  297.3 6.7 %collective-permute-done.13.refs_2_ = bf16[2,320,128]{2,1,0:T(8,128)(2,1)S(1)} collective-permute-done((bf16[2,320,128]{2,1,0:T(8,128)(2,1)S(1)}, bf16[2,320,128]{2,1,0:T(8,128)(2,1)S(1)}, u32[]{:S(2)}, u32[]{:S(2)}) %collective-permute-start.13) | collective-permute-done | bytes 163872 | tf_op jit(solution)/shard_map/ppermute | solution.py:686
  308.2 3.8 all-to-all-start.5
  312.1 2.9 fusion.refs_0_
  315.0 8.1 %all-to-all-done.5.refs_2_.refs_1_ = bf16[8,5,64,128]{3,2,1,0:T(8,128)(2,1)S(1)} async-done(((bf16[8,5,64,128]{3,2,1,0:T(8,128)(2,1)}), bf16[8,5,64,128]{3,2,1,0:T(8,128)(2,1)S(1)}, u32[]{:S(2)}, u32[]{:S(2)}) %all-to-all-start.5) | async-done | bytes 655392 | tf_op jit(solution)/shard_map/all_to_all | solution.py:928
  323.9 3.5 all-to-all-start.6
  327.5 16.5 %self_backward.1.refs_4_ = bf16[8,5,64,384]{3,2,1,0:T(8,128)(2,1)} custom-call(s32[5,2]{1,0:T(8,128)} %get-tuple-element.167.refs_0_, bf16[8,5,64,384]{3,2,1,0:T(8,128)(2,1)} %copy-done.9, bf16[8,5,64,128]{3,2,1,0:T(8,128)(2,1)} %copy-done.15), custom_call_target="tpu_custom_call" | custom-call | flops 1342177280 | bytes 4587520 | tf_op jit(solution)/shard_map/self_backward/pallas_call | solution.py:43
  344.0 3.0 copy.104.refs_0_
  348.0 4.6 all-to-all-start.7
  354.8 5.3 text_grad.1.refs_26_
  360.1 6.8 %weight_grad.8 = (bf16[5,128,1024]{2,1,0:T(8,128)(2,1)}, bf16[5,128,1024]{2,1,0:T(8,128)(2,1)}, bf16[5,128,1024]{2,1,0:T(8,128)(2,1)}, bf16[5,128,1024]{2,1,0:T(8,128)(2,1)}) custom-call(s32[4]{0:T(128)} %add_subtract_fusion.refs_0_, bf16[320,1024]{1,0:T(8,128)(2,1)} %get-tuple-element.77.refs_1_.refs_2_.refs_3_.refs_4_, ...), custom_call_target="tpu_custom_call" | custom-call | flops 1174405120 | bytes 17039360 | tf_op jit(solution)/shard_map/weight_grad/pallas_call | solution.py:43
  368.0 3.6 ffn_sum.1
  376.0 7.9 %weight_grad.9 = (bf16[5,128,1024]{2,1,0:T(8,128)(2,1)}, bf16[5,128,1024]{2,1,0:T(8,128)(2,1)}, bf16[5,128,1024]{2,1,0:T(8,128)(2,1)}, bf16[5,128,1024]{2,1,0:T(8,128)(2,1)}) custom-call(s32[4]{0:T(128)} %fusion.9.refs_0_, bf16[320,1024]{1,0:T(8,128)(2,1)} %get-tuple-element.77.refs_1_.refs_2_.refs_3_.refs_4_, ...), custom_call_target="tpu_custom_call" | custom-call | flops 1174405120 | bytes 22282240 | tf_op jit(solution)/shard_map/weight_grad/pallas_call | solution.py:43
  384.0 14.1 %collective-permute-done.20.refs_3_ = bf16[2,128,1024]{2,1,0:T(8,128)(2,1)} collective-permute-done((bf16[2,128,1024]{2,1,0:T(8,128)(2,1)}, bf16[2,128,1024]{2,1,0:T(8,128)(2,1)}, u32[]{:S(2)}, u32[]{:S(2)}) %collective-permute-start.20) | collective-permute-done | bytes 524320 | tf_op jit(solution)/shard_map/ppermute | solution.py:962
  399.3 5.9 qkv_grad.1
  405.2 4.5 all-to-all-start.8
  413.4 4.8 weight_grad.10
  421.5 3.7 collective-permute-start.30
  425.2 16.6 %collective-permute-done.21.refs_10_.refs_4_ = bf16[5,128,1024]{2,1,0:T(8,128)(2,1)S(1)} collective-permute-done((bf16[5,128,1024]{2,1,0:T(8,128)(2,1)}, bf16[5,128,1024]{2,1,0:T(8,128)(2,1)S(1)}, u32[]{:S(2)}, u32[]{:S(2)}) %collective-permute-start.21) | collective-permute-done | bytes 1310752 | tf_op jit(solution)/shard_map/ppermute | solution.py:712
  443.6 26.7 %collective-permute-done.22.refs_11_.refs_5_ = bf16[5,128,1024]{2,1,0:T(8,128)(2,1)S(1)} collective-permute-done((bf16[5,128,1024]{2,1,0:T(8,128)(2,1)}, bf16[5,128,1024]{2,1,0:T(8,128)(2,1)S(1)}, u32[]{:S(2)}, u32[]{:S(2)}) %collective-permute-start.22) | collective-permute-done | bytes 1310752 | tf_op jit(solution)/shard_map/ppermute | solution.py:712
  471.4 4.8 weight_grad.11
  476.9 6.8 %collective-permute-done.29.refs_0_ = bf16[80,1024]{1,0:T(8,128)(2,1)S(1)} collective-permute-done((bf16[80,1024]{1,0:T(8,128)(2,1)S(1)}, bf16[80,1024]{1,0:T(8,128)(2,1)S(1)}, u32[]{:S(2)}, u32[]{:S(2)}) %collective-permute-start.29) | collective-permute-done | bytes 163872 | tf_op jit(solution)/shard_map/ppermute | solution.py:686
  487.6 5.0 to_frames.1.refs_1_
  492.7 3.8 all-to-all-start.9
  496.6 4.8 convert.8
  503.6 5.0 first_norm.1
  514.7 5.4 add_convert_fusion
  520.1 2.4 copy.77
  527.8 2.2 constant_dynamic-slice_fusion.4
  537.4 2.4 collective-permute-start.41
  541.5 3.0 collective-permute-start.36
  546.8 23.5 %collective-permute-done.35 = f32[6,128]{1,0:T(8,128)S(1)} collective-permute-done((f32[6,128]{1,0:T(8,128)S(1)}, f32[6,128]{1,0:T(8,128)S(1)}, u32[]{:S(2)}, u32[]{:S(2)}) %collective-permute-start.35) | collective-permute-done | bytes 3104 | tf_op jit(solution)/shard_map/ppermute | solution.py:686
  572.7 7.0 %text_out.1 = f32[4,640,1024]{2,1,0:T(8,128)} custom-call(bf16[8,4,80,1024]{3,2,1,0:T(8,128)(2,1)} %bitcast.123), custom_call_target="tpu_custom_call" | custom-call | bytes 15728640 | tf_op jit(solution)/shard_map/text_out/pallas_call | solution.py:43
  581.3 4.7 convert.6.refs_1_
  (274 shorter events, 107.9 us)
Async XLA Ops:
  7.2 156.0 %copy-start = (s32[20,2]{0,1:T(2,128)S(1)}, s32[20,2]{0,1:T(2,128)}, u32[]{:S(2)}) copy-start(s32[20,2]{0,1:T(2,128)} %param.17) | copy-start | bytes 484
  7.2 40.0 %all-gather.11.cloned.1.call-start = ((), (), s32[]{:S(2)}) async-start(), calls=%async_computation.12 | async-start | bytes 1638400 | tf_op jit(solution)/shard_map/all_gather | solution.py:749
  22.1 30.4 %all-to-all-start = ((bf16[8,5,64,384]{3,2,1,0:T(8,128)(2,1)}), bf16[8,5,64,384]{3,2,1,0:T(8,128)(2,1)S(1)}, u32[]{:S(2)}, u32[]{:S(2)}) async-start(bf16[8,5,64,384]{3,2,1,0:T(8,128)(2,1)} %bitcast.129), calls=%async_computation | async-start | bytes 3932160 | tf_op jit(solution)/shard_map/all_to_all | solution.py:744
  56.4 27.9 %all-to-all-start.1 = ((bf16[4,4,128,512]{3,2,1,0:T(8,128)(2,1)}), bf16[4,4,128,512]{3,2,1,0:T(8,128)(2,1)S(1)}, u32[]{:S(2)}, u32[]{:S(2)}) async-start(bf16[4,4,128,512]{3,2,1,0:T(8,128)(2,1)} %broadcast_in_dim.20), calls=%async_computation.1 | async-start | bytes 4194304 | tf_op jit(solution)/shard_map/all_to_all | solution.py:690
  85.6 19.9 %copy-start.24 = (bf16[512,1280]{1,0:T(8,128)(2,1)S(1)}, bf16[512,1280]{1,0:T(8,128)(2,1)}, u32[]{:S(2)}) copy-start(bf16[512,1280]{1,0:T(8,128)(2,1)} %all-gather.11.cloned.1.call-done) | copy-start | bytes 3932164
  85.6 14.8 %all-to-all-start.2 = ((bf16[8,5,64,128]{3,2,1,0:T(8,128)(2,1)}), bf16[8,5,64,128]{3,2,1,0:T(8,128)(2,1)S(1)}, u32[]{:S(2)}, u32[]{:S(2)}) async-start(bf16[8,5,64,128]{3,2,1,0:T(8,128)(2,1)} %tied.20), calls=%async_computation.2 | async-start | bytes 1310720 | tf_op jit(solution)/shard_map/all_to_all | solution.py:757
  101.1 8.6 %collective-permute-start.2 = (bf16[2,320,128]{2,1,0:T(8,128)(2,1)S(1)}, bf16[2,320,128]{2,1,0:T(8,128)(2,1)S(1)}, u32[]{:S(2)}, u32[]{:S(2)}) collective-permute-start(bf16[2,320,128]{2,1,0:T(8,128)(2,1)S(1)} %get-tuple-element.157), channel_id=1, source_target_pairs={{0,3},{1,2},{2,1},{3,0},{4,7},{5,6},{6,5},{7,4},{8,11},{9,10},{10,... | collective-permute-start | bytes 491528 | tf_op jit(solution)/shard_map/ppermute | solution.py:686
  104.7 11.0 %collective-permute-start.1 = (bf16[2,320,128]{2,1,0:T(8,128)(2,1)S(1)}, bf16[2,320,128]{2,1,0:T(8,128)(2,1)S(1)}, u32[]{:S(2)}, u32[]{:S(2)}) collective-permute-start(bf16[2,320,128]{2,1,0:T(8,128)(2,1)S(1)} %get-tuple-element.158), channel_id=1, source_target_pairs={{0,2},{1,3},{2,0},{3,1},{4,6},{5,7},{6,4},{7,5},{8,10},{9,11},{10,... | collective-permute-start | bytes 491528 | tf_op jit(solution)/shard_map/ppermute | solution.py:686
  104.7 11.0 %collective-permute-start = (bf16[2,320,128]{2,1,0:T(8,128)(2,1)S(1)}, bf16[2,320,128]{2,1,0:T(8,128)(2,1)S(1)}, u32[]{:S(2)}, u32[]{:S(2)}) collective-permute-start(bf16[2,320,128]{2,1,0:T(8,128)(2,1)S(1)} %get-tuple-element.159), channel_id=1, source_target_pairs={{0,1},{1,0},{2,3},{3,2},{4,5},{5,4},{6,7},{7,6},{8,9},{9,8},{10,11... | collective-permute-start | bytes 491528 | tf_op jit(solution)/shard_map/ppermute | solution.py:686
  119.5 41.4 %all-to-all-start.3 = ((bf16[4,4,128,768]{3,2,1,0:T(8,128)(2,1)}), bf16[4,4,128,768]{3,2,1,0:T(8,128)(2,1)S(1)}, u32[]{:S(2)}, u32[]{:S(2)}) async-start(bf16[4,4,128,768]{3,2,1,0:T(8,128)(2,1)} %broadcast_in_dim.21), calls=%async_computation.3 | async-start | bytes 6291456 | tf_op jit(solution)/shard_map/all_to_all | solution.py:690
  124.4 75.0 %all-gather.7.cloned.1.call-start = ((), (), s32[]{:S(2)}) async-start(), calls=%async_computation.10 | async-start | bytes 4718592 | tf_op jit(solution)/shard_map/all_gather | solution.py:773
  124.4 25.1 %collective-permute-start.5 = (bf16[128,2048]{1,0:T(8,128)(2,1)}, bf16[128,2048]{1,0:T(8,128)(2,1)}, u32[]{:S(2)}, u32[]{:S(2)}) collective-permute-start(bf16[128,2048]{1,0:T(8,128)(2,1)} %tied.22), channel_id=1, source_target_pairs={{0,2},{1,3},{2,0},{3,1},{4,6},{5,7},{6,4},{7,5},{8,10},{9,11},{10,... | collective-permute-start | bytes 1572872 | tf_op jit(solution)/shard_map/ppermute | solution.py:771
  162.6 16.4 %collective-permute-start.3 = (bf16[4,4,128,768]{3,2,1,0:T(8,128)(2,1)}, bf16[4,4,128,768]{3,2,1,0:T(8,128)(2,1)S(1)}, u32[]{:S(2)}, u32[]{:S(2)}) collective-permute-start(bf16[4,4,128,768]{3,2,1,0:T(8,128)(2,1)} %copy-done.2), channel_id=1, source_target_pairs={{0,4},{4,0},{8,12},{12,8},{16,20},{20,16},{24,28},{28,24},{1,5},{5... | collective-permute-start | bytes 9437192 | tf_op jit(solution)/shard_map/ppermute | solution.py:693
  162.7 8.6 %collective-permute-start.4 = (bf16[4,4,128,512]{3,2,1,0:T(8,128)(2,1)}, bf16[4,4,128,512]{3,2,1,0:T(8,128)(2,1)}, u32[]{:S(2)}, u32[]{:S(2)}) collective-permute-start(bf16[4,4,128,512]{3,2,1,0:T(8,128)(2,1)} %copy-done.6), channel_id=1, source_target_pairs={{0,4},{4,0},{8,12},{12,8},{16,20},{20,16},{24,28},{28,24},{1,5},{5... | collective-permute-start | bytes 6291464 | tf_op jit(solution)/shard_map/ppermute | solution.py:693
  197.7 17.2 %collective-permute-start.6 = (bf16[320,1024]{1,0:T(8,128)(2,1)}, bf16[320,1024]{1,0:T(8,128)(2,1)S(1)}, u32[]{:S(2)}, u32[]{:S(2)}) collective-permute-start(bf16[320,1024]{1,0:T(8,128)(2,1)} %get-tuple-element.63.refs_0_.refs_1_.refs_2_.refs_3_.refs_4_), channel_id=1, source_target_pairs={{0,1},{1,0},{2,3},{3,2},{4,5},{5,4},{6,7},{7,6},{8,9},{9,8},{10,11... | collective-permute-start | bytes 1966088 | tf_op jit(solution)/shard_map/ppermute | solution.py:855
  236.8 2.9 collective-permute-start.8
  236.8 4.4 collective-permute-start.9
  237.3 5.4 collective-permute-start.10
  237.4 6.8 %collective-permute-start.11 = (bf16[2,128,2048]{2,1,0:T(8,128)(2,1)}, bf16[2,128,2048]{2,1,0:T(8,128)(2,1)S(1)}, u32[]{:S(2)}, u32[]{:S(2)}) collective-permute-start(bf16[2,128,2048]{2,1,0:T(8,128)(2,1)} %get-tuple-element.74), channel_id=1, source_target_pairs={{0,4},{4,0},{8,12},{12,8},{16,20},{20,16},{24,28},{28,24},{1,5},{5... | collective-permute-start | bytes 3145736 | tf_op jit(solution)/shard_map/ppermute | solution.py:693
  237.8 30.8 %collective-permute-start.7 = (bf16[2,320,1024]{2,1,0:T(8,128)(2,1)S(1)}, bf16[2,320,1024]{2,1,0:T(8,128)(2,1)S(1)}, u32[]{:S(2)}, u32[]{:S(2)}) collective-permute-start(bf16[2,320,1024]{2,1,0:T(8,128)(2,1)S(1)} %copy-done.49), channel_id=1, source_target_pairs={{0,1},{1,0},{2,3},{3,2},{4,5},{5,4},{6,7},{7,6},{8,9},{9,8},{10,11... | collective-permute-start | bytes 3932168 | tf_op jit(solution)/shard_map/ppermute | solution.py:863
  255.4 52.8 %all-to-all-start.4 = ((bf16[4,2,128,2048]{3,2,1,0:T(8,128)(2,1)}), bf16[4,2,128,2048]{3,2,1,0:T(8,128)(2,1)}, u32[]{:S(2)}, u32[]{:S(2)}) async-start(bf16[4,2,128,2048]{3,2,1,0:T(8,128)(2,1)} %weight_grad.7.refs_13_), calls=%async_computation.4 | async-start | bytes 8388608 | tf_op jit(solution)/shard_map/all_to_all | solution.py:690
  260.2 111.3 %all-gather.9.cloned.1.call-start = ((), (), s32[]{:S(2)}) async-start(), calls=%async_computation.11 | async-start | bytes 3276800 | tf_op jit(solution)/shard_map/all_gather | solution.py:920
  288.2 9.1 %collective-permute-start.14 = (bf16[2,320,128]{2,1,0:T(8,128)(2,1)S(1)}, bf16[2,320,128]{2,1,0:T(8,128)(2,1)S(1)}, u32[]{:S(2)}, u32[]{:S(2)}) collective-permute-start(bf16[2,320,128]{2,1,0:T(8,128)(2,1)S(1)} %get-tuple-element.154), channel_id=1, source_target_pairs={{0,3},{1,2},{2,1},{3,0},{4,7},{5,6},{6,5},{7,4},{8,11},{9,10},{10,... | collective-permute-start | bytes 491528 | tf_op jit(solution)/shard_map/ppermute | solution.py:686
  290.4 13.5 %collective-permute-start.13 = (bf16[2,320,128]{2,1,0:T(8,128)(2,1)S(1)}, bf16[2,320,128]{2,1,0:T(8,128)(2,1)S(1)}, u32[]{:S(2)}, u32[]{:S(2)}) collective-permute-start(bf16[2,320,128]{2,1,0:T(8,128)(2,1)S(1)} %get-tuple-element.155), channel_id=1, source_target_pairs={{0,2},{1,3},{2,0},{3,1},{4,6},{5,7},{6,4},{7,5},{8,10},{9,11},{10,... | collective-permute-start | bytes 491528 | tf_op jit(solution)/shard_map/ppermute | solution.py:686
  290.4 13.5 %collective-permute-start.12 = (bf16[2,320,128]{2,1,0:T(8,128)(2,1)S(1)}, bf16[2,320,128]{2,1,0:T(8,128)(2,1)S(1)}, u32[]{:S(2)}, u32[]{:S(2)}) collective-permute-start(bf16[2,320,128]{2,1,0:T(8,128)(2,1)S(1)} %get-tuple-element.156), channel_id=1, source_target_pairs={{0,1},{1,0},{2,3},{3,2},{4,5},{5,4},{6,7},{7,6},{8,9},{9,8},{10,11... | collective-permute-start | bytes 491528 | tf_op jit(solution)/shard_map/ppermute | solution.py:686
  295.3 16.7 %collective-permute-start.15 = (bf16[4,80,2048]{2,1,0:T(8,128)(2,1)}, bf16[4,80,2048]{2,1,0:T(8,128)(2,1)}, u32[]{:S(2)}, u32[]{:S(2)}) collective-permute-start(bf16[4,80,2048]{2,1,0:T(8,128)(2,1)} %dynamic-slice_bitcast_fusion), channel_id=1, source_target_pairs={{0,4},{4,0},{8,12},{12,8},{16,20},{20,16},{24,28},{28,24},{1,5},{5... | collective-permute-start | bytes 3932168 | tf_op jit(solution)/shard_map/ppermute | solution.py:693
  308.2 14.9 %all-to-all-start.5 = ((bf16[8,5,64,128]{3,2,1,0:T(8,128)(2,1)}), bf16[8,5,64,128]{3,2,1,0:T(8,128)(2,1)S(1)}, u32[]{:S(2)}, u32[]{:S(2)}) async-start(bf16[8,5,64,128]{3,2,1,0:T(8,128)(2,1)} %tied.25), calls=%async_computation.5 | async-start | bytes 1310720 | tf_op jit(solution)/shard_map/all_to_all | solution.py:928
  323.9 23.1 %all-to-all-start.6 = ((bf16[4,80,2048]{2,1,0:T(8,128)(2,1)}), bf16[4,80,2048]{2,1,0:T(8,128)(2,1)S(1)}, u32[]{:S(2)}, u32[]{:S(2)}) async-start(bf16[4,80,2048]{2,1,0:T(8,128)(2,1)} %tied.26), calls=%async_computation.6 | async-start | bytes 2621440 | tf_op jit(solution)/shard_map/all_to_all | solution.py:690
  348.0 50.0 %all-to-all-start.7 = ((bf16[8,5,64,384]{3,2,1,0:T(8,128)(2,1)}), bf16[8,5,64,384]{3,2,1,0:T(8,128)(2,1)S(1)}, u32[]{:S(2)}, u32[]{:S(2)}) async-start(bf16[8,5,64,384]{3,2,1,0:T(8,128)(2,1)} %tied.27), calls=%async_computation.7 | async-start | bytes 3932160 | tf_op jit(solution)/shard_map/all_to_all | solution.py:946
  366.8 6.2 %collective-permute-start.16 = (bf16[5,128,1024]{2,1,0:T(8,128)(2,1)}, bf16[5,128,1024]{2,1,0:T(8,128)(2,1)S(1)}, u32[]{:S(2)}, u32[]{:S(2)}) collective-permute-start(bf16[5,128,1024]{2,1,0:T(8,128)(2,1)} %get-tuple-element.83), channel_id=1, source_target_pairs={{0,4},{4,0},{8,12},{12,8},{16,20},{20,16},{24,28},{28,24},{1,5},{5... | collective-permute-start | bytes 3932168 | tf_op jit(solution)/shard_map/ppermute | solution.py:693
  367.4 5.7 collective-permute-start.17
  367.5 6.7 %collective-permute-start.18 = (bf16[5,128,1024]{2,1,0:T(8,128)(2,1)}, bf16[5,128,1024]{2,1,0:T(8,128)(2,1)}, u32[]{:S(2)}, u32[]{:S(2)}) collective-permute-start(bf16[5,128,1024]{2,1,0:T(8,128)(2,1)} %get-tuple-element.85), channel_id=1, source_target_pairs={{0,4},{4,0},{8,12},{12,8},{16,20},{20,16},{24,28},{28,24},{1,5},{5... | collective-permute-start | bytes 3932168 | tf_op jit(solution)/shard_map/ppermute | solution.py:693
  367.9 8.1 %collective-permute-start.19 = (bf16[5,128,1024]{2,1,0:T(8,128)(2,1)}, bf16[5,128,1024]{2,1,0:T(8,128)(2,1)}, u32[]{:S(2)}, u32[]{:S(2)}) collective-permute-start(bf16[5,128,1024]{2,1,0:T(8,128)(2,1)} %get-tuple-element.86), channel_id=1, source_target_pairs={{0,4},{4,0},{8,12},{12,8},{16,20},{20,16},{24,28},{28,24},{1,5},{5... | collective-permute-start | bytes 3932168 | tf_op jit(solution)/shard_map/ppermute | solution.py:693
  371.6 26.5 %collective-permute-start.20 = (bf16[2,128,1024]{2,1,0:T(8,128)(2,1)}, bf16[2,128,1024]{2,1,0:T(8,128)(2,1)}, u32[]{:S(2)}, u32[]{:S(2)}) collective-permute-start(bf16[2,128,1024]{2,1,0:T(8,128)(2,1)} %tied.28), channel_id=1, source_target_pairs={{0,2},{1,3},{2,0},{3,1},{4,6},{5,7},{6,4},{7,5},{8,10},{9,11},{10,... | collective-permute-start | bytes 1572872 | tf_op jit(solution)/shard_map/ppermute | solution.py:962
  405.2 82.4 %all-to-all-start.8 = ((bf16[4,320,1024]{2,1,0:T(8,128)(2,1)}), bf16[4,320,1024]{2,1,0:T(8,128)(2,1)}, u32[]{:S(2)}, u32[]{:S(2)}) async-start(bf16[4,320,1024]{2,1,0:T(8,128)(2,1)} %get-tuple-element.89.refs_6_.refs_0_), calls=%async_computation.8 | async-start | bytes 5242880 | tf_op jit(solution)/shard_map/all_to_all | solution.py:1000
  409.8 163.0 %all-gather.13.cloned.1.call-start = ((), (), s32[]{:S(2)}) async-start(), calls=%async_computation.13 | async-start | bytes 5898240 | tf_op jit(solution)/shard_map/all_gather | solution.py:1032
  409.8 31.9 %collective-permute-start.21 = (bf16[5,128,1024]{2,1,0:T(8,128)(2,1)}, bf16[5,128,1024]{2,1,0:T(8,128)(2,1)S(1)}, u32[]{:S(2)}, u32[]{:S(2)}) collective-permute-start(bf16[5,128,1024]{2,1,0:T(8,128)(2,1)} %get-tuple-element.91), channel_id=1, source_target_pairs={{0,8},{4,12},{8,0},{12,4},{16,24},{20,28},{24,16},{28,20},{1,9},{5... | collective-permute-start | bytes 3932168 | tf_op jit(solution)/shard_map/ppermute | solution.py:712
  411.5 58.7 %collective-permute-start.22 = (bf16[5,128,1024]{2,1,0:T(8,128)(2,1)}, bf16[5,128,1024]{2,1,0:T(8,128)(2,1)S(1)}, u32[]{:S(2)}, u32[]{:S(2)}) collective-permute-start(bf16[5,128,1024]{2,1,0:T(8,128)(2,1)} %get-tuple-element.92), channel_id=1, source_target_pairs={{0,16},{4,20},{8,24},{12,28},{16,0},{20,4},{24,8},{28,12},{1,17},{... | collective-permute-start | bytes 3932168 | tf_op jit(solution)/shard_map/ppermute | solution.py:712
  413.0 74.6 %collective-permute-start.23 = (bf16[5,128,1024]{2,1,0:T(8,128)(2,1)}, bf16[5,128,1024]{2,1,0:T(8,128)(2,1)}, u32[]{:S(2)}, u32[]{:S(2)}) collective-permute-start(bf16[5,128,1024]{2,1,0:T(8,128)(2,1)} %get-tuple-element.93), channel_id=1, source_target_pairs={{0,24},{4,28},{8,16},{12,20},{16,8},{20,12},{24,0},{28,4},{1,25},{... | collective-permute-start | bytes 3932168 | tf_op jit(solution)/shard_map/ppermute | solution.py:712
  418.2 1.7 collective-permute-start.24
  418.2 1.9 collective-permute-start.25
  419.8 50.5 %copy-start.41 = (bf16[1,128,768]{2,1,0:T(8,128)(2,1)}, bf16[1,128,768]{2,1,0:T(8,128)(2,1)S(1)}, u32[]{:S(2)}) copy-start(bf16[1,128,768]{2,1,0:T(8,128)(2,1)S(1)} %collective-permute-done.24.refs_6_) | copy-start | bytes 589828
  419.8 1.7 collective-permute-start.26
  420.1 50.2 %copy-start.42 = (bf16[1,128,768]{2,1,0:T(8,128)(2,1)}, bf16[1,128,768]{2,1,0:T(8,128)(2,1)S(1)}, u32[]{:S(2)}) copy-start(bf16[1,128,768]{2,1,0:T(8,128)(2,1)S(1)} %collective-permute-done.25.refs_7_) | copy-start | bytes 589828
  420.1 5.0 collective-permute-start.27
  421.5 48.8 %copy-start.43 = (bf16[1,128,768]{2,1,0:T(8,128)(2,1)}, bf16[1,128,768]{2,1,0:T(8,128)(2,1)S(1)}, u32[]{:S(2)}) copy-start(bf16[1,128,768]{2,1,0:T(8,128)(2,1)S(1)} %collective-permute-done.26.refs_8_) | copy-start | bytes 589828
  421.5 54.7 %collective-permute-start.30 = (bf16[80,1024]{1,0:T(8,128)(2,1)S(1)}, bf16[80,1024]{1,0:T(8,128)(2,1)S(1)}, u32[]{:S(2)}, u32[]{:S(2)}) collective-permute-start(bf16[80,1024]{1,0:T(8,128)(2,1)S(1)} %copy-done.20), channel_id=1, source_target_pairs={{0,3},{1,2},{2,1},{3,0},{4,7},{5,6},{6,5},{7,4},{8,11},{9,10},{10,... | collective-permute-start | bytes 491528 | tf_op jit(solution)/shard_map/ppermute | solution.py:686
  425.2 45.1 %copy-start.44 = (bf16[1,128,768]{2,1,0:T(8,128)(2,1)}, bf16[1,128,768]{2,1,0:T(8,128)(2,1)S(1)}, u32[]{:S(2)}) copy-start(bf16[1,128,768]{2,1,0:T(8,128)(2,1)S(1)} %collective-permute-done.27.refs_9_) | copy-start | bytes 589828
  425.2 58.6 %collective-permute-start.29 = (bf16[80,1024]{1,0:T(8,128)(2,1)S(1)}, bf16[80,1024]{1,0:T(8,128)(2,1)S(1)}, u32[]{:S(2)}, u32[]{:S(2)}) collective-permute-start(bf16[80,1024]{1,0:T(8,128)(2,1)S(1)} %copy-done.20), channel_id=1, source_target_pairs={{0,2},{1,3},{2,0},{3,1},{4,6},{5,7},{6,4},{7,5},{8,10},{9,11},{10,... | collective-permute-start | bytes 491528 | tf_op jit(solution)/shard_map/ppermute | solution.py:686
  441.7 28.6 %copy-start.7 = (bf16[5,128,1024]{2,1,0:T(8,128)(2,1)}, bf16[5,128,1024]{2,1,0:T(8,128)(2,1)S(1)}, u32[]{:S(2)}) copy-start(bf16[5,128,1024]{2,1,0:T(8,128)(2,1)S(1)} %collective-permute-done.21.refs_10_.refs_4_) | copy-start | bytes 3932164
  441.7 42.7 %collective-permute-start.28 = (bf16[80,1024]{1,0:T(8,128)(2,1)S(1)}, bf16[80,1024]{1,0:T(8,128)(2,1)S(1)}, u32[]{:S(2)}, u32[]{:S(2)}) collective-permute-start(bf16[80,1024]{1,0:T(8,128)(2,1)S(1)} %copy-done.20), channel_id=1, source_target_pairs={{0,1},{1,0},{2,3},{3,2},{4,5},{5,4},{6,7},{7,6},{8,9},{9,8},{10,11... | collective-permute-start | bytes 491528 | tf_op jit(solution)/shard_map/ppermute | solution.py:686
  492.7 87.1 %all-to-all-start.9 = ((bf16[4,320,1024]{2,1,0:T(8,128)(2,1)}), bf16[4,320,1024]{2,1,0:T(8,128)(2,1)S(1)}, u32[]{:S(2)}, u32[]{:S(2)}) async-start(bf16[4,320,1024]{2,1,0:T(8,128)(2,1)} %to_frames.1.refs_1_), calls=%async_computation.9 | async-start | bytes 5242880 | tf_op jit(solution)/shard_map/all_to_all | solution.py:1050
  509.9 3.1 collective-permute-start.31
  513.0 13.0 %collective-permute-start.32 = (f32[6,1024]{1,0:T(8,128)S(1)}, f32[6,1024]{1,0:T(8,128)S(1)}, u32[]{:S(2)}, u32[]{:S(2)}) collective-permute-start(f32[6,1024]{1,0:T(8,128)S(1)} %add.164), channel_id=1, source_target_pairs={{0,8},{4,12},{8,0},{12,4},{16,24},{20,28},{24,16},{28,20},{1,9},{5... | collective-permute-start | bytes 73736 | tf_op jit(solution)/shard_map/ppermute | solution.py:1055
  522.5 17.2 %collective-permute-start.37 = (bf16[1,128,768]{2,1,0:T(8,128)(2,1)}, bf16[1,128,768]{2,1,0:T(8,128)(2,1)}, u32[]{:S(2)}, u32[]{:S(2)}) collective-permute-start(bf16[1,128,768]{2,1,0:T(8,128)(2,1)} %get-tuple-element.102), channel_id=1, source_target_pairs={{0,8},{4,12},{8,0},{12,4},{16,24},{20,28},{24,16},{28,20},{1,9},{5... | collective-permute-start | bytes 589832 | tf_op jit(solution)/shard_map/ppermute | solution.py:712
  522.7 17.6 %collective-permute-start.38 = (bf16[1,128,768]{2,1,0:T(8,128)(2,1)}, bf16[1,128,768]{2,1,0:T(8,128)(2,1)}, u32[]{:S(2)}, u32[]{:S(2)}) collective-permute-start(bf16[1,128,768]{2,1,0:T(8,128)(2,1)} %get-tuple-element.103), channel_id=1, source_target_pairs={{0,16},{4,20},{8,24},{12,28},{16,0},{20,4},{24,8},{28,12},{1,17},{... | collective-permute-start | bytes 589832 | tf_op jit(solution)/shard_map/ppermute | solution.py:712
  524.5 17.0 %collective-permute-start.39 = (bf16[1,128,768]{2,1,0:T(8,128)(2,1)}, bf16[1,128,768]{2,1,0:T(8,128)(2,1)}, u32[]{:S(2)}, u32[]{:S(2)}) collective-permute-start(bf16[1,128,768]{2,1,0:T(8,128)(2,1)} %get-tuple-element.104), channel_id=1, source_target_pairs={{0,24},{4,28},{8,16},{12,20},{16,8},{20,12},{24,0},{28,4},{1,25},{... | collective-permute-start | bytes 589832 | tf_op jit(solution)/shard_map/ppermute | solution.py:712
  526.0 11.3 %collective-permute-start.33 = (f32[6,1024]{1,0:T(8,128)S(1)}, f32[6,1024]{1,0:T(8,128)S(1)}, u32[]{:S(2)}, u32[]{:S(2)}) collective-permute-start(f32[6,1024]{1,0:T(8,128)S(1)} %add.165), channel_id=1, source_target_pairs={{0,16},{4,20},{8,24},{12,28},{16,0},{20,4},{24,8},{28,12},{1,17},{... | collective-permute-start | bytes 73736 | tf_op jit(solution)/shard_map/ppermute | solution.py:1055
  535.7 51.1 %collective-permute-start.40 = (bf16[5,128,256]{2,1,0:T(8,128)(2,1)}, bf16[5,128,256]{2,1,0:T(8,128)(2,1)}, u32[]{:S(2)}, u32[]{:S(2)}) collective-permute-start(bf16[5,128,256]{2,1,0:T(8,128)(2,1)} %bitcast.45), channel_id=1, source_target_pairs={{0,1},{1,0},{2,3},{3,2},{4,5},{5,4},{6,7},{7,6},{8,9},{9,8},{10,11... | collective-permute-start | bytes 983048 | tf_op jit(solution)/shard_map/ppermute | solution.py:686
  537.4 49.4 %collective-permute-start.41 = (bf16[5,128,256]{2,1,0:T(8,128)(2,1)}, bf16[5,128,256]{2,1,0:T(8,128)(2,1)}, u32[]{:S(2)}, u32[]{:S(2)}) collective-permute-start(bf16[5,128,256]{2,1,0:T(8,128)(2,1)} %bitcast.143), channel_id=1, source_target_pairs={{0,2},{1,3},{2,0},{3,1},{4,6},{5,7},{6,4},{7,5},{8,10},{9,11},{10,... | collective-permute-start | bytes 983048 | tf_op jit(solution)/shard_map/ppermute | solution.py:686
  539.8 30.5 %collective-permute-start.35 = (f32[6,128]{1,0:T(8,128)S(1)}, f32[6,128]{1,0:T(8,128)S(1)}, u32[]{:S(2)}, u32[]{:S(2)}) collective-permute-start(f32[6,128]{1,0:T(8,128)S(1)} %fusion.6), channel_id=1, source_target_pairs={{0,2},{1,3},{2,0},{3,1},{4,6},{5,7},{6,4},{7,5},{8,10},{9,11},{10,... | collective-permute-start | bytes 9224 | tf_op jit(solution)/shard_map/ppermute | solution.py:686
  540.3 31.2 %collective-permute-start.34 = (f32[6,128]{1,0:T(8,128)S(1)}, f32[6,128]{1,0:T(8,128)S(1)}, u32[]{:S(2)}, u32[]{:S(2)}) collective-permute-start(f32[6,128]{1,0:T(8,128)S(1)} %fusion.6), channel_id=1, source_target_pairs={{0,1},{1,0},{2,3},{3,2},{4,5},{5,4},{6,7},{7,6},{8,9},{9,8},{10,11... | collective-permute-start | bytes 9224 | tf_op jit(solution)/shard_map/ppermute | solution.py:686
  541.5 30.0 %collective-permute-start.36 = (f32[6,128]{1,0:T(8,128)S(1)}, f32[6,128]{1,0:T(8,128)S(1)}, u32[]{:S(2)}, u32[]{:S(2)}) collective-permute-start(f32[6,128]{1,0:T(8,128)S(1)} %fusion.6), channel_id=1, source_target_pairs={{0,3},{1,2},{2,1},{3,0},{4,7},{5,6},{6,5},{7,4},{8,11},{9,10},{10,... | collective-permute-start | bytes 9224 | tf_op jit(solution)/shard_map/ppermute | solution.py:686
  570.3 15.7 %collective-permute-start.42 = (bf16[5,128,256]{2,1,0:T(8,128)(2,1)}, bf16[5,128,256]{2,1,0:T(8,128)(2,1)S(1)}, u32[]{:S(2)}, u32[]{:S(2)}) collective-permute-start(bf16[5,128,256]{2,1,0:T(8,128)(2,1)} %bitcast.144), channel_id=1, source_target_pairs={{0,3},{1,2},{2,1},{3,0},{4,7},{5,6},{6,5},{7,4},{8,11},{9,10},{10,... | collective-permute-start | bytes 983048 | tf_op jit(solution)/shard_map/ppermute | solution.py:686
  (43 other events, 138.1 us)
Sparse Core Ops, SparseCore 0:
  11.8 35.3 all-gather.10
  162.7 35.8 all-gather.6
  305.4 53.6 all-gather.8
  492.8 46.1 all-gather.12

commit v4 on v3

--- a/solution.py
+++ b/solution.py
@@ -255,17 +255,16 @@
     per = block // rows
     for first in range(0, length, block):
         top = first + block
-        dq = jnp.zeros((block, width), F32)
-        for h in range(len(masks)):
-            q_part = q_of[h][first:top]
-            g_part = g_of[h][first:top]
-            probs = causal_probs(ends_ref, stream, slots, q_part, k[:top], first)
-            d_probs = dot(g_part, v[:top], NT)
-            delta = jnp.sum(probs * d_probs, axis=1, keepdims=True)
-            d_scores = (probs * (d_probs - delta)).astype(BF)
-            dq += dot(d_scores, k_of[h][:top], NN)
-            dk_ref[:top] += dot(d_scores, q_part, TN)
-            dv_ref[:top] += dot(probs.astype(BF), g_part, TN)
+        heads = range(len(masks))
+        q_part = [q_of[h][first:top] for h in heads]
+        g_part = [g_of[h][first:top] for h in heads]
+        d_probs = [dot(g, v[:top], NT) for g in g_part]
+        probs = [causal_probs(ends_ref, stream, slots, a, k[:top], first) for a in q_part]
+        delta = [jnp.sum(a * b, axis=1, keepdims=True) for a, b in zip(probs, d_probs)]
+        d_scores = [(a * (b - c)).astype(BF) for a, b, c in zip(probs, d_probs, delta)]
+        dq = sum(dot(a, k_of[h][:top], NN) for h, a in zip(heads, d_scores))
+        dk_ref[:top] += sum(dot(a, b, TN) for a, b in zip(d_scores, q_part))
+        dv_ref[:top] += sum(dot(a.astype(BF), b, TN) for a, b in zip(probs, g_part))
         at = first // rows
         out_ref[at : at + per, 0, :, :width] = (dq * SCALE).astype(BF).reshape(per, rows, width)
     out_ref[:, 0, :, width : 2 * width] = dk_ref[...].astype(BF).reshape(parts, rows, width)
@@ -692,8 +691,8 @@
     def other_core(values):
         return lax.ppermute(values, "blk", swapped(blk, 1))
 
-    def spread(w):
-        near = over_chips(jnp.broadcast_to(w, (chips,) + w.shape))
+    def spread(w, *first):
+        near = over_chips(tied(jnp.broadcast_to(w, (chips,) + w.shape), *first))
         return near, other_core(near)
 
     def weight_grads(sums, order, apart, deps=(), later=()):
@@ -739,7 +738,7 @@
     if slices * group > streams:
         padded = jnp.pad(frames, ((0, slices * group - streams), (0, 0), (0, 0)))
     pieces, h_all = qkv_pieces(
-        padded, norm_rows(0), self_proj, slices, per, width, deps=(shared, piece)
+        padded, norm_rows(0), self_proj, slices, per, width, deps=(shared,)
     )
     qkv = lax.all_to_all(pieces.reshape(blk, group, rows, 3 * width), "blk", 0, 0)
     all_ends = jnp.cumsum(clip_lengths, axis=1).astype(jnp.int32)
@@ -747,10 +746,14 @@
     own_ends = jnp.pad(all_ends, ((0, slices * group - streams), (0, 0)))
     own_ends = lax.dynamic_slice_in_dim(own_ends, b // per * group, group, 0)
     shared = lax.all_gather(shared, "tp")
-    memory_weights = spread(tied(shared[:, :, : 2 * local], qkv))
+    memory_weights = spread(shared[:, :, : 2 * local], qkv)
     w_mem = columns(memory_weights, 2 * local, 0)
+    ct = of_rank(cotangent, t).reshape(count, model)
+    ct_other = of_rank(cotangent, t ^ 1).reshape(count, model)
+    x = of_rank(frames, t).reshape(count, model)
+    texts = of_rank(text_states, t).reshape(mine * text_rows, model)
     attn_own = self_attention(
-        own_ends, [qkv], width, self_forward_kernel, width, 0, "self_forward"
+        own_ends, [qkv], width, self_forward_kernel, width, 0, "self_forward", deps=(ct, ct_other, x, texts)
     )
     even = slices == tp and group == mine
 
@@ -764,7 +767,7 @@
         attn = attn.reshape(tp, per, count, width)
     attn = from_ranks([at(attn, t ^ j) for j in range(tp)])
 
-    weights = spread(tied(shared[:, :, 2 * local :], *attn))
+    weights = spread(shared[:, :, 2 * local :], *attn)
     w_first = columns(weights, 2 * local, 0)
     w_cross_out = columns(weights, local, 2)
     piece = tied(piece, *attn)
@@ -783,10 +786,8 @@
         ],
         axis=1,
     )
-    x = of_rank(frames, t).reshape(count, model)
     flat = struct((count, model))
     wide = struct((count, model), F32)
-    texts = of_rank(text_states, t).reshape(mine * text_rows, model)
     tile = model // 2
     (ckv,) = call(
         memory_kernel,
@@ -853,8 +854,6 @@
 
     swap = swapped(tp, 1)
     h3_other = lax.ppermute(h3, "tp", swap)
-    ct = of_rank(cotangent, t).reshape(count, model)
-    ct_other = of_rank(cotangent, t ^ 1).reshape(count, model)
     own_weights = (ffn_up, ffn_down)
     act, d_up, d_h3, out = feed_forward(h3, ct, own_weights, ffn_others, hidden, False)
     act_other, d_up_other, pair = feed_forward(
@@ -941,9 +940,11 @@
     received = other_core(lax.dynamic_index_in_dim(d_ckv, 1 - core, 1, keepdims=False))
     d_ckv = lax.dynamic_index_in_dim(d_ckv, core, 1, keepdims=False).astype(F32)
     d_ckv = tied((d_ckv + received.astype(F32)).astype(BF), d_attn)
-    d_ckv = jnp.sum(over_chips(d_ckv).astype(F32), axis=0).astype(BF)
-
-    d_qkv = lax.all_to_all(tied(d_qkv_own, d_ckv), "blk", 0, 0)
+    ckv_got = over_chips(d_ckv)
+    d_ckv = jnp.sum(ckv_got.astype(F32), axis=0).astype(BF)
+
+    d_qkv_own = tied(d_qkv_own, ckv_got)
+    d_qkv = lax.all_to_all(d_qkv_own, "blk", 0, 0)
     texts = lax.dynamic_slice_in_dim(texts, b * part, part, 0)
     (d_text_own,) = call(
         text_grad_kernel,
@@ -953,7 +954,7 @@
         [(struct((part, model)), None)],
         scalars=(device,),
         scratch=[pltpu.VMEM((model, 2 * model), BF)],
-        deps=(d_qkv_own,),
+        deps=(d_qkv_own, ffn_total),
         flops=4 * part * model * model,
     )
     text_got = from_ranks([d_text_own] * tp)
@@ -999,10 +1000,8 @@
     parts_own = parts.reshape(padded_rows, model)[: streams * rows].reshape(tp, count, model)
     parts = lax.all_to_all(parts_own, "tp", 0, 0)
     attn_got = from_chips(attn_blocks)
-    qkv_blocks = weight_grads([[(h_all, d_qkv)]], near_chips, True, deps=(parts_own,), later=tuple(attn_got[1:3]))
+    qkv_blocks = weight_grads([[(h_all, d_qkv)]], near_chips, True, deps=(parts_own,), later=(attn_got[1],))
     qkv_got = from_chips(qkv_blocks)
-    d_text = jnp.stack([text_got[0]] + [tied(g, qkv_blocks[0]) for g in text_got[1:]])
-    d_text = d_text[jnp.arange(tp) ^ t]
 
     out_frames = out_all.reshape(streams, rows, model).astype(F32)
 
@@ -1029,7 +1028,9 @@
         deps=(*attn_got[1:], qkv_blocks[0]),
         flops=20 * count * model,
     )
-    d_text = lax.all_gather(tied(d_text, d_x), "blk")
+    d_text = jnp.stack([text_got[0]] + [tied(g, d_x) for g in text_got[1:]])
+    d_text = d_text[jnp.arange(tp) ^ t]
+    d_text = lax.all_gather(d_text, "blk")
     if part % 16:
         d_text = d_text.transpose(1, 0, 2, 3)
         grad_text = d_text.reshape(streams, slots, text, model).astype(F32)
@@ -1054,7 +1055,8 @@
     for step in (1 << i for i in range(blk.bit_length() - 1)):
         sums = sums + lax.ppermute(sums, "blk", swapped(blk, step))
     sums = lax.dynamic_slice_in_dim(sums, b * share, share, 1)
-    sums = added(from_ranks([sums] * tp))
+    mine_of, *got = from_ranks([sums] * tp)
+    sums = added([mine_of] + [tied(g, grad_frames) for g in got])
     grad_gain = jnp.stack([sums[4], sums[0], sums[1]])
     grad_bias = jnp.stack([sums[5], sums[2], sums[3]])
     g_attn_own = over_ranks(added(attn_got), grad_frames)

time: 606 us -> 591 us (0.975)
  waiting for transfers between devices: 224 us -> 211 us
    ppermute x15, waiting for transfers between devices: 47.1 us -> 23.5 us  [from_ranks(): lax.ppermute(values[j], 'tp', swapped(tp, j))]
    all_to_all x1, waiting for transfers between devices: 0.01 us -> 9.95 us  [shards(): grad_frames = tied(lax.all_to_all(d_x, 'tp', 0, 0), grad_text)]
    ppermute x15, waiting for transfers between devices: 12.3 us -> 20.6 us  [other_core(): return lax.ppermute(values, 'blk', swapped(blk, 1))]
    all_to_all x4, waiting for transfers between devices: 27.4 us -> 19.6 us  [over_chips(): return lax.all_to_all(blocks, 'blk', 0, 0, axis_index_groups=plane)]
    all_to_all x1, waiting for transfers between devices: 0.01 us -> 7.39 us  [shards(): parts = lax.all_to_all(parts_own, 'tp', 0, 0)]
    unnamed x115 -> x130, local copies, waits for them, and re-layouts: 31.7 us -> 29.3 us
  transfers between devices with their start and end apart: 57 -> 57, of which waited for: 29 -> 35; matrix products, arithmetic and copies ran while one was open for 12% -> 12% of each run, Pallas kernels for 23% -> 24%
where the time goes in v4:
time: 591 us; the launch traced here: 581 us
  waiting for transfers between devices  211 us (36%)
  Pallas kernels  169 us (29%)
  starting transfers between devices  83.1 us (14%)
  local copies, waits for them, and re-layouts  66.8 us (11%)
  other arithmetic  36.2 us (6%)
  between operations  14.6 us (2%)
    pallas_call x21, Pallas kernels, call(): pl.pallas_call(body, out_shape=[o for o, _ in outs], grid_spec=pltpu.Pref...  169 us
    ppermute x6, waiting for transfers between devices, from_chips(): lax.ppermute(blocks[j], 'blk', swapped(blk, 2 * j))  38.4 us
    unnamed x130, local copies, waits for them, and re-layouts  29.3 us
    ppermute x15, starting transfers between devices, from_ranks(): lax.ppermute(values[j], 'tp', swapped(tp, j))  25.4 us
    ppermute x1, waiting for transfers between devices, shards(): lax.ppermute(piece, 'tp', swapped(tp, 2 * j))  25.1 us
    ppermute x15, waiting for transfers between devices, from_ranks(): lax.ppermute(values[j], 'tp', swapped(tp, j))  23.5 us
    all_gather x1, waiting for transfers between devices, shards(): shared = lax.all_gather(shared, 'tp')  21.4 us
    ppermute x15, waiting for transfers between devices, other_core(): return lax.ppermute(values, 'blk', swapped(blk, 1))  20.6 us
  transfers between devices with their start and end apart: 57, of which 35 were waited for; matrix products, arithmetic and copies ran while one was open for 12% of the time, Pallas kernels for 24%

profile of v4, /device:TPU:0, one launch (start us, length us, event | category | flops | bytes accessed | tf_op | source)
XLA Modules:
  0.0 580.5 jit_solution(4217699809532058330)
XLA Ops:
  14.0 6.8 %qkv.1 = (bf16[4,2,320,384]{3,2,1,0:T(8,128)(2,1)}, bf16[1280,1024]{1,0:T(8,128)(2,1)}) custom-call(bf16[20,64,1024]{2,1,0:T(8,128)(2,1)} %refs_0_.1, f32[2,1024]{1,0:T(2,128)} %pad_maximum_fusion.5.refs_1_.refs_3_, bf16[3,1024,256]{2,1,0:T(8,128)(2,1)} %refs_1_.1, bf16[128,1280]{1,0:T(8,128)(2,1)} %copy-done.42), custom_call_target="tpu_custom_call" | custom-call | flops 2013265920 | bytes 8790016 | tf_op jit(solution)/shard_map/qkv/pallas_call | solution.py:43
  20.8 5.2 all-to-all-start
  25.9 21.4 %all-gather.11.cloned.1.call-done = bf16[512,1280]{1,0:T(8,128)(2,1)} async-done(((bf16[128,1280]{1,0:T(8,128)(2,1)}), bf16[512,1280]{1,0:T(8,128)(2,1)}) %all-gather.11.cloned.1.call-update) | async-done | bytes 1310736 | tf_op jit(solution)/shard_map/all_gather | solution.py:748
  48.4 2.8 all-to-all-done.refs_1_
  53.2 3.7 all-to-all-start.1
  59.8 2.6 constant_dynamic-slice_fusion.9
  63.6 7.5 %self_forward.1.refs_0_ = bf16[8,5,64,128]{3,2,1,0:T(8,128)(2,1)} custom-call(s32[5,2]{1,0:T(8,128)} %get-tuple-element.167.refs_0_, bf16[8,5,64,384]{3,2,1,0:T(8,128)(2,1)} %copy-done.7, bf16[320,1024]{1,0:T(8,128)(2,1)} %bitcast.94, bf16[320,1024]{1,0:T(8,128)(2,1)} %bitcast.105, bf16[320,1024]{1,0:T(8,128)(2,1)} %bitcast.120, bf16[640,1024]{1,0:T(8,128)(2,1)} %bitcast.124), custom_call_target="tpu_custom_call" | custom-call | flops 671088640 | bytes 2621440 | tf_op jit(solution)/shard_map/self_forward/pallas_call | solution.py:43
  71.1 9.9 %all-to-all-done.1.refs_1_.refs_2_ = bf16[4,4,128,512]{3,2,1,0:T(8,128)(2,1)S(1)} async-done(((bf16[4,4,128,512]{3,2,1,0:T(8,128)(2,1)}), bf16[4,4,128,512]{3,2,1,0:T(8,128)(2,1)S(1)}, u32[]{:S(2)}, u32[]{:S(2)}) %all-to-all-start.1) | async-done | bytes 2097184 | tf_op jit(solution)/shard_map/all_to_all | solution.py:689
  82.4 3.7 all-to-all-start.2
  86.1 11.1 %all-to-all-done.2 = bf16[8,5,64,128]{3,2,1,0:T(8,128)(2,1)S(1)} async-done(((bf16[8,5,64,128]{3,2,1,0:T(8,128)(2,1)}), bf16[8,5,64,128]{3,2,1,0:T(8,128)(2,1)S(1)}, u32[]{:S(2)}, u32[]{:S(2)}) %all-to-all-start.2) | async-done | bytes 655392 | tf_op jit(solution)/shard_map/all_to_all | solution.py:760
  97.8 3.6 collective-permute-start.2
  102.3 4.1 collective-permute-done.2.refs_4_.refs_8_
  106.4 6.1 %collective-permute-done.1.refs_3_.refs_7_ = bf16[2,320,128]{2,1,0:T(8,128)(2,1)S(1)} collective-permute-done((bf16[2,320,128]{2,1,0:T(8,128)(2,1)S(1)}, bf16[2,320,128]{2,1,0:T(8,128)(2,1)S(1)}, u32[]{:S(2)}, u32[]{:S(2)}) %collective-permute-start.1) | collective-permute-done | bytes 163872 | tf_op jit(solution)/shard_map/ppermute | solution.py:685
  114.5 4.9 all-to-all-start.3
  124.0 25.1 %collective-permute-done.5.refs_0_ = bf16[128,2048]{1,0:T(8,128)(2,1)} collective-permute-done((bf16[128,2048]{1,0:T(8,128)(2,1)}, bf16[128,2048]{1,0:T(8,128)(2,1)}, u32[]{:S(2)}, u32[]{:S(2)}) %collective-permute-start.5) | collective-permute-done | bytes 524320 | tf_op jit(solution)/shard_map/ppermute | solution.py:774
  149.0 6.8 %all-to-all-done.3.refs_3_.refs_5_.refs_1_.refs_9_.refs_11_ = bf16[4,4,128,768]{3,2,1,0:T(8,128)(2,1)S(1)} async-done(((bf16[4,4,128,768]{3,2,1,0:T(8,128)(2,1)}), bf16[4,4,128,768]{3,2,1,0:T(8,128)(2,1)S(1)}, u32[]{:S(2)}, u32[]{:S(2)}) %all-to-all-start.3) | async-done | bytes 3145760 | tf_op jit(solution)/shard_map/all_to_all | solution.py:689
  160.2 6.0 %collective-permute-done.4.refs_3_ = bf16[4,4,128,512]{3,2,1,0:T(8,128)(2,1)} collective-permute-done((bf16[4,4,128,512]{3,2,1,0:T(8,128)(2,1)}, bf16[4,4,128,512]{3,2,1,0:T(8,128)(2,1)}, u32[]{:S(2)}, u32[]{:S(2)}) %collective-permute-start.4) | collective-permute-done | bytes 2097184 | tf_op jit(solution)/shard_map/ppermute | solution.py:692
  166.2 7.7 %memory.1.refs_9_ = bf16[640,2048]{1,0:T(8,128)(2,1)} custom-call(s32[2]{0:T(128)} %pad_add_fusion.refs_0_, bf16[640,1024]{1,0:T(8,128)(2,1)} %bitcast.125, bf16[4,4,128,512]{3,2,1,0:T(8,128)(2,1)} %copy-done.6, bf16[4,4,128,512]{3,2,1,0:T(8,128)(2,1)} %collective-permute-done.4.refs_3_), custom_call_target="tpu_custom_call" | custom-call | flops 2684354560 | bytes 8126464 | tf_op jit(solution)/shard_map/memory/pallas_call | solution.py:43
  175.6 6.7 %to_cross.1 = (f32[320,1024]{1,0:T(8,128)}, bf16[320,1024]{1,0:T(8,128)(2,1)}, bf16[320,1024]{1,0:T(8,128)(2,1)}, bf16[320,1024]{1,0:T(8,128)(2,1)}) custom-call(s32[2]{0:T(128)} %pad_add_fusion.refs_0_, bf16[320,1024]{1,0:T(8,128)(2,1)} %bitcast.121, f32[2,1024]{1,0:T(2,128)} %get-tuple-element.173.refs_2_, bf16[4,4,128,768]{3,2,1,0:T(8,128)(2,1)} %copy-done.2, ...), custom_call_target="tpu_custom_call" | custom-call | flops 1342177280 | bytes 10887168 | tf_op jit(solution)/shard_map/to_cross/pallas_call | solution.py:43
  182.2 10.3 %cross_forward.1 = (bf16[320,1024]{1,0:T(8,128)(2,1)}, f32[320,1024]{1,0:T(8,128)}, bf16[320,1024]{1,0:T(8,128)(2,1)}) custom-call(s32[5,7]{1,0:T(8,128)} %concatenate.12.refs_0_, f32[320,1024]{1,0:T(8,128)} %get-tuple-element.60.refs_1_.refs_5_, bf16[320,1024]{1,0:T(8,128)(2,1)} %get-tuple-element.61.refs_2_.refs_6_, bf16[5,128,2048]{2,1,0:T(8,128)(2,1)} %bitcast.117, ...), custom_call_target="tpu_custom_call" | custom-call | flops 838860800 | bytes 13508608 | tf_op jit(solution)/shard_map/cross_forward/pallas_call | solution.py:43
  193.5 12.1 %feed_forward.2 = (bf16[320,2048]{1,0:T(8,128)(2,1)}, bf16[320,2048]{1,0:T(8,128)(2,1)}, f32[320,1024]{1,0:T(8,128)}, f32[320,1024]{1,0:T(8,128)}) custom-call(bf16[320,1024]{1,0:T(8,128)(2,1)} %get-tuple-element.63.refs_0_.refs_1_.refs_2_.refs_3_.refs_4_, bf16[320,1024]{1,0:T(8,128)(2,1)} %bitcast.95, bf16[1024,1024]{1,0:T(8,128)(2,1)} %refs_2_.5, ...), custom_call_target="tpu_custom_call" | custom-call | flops 5368709120 | bytes 19136512 | tf_op jit(solution)/shard_map/feed_forward/pallas_call | solution.py:43
  205.6 4.2 collective-permute-done.6.refs_0_.refs_6_.refs_7_.refs_8_.refs_9_
  210.7 11.6 %feed_forward.3 = (bf16[320,2048]{1,0:T(8,128)(2,1)}, bf16[320,2048]{1,0:T(8,128)(2,1)}, bf16[2,320,1024]{2,1,0:T(8,128)(2,1)}) custom-call(bf16[320,1024]{1,0:T(8,128)(2,1)} %copy-done.4, bf16[320,1024]{1,0:T(8,128)(2,1)} %bitcast.106, bf16[1024,1024]{1,0:T(8,128)(2,1)} %refs_2_.5, bf16[1024,1024]{1,0:T(8,128)(2,1)} %refs_3_.3, ...), custom_call_target="tpu_custom_call" | custom-call | flops 5368709120 | bytes 17825792 | tf_op jit(solution)/shard_map/feed_forward/pallas_call | solution.py:43
  222.2 9.2 %weight_grad.6 = (bf16[2,128,2048]{2,1,0:T(8,128)(2,1)}, bf16[2,128,2048]{2,1,0:T(8,128)(2,1)}, bf16[2,128,2048]{2,1,0:T(8,128)(2,1)}, bf16[2,128,2048]{2,1,0:T(8,128)(2,1)}) custom-call(s32[4]{0:T(128)} %add_subtract_fusion.1.refs_0_, bf16[320,1024]{1,0:T(8,128)(2,1)} %get-tuple-element.63.refs_0_.refs_1_.refs_2_.refs_3_.refs_4_, ...), custom_call_target="tpu_custom_call" | custom-call | flops 2684354560 | bytes 19922944 | tf_op jit(solution)/shard_map/weight_grad/pallas_call | solution.py:43
  239.9 10.4 %weight_grad.7.refs_13_ = bf16[4,2,128,2048]{3,2,1,0:T(8,128)(2,1)} custom-call(s32[4]{0:T(128)} %fusion.8.refs_0_, bf16[320,1024]{1,0:T(8,128)(2,1)} %get-tuple-element.63.refs_0_.refs_1_.refs_2_.refs_3_.refs_4_, bf16[320,1024]{1,0:T(8,128)(2,1)} %get-tuple-element.63.refs_0_.refs_1_.refs_2_.refs_3_.refs_4_, ...), custom_call_target="tpu_custom_call" | custom-call | flops 2684354560 | bytes 24117248 | tf_op jit(solution)/shard_map/weight_grad/pallas_call | solution.py:43
  250.3 4.9 all-to-all-start.4
  255.2 8.1 %collective-permute-done.7.refs_2_ = bf16[2,320,1024]{2,1,0:T(8,128)(2,1)S(1)} collective-permute-done((bf16[2,320,1024]{2,1,0:T(8,128)(2,1)S(1)}, bf16[2,320,1024]{2,1,0:T(8,128)(2,1)S(1)}, u32[]{:S(2)}, u32[]{:S(2)}) %collective-permute-start.7) | collective-permute-done | bytes 1310752 | tf_op jit(solution)/shard_map/ppermute | solution.py:862
  264.4 17.2 %cross_backward.1 = (bf16[320,1024]{1,0:T(8,128)(2,1)}, bf16[320,1024]{1,0:T(8,128)(2,1)}, f32[320,1024]{1,0:T(8,128)}, bf16[320,1024]{1,0:T(8,128)(2,1)}, bf16[...) custom-call(s32[5,7]{1,0:T(8,128)} %concatenate.12.refs_0_, ...), custom_call_target="tpu_custom_call" | custom-call | flops 2432696320 | bytes 28340224 | tf_op jit(solution)/shard_map/cross_backward/pallas_call | solution.py:43
  287.4 2.5 dynamic-slice_bitcast_fusion
  292.0 6.7 %collective-permute-done.13.refs_2_ = bf16[2,320,128]{2,1,0:T(8,128)(2,1)S(1)} collective-permute-done((bf16[2,320,128]{2,1,0:T(8,128)(2,1)S(1)}, bf16[2,320,128]{2,1,0:T(8,128)(2,1)S(1)}, u32[]{:S(2)}, u32[]{:S(2)}) %collective-permute-start.13) | collective-permute-done | bytes 163872 | tf_op jit(solution)/shard_map/ppermute | solution.py:685
  303.1 3.8 all-to-all-start.5
  307.0 3.0 fusion.refs_0_
  309.9 8.1 %all-to-all-done.5.refs_2_.refs_1_ = bf16[8,5,64,128]{3,2,1,0:T(8,128)(2,1)S(1)} async-done(((bf16[8,5,64,128]{3,2,1,0:T(8,128)(2,1)}), bf16[8,5,64,128]{3,2,1,0:T(8,128)(2,1)S(1)}, u32[]{:S(2)}, u32[]{:S(2)}) %all-to-all-start.5) | async-done | bytes 655392 | tf_op jit(solution)/shard_map/all_to_all | solution.py:927
  318.9 3.5 all-to-all-start.6
  322.4 13.3 %self_backward.1.refs_0_ = bf16[8,5,64,384]{3,2,1,0:T(8,128)(2,1)} custom-call(s32[5,2]{1,0:T(8,128)} %get-tuple-element.167.refs_0_, bf16[8,5,64,384]{3,2,1,0:T(8,128)(2,1)} %copy-done.7, bf16[8,5,64,128]{3,2,1,0:T(8,128)(2,1)} %copy-done.17), custom_call_target="tpu_custom_call" | custom-call | flops 1342177280 | bytes 4587520 | tf_op jit(solution)/shard_map/self_backward/pallas_call | solution.py:43
  335.7 2.5 all-to-all-done.6.refs_1_
  339.3 4.0 all-to-all-start.7
  345.4 3.7 ffn_sum.1
  350.1 5.3 text_grad.1.refs_26_
  355.4 6.8 %weight_grad.8 = (bf16[5,128,1024]{2,1,0:T(8,128)(2,1)}, bf16[5,128,1024]{2,1,0:T(8,128)(2,1)}, bf16[5,128,1024]{2,1,0:T(8,128)(2,1)}, bf16[5,128,1024]{2,1,0:T(8,128)(2,1)}) custom-call(s32[4]{0:T(128)} %add_subtract_fusion.refs_0_, bf16[320,1024]{1,0:T(8,128)(2,1)} %get-tuple-element.77.refs_1_.refs_2_.refs_3_.refs_4_, ...), custom_call_target="tpu_custom_call" | custom-call | flops 1174405120 | bytes 17039360 | tf_op jit(solution)/shard_map/weight_grad/pallas_call | solution.py:43
  371.3 8.0 %weight_grad.9 = (bf16[5,128,1024]{2,1,0:T(8,128)(2,1)}, bf16[5,128,1024]{2,1,0:T(8,128)(2,1)}, bf16[5,128,1024]{2,1,0:T(8,128)(2,1)}, bf16[5,128,1024]{2,1,0:T(8,128)(2,1)}) custom-call(s32[4]{0:T(128)} %fusion.9.refs_0_, bf16[320,1024]{1,0:T(8,128)(2,1)} %get-tuple-element.77.refs_1_.refs_2_.refs_3_.refs_4_, ...), custom_call_target="tpu_custom_call" | custom-call | flops 1174405120 | bytes 22282240 | tf_op jit(solution)/shard_map/weight_grad/pallas_call | solution.py:43
  379.3 10.4 %collective-permute-done.20.refs_3_ = bf16[2,128,1024]{2,1,0:T(8,128)(2,1)} collective-permute-done((bf16[2,128,1024]{2,1,0:T(8,128)(2,1)}, bf16[2,128,1024]{2,1,0:T(8,128)(2,1)}, u32[]{:S(2)}, u32[]{:S(2)}) %collective-permute-start.20) | collective-permute-done | bytes 524320 | tf_op jit(solution)/shard_map/ppermute | solution.py:963
  391.0 5.9 %qkv_grad.1 = (bf16[4,320,1024]{2,1,0:T(8,128)(2,1)}, bf16[1280,768]{1,0:T(8,128)(2,1)}) custom-call(bf16[4,2,320,384]{3,2,1,0:T(8,128)(2,1)} %bitcast.134, bf16[3,1024,256]{2,1,0:T(8,128)(2,1)} %refs_1_.1, bf16[5,128,1024]{2,1,0:T(8,128)(2,1)} %get-tuple-element.88.refs_2_, bf16[2,128,1024]{2,1,0:T(8,128)(2,1)} %collective-permute-done.20.refs_3_), custom_call_target="tpu_custom_call" | custom-call | flops 2013265920 | bytes 8126464 | tf_op jit(solution)/shard_map/qkv_grad/pallas_call | solution.py:43
  396.9 4.6 all-to-all-start.8
  405.1 4.8 weight_grad.10
  413.2 3.7 collective-permute-start.30
  416.8 16.6 %collective-permute-done.21.refs_10_.refs_4_ = bf16[5,128,1024]{2,1,0:T(8,128)(2,1)S(1)} collective-permute-done((bf16[5,128,1024]{2,1,0:T(8,128)(2,1)}, bf16[5,128,1024]{2,1,0:T(8,128)(2,1)S(1)}, u32[]{:S(2)}, u32[]{:S(2)}) %collective-permute-start.21) | collective-permute-done | bytes 1310752 | tf_op jit(solution)/shard_map/ppermute | solution.py:711
  435.3 4.8 weight_grad.11
  440.2 21.8 %collective-permute-done.22.refs_5_ = bf16[5,128,1024]{2,1,0:T(8,128)(2,1)S(1)} collective-permute-done((bf16[5,128,1024]{2,1,0:T(8,128)(2,1)}, bf16[5,128,1024]{2,1,0:T(8,128)(2,1)S(1)}, u32[]{:S(2)}, u32[]{:S(2)}) %collective-permute-start.22) | collective-permute-done | bytes 1310752 | tf_op jit(solution)/shard_map/ppermute | solution.py:711
  462.0 7.4 %all-to-all-done.8.refs_0_ = bf16[4,320,1024]{2,1,0:T(8,128)(2,1)} async-done(((bf16[4,320,1024]{2,1,0:T(8,128)(2,1)}), bf16[4,320,1024]{2,1,0:T(8,128)(2,1)}, u32[]{:S(2)}, u32[]{:S(2)}) %all-to-all-start.8) | async-done | bytes 2621472 | tf_op jit(solution)/shard_map/all_to_all | solution.py:1001
  469.4 5.0 to_frames.1.refs_1_
  479.6 3.8 all-to-all-start.9
  483.4 4.8 convert.8
  488.3 2.2 convert_add_fusion.2
  490.5 5.0 first_norm.1
  501.7 5.3 add_convert_fusion
  507.0 2.4 copy.79
  524.2 2.4 collective-permute-start.41
  528.5 2.9 collective-permute-start.36
  533.8 7.0 %text_out.1 = f32[4,640,1024]{2,1,0:T(8,128)} custom-call(bf16[8,4,80,1024]{3,2,1,0:T(8,128)(2,1)} %bitcast.129), custom_call_target="tpu_custom_call" | custom-call | bytes 15728640 | tf_op jit(solution)/shard_map/text_out/pallas_call | solution.py:43
  540.8 9.9 %all-to-all-done.9.refs_0_ = bf16[4,320,1024]{2,1,0:T(8,128)(2,1)S(1)} async-done(((bf16[4,320,1024]{2,1,0:T(8,128)(2,1)}), bf16[4,320,1024]{2,1,0:T(8,128)(2,1)S(1)}, u32[]{:S(2)}, u32[]{:S(2)}) %all-to-all-start.9) | async-done | bytes 2621472 | tf_op jit(solution)/shard_map/all_to_all | solution.py:1051
  552.3 4.8 convert.6.refs_1_
  557.1 2.3 collective-permute-start.42
  561.4 5.3 collective-permute-done.42.refs_0_
  (291 shorter events, 118.1 us)
Async XLA Ops:
  7.2 150.9 %copy-start = (s32[20,2]{0,1:T(2,128)S(1)}, s32[20,2]{0,1:T(2,128)}, u32[]{:S(2)}) copy-start(s32[20,2]{0,1:T(2,128)} %param.17) | copy-start | bytes 484
  7.2 40.2 %all-gather.11.cloned.1.call-start = ((), (), s32[]{:S(2)}) async-start(), calls=%async_computation.12 | async-start | bytes 1638400 | tf_op jit(solution)/shard_map/all_gather | solution.py:748
  20.8 30.4 %all-to-all-start = ((bf16[8,5,64,384]{3,2,1,0:T(8,128)(2,1)}), bf16[8,5,64,384]{3,2,1,0:T(8,128)(2,1)S(1)}, u32[]{:S(2)}, u32[]{:S(2)}) async-start(bf16[8,5,64,384]{3,2,1,0:T(8,128)(2,1)} %bitcast.135), calls=%async_computation | async-start | bytes 3932160 | tf_op jit(solution)/shard_map/all_to_all | solution.py:743
  53.2 27.9 %all-to-all-start.1 = ((bf16[4,4,128,512]{3,2,1,0:T(8,128)(2,1)}), bf16[4,4,128,512]{3,2,1,0:T(8,128)(2,1)S(1)}, u32[]{:S(2)}, u32[]{:S(2)}) async-start(bf16[4,4,128,512]{3,2,1,0:T(8,128)(2,1)} %tied.21), calls=%async_computation.1 | async-start | bytes 4194304 | tf_op jit(solution)/shard_map/all_to_all | solution.py:689
  82.4 19.9 %copy-start.26 = (bf16[512,1280]{1,0:T(8,128)(2,1)S(1)}, bf16[512,1280]{1,0:T(8,128)(2,1)}, u32[]{:S(2)}) copy-start(bf16[512,1280]{1,0:T(8,128)(2,1)} %all-gather.11.cloned.1.call-done) | copy-start | bytes 3932164
  82.4 14.8 %all-to-all-start.2 = ((bf16[8,5,64,128]{3,2,1,0:T(8,128)(2,1)}), bf16[8,5,64,128]{3,2,1,0:T(8,128)(2,1)S(1)}, u32[]{:S(2)}, u32[]{:S(2)}) async-start(bf16[8,5,64,128]{3,2,1,0:T(8,128)(2,1)} %tied.22), calls=%async_computation.2 | async-start | bytes 1310720 | tf_op jit(solution)/shard_map/all_to_all | solution.py:760
  97.8 8.6 %collective-permute-start.2 = (bf16[2,320,128]{2,1,0:T(8,128)(2,1)S(1)}, bf16[2,320,128]{2,1,0:T(8,128)(2,1)S(1)}, u32[]{:S(2)}, u32[]{:S(2)}) collective-permute-start(bf16[2,320,128]{2,1,0:T(8,128)(2,1)S(1)} %get-tuple-element.157), channel_id=1, source_target_pairs={{0,3},{1,2},{2,1},{3,0},{4,7},{5,6},{6,5},{7,4},{8,11},{9,10},{10,... | collective-permute-start | bytes 491528 | tf_op jit(solution)/shard_map/ppermute | solution.py:685
  101.4 11.0 %collective-permute-start.1 = (bf16[2,320,128]{2,1,0:T(8,128)(2,1)S(1)}, bf16[2,320,128]{2,1,0:T(8,128)(2,1)S(1)}, u32[]{:S(2)}, u32[]{:S(2)}) collective-permute-start(bf16[2,320,128]{2,1,0:T(8,128)(2,1)S(1)} %get-tuple-element.158), channel_id=1, source_target_pairs={{0,2},{1,3},{2,0},{3,1},{4,6},{5,7},{6,4},{7,5},{8,10},{9,11},{10,... | collective-permute-start | bytes 491528 | tf_op jit(solution)/shard_map/ppermute | solution.py:685
  101.4 11.0 %collective-permute-start = (bf16[2,320,128]{2,1,0:T(8,128)(2,1)S(1)}, bf16[2,320,128]{2,1,0:T(8,128)(2,1)S(1)}, u32[]{:S(2)}, u32[]{:S(2)}) collective-permute-start(bf16[2,320,128]{2,1,0:T(8,128)(2,1)S(1)} %get-tuple-element.159), channel_id=1, source_target_pairs={{0,1},{1,0},{2,3},{3,2},{4,5},{5,4},{6,7},{7,6},{8,9},{9,8},{10,11... | collective-permute-start | bytes 491528 | tf_op jit(solution)/shard_map/ppermute | solution.py:685
  114.5 41.4 %all-to-all-start.3 = ((bf16[4,4,128,768]{3,2,1,0:T(8,128)(2,1)}), bf16[4,4,128,768]{3,2,1,0:T(8,128)(2,1)S(1)}, u32[]{:S(2)}, u32[]{:S(2)}) async-start(bf16[4,4,128,768]{3,2,1,0:T(8,128)(2,1)} %tied.23), calls=%async_computation.3 | async-start | bytes 6291456 | tf_op jit(solution)/shard_map/all_to_all | solution.py:689
  119.4 74.1 %all-gather.7.cloned.1.call-start = ((), (), s32[]{:S(2)}) async-start(), calls=%async_computation.10 | async-start | bytes 4718592 | tf_op jit(solution)/shard_map/all_gather | solution.py:776
  124.0 25.1 %collective-permute-start.5 = (bf16[128,2048]{1,0:T(8,128)(2,1)}, bf16[128,2048]{1,0:T(8,128)(2,1)}, u32[]{:S(2)}, u32[]{:S(2)}) collective-permute-start(bf16[128,2048]{1,0:T(8,128)(2,1)} %tied.24), channel_id=1, source_target_pairs={{0,2},{1,3},{2,0},{3,1},{4,6},{5,7},{6,4},{7,5},{8,10},{9,11},{10,... | collective-permute-start | bytes 1572872 | tf_op jit(solution)/shard_map/ppermute | solution.py:774
  157.5 16.4 %collective-permute-start.3 = (bf16[4,4,128,768]{3,2,1,0:T(8,128)(2,1)}, bf16[4,4,128,768]{3,2,1,0:T(8,128)(2,1)S(1)}, u32[]{:S(2)}, u32[]{:S(2)}) collective-permute-start(bf16[4,4,128,768]{3,2,1,0:T(8,128)(2,1)} %copy-done.2), channel_id=1, source_target_pairs={{0,4},{4,0},{8,12},{12,8},{16,20},{20,16},{24,28},{28,24},{1,5},{5... | collective-permute-start | bytes 9437192 | tf_op jit(solution)/shard_map/ppermute | solution.py:692
  157.6 8.6 %collective-permute-start.4 = (bf16[4,4,128,512]{3,2,1,0:T(8,128)(2,1)}, bf16[4,4,128,512]{3,2,1,0:T(8,128)(2,1)}, u32[]{:S(2)}, u32[]{:S(2)}) collective-permute-start(bf16[4,4,128,512]{3,2,1,0:T(8,128)(2,1)} %copy-done.6), channel_id=1, source_target_pairs={{0,4},{4,0},{8,12},{12,8},{16,20},{20,16},{24,28},{28,24},{1,5},{5... | collective-permute-start | bytes 6291464 | tf_op jit(solution)/shard_map/ppermute | solution.py:692
  192.5 17.3 %collective-permute-start.6 = (bf16[320,1024]{1,0:T(8,128)(2,1)}, bf16[320,1024]{1,0:T(8,128)(2,1)S(1)}, u32[]{:S(2)}, u32[]{:S(2)}) collective-permute-start(bf16[320,1024]{1,0:T(8,128)(2,1)} %get-tuple-element.63.refs_0_.refs_1_.refs_2_.refs_3_.refs_4_), channel_id=1, source_target_pairs={{0,1},{1,0},{2,3},{3,2},{4,5},{5,4},{6,7},{7,6},{8,9},{9,8},{10,11... | collective-permute-start | bytes 1966088 | tf_op jit(solution)/shard_map/ppermute | solution.py:856
  222.2 10.3 %copy-start.57 = (bf16[2,320,1024]{2,1,0:T(8,128)(2,1)S(1)}, bf16[2,320,1024]{2,1,0:T(8,128)(2,1)}, u32[]{:S(2)}) copy-start(bf16[2,320,1024]{2,1,0:T(8,128)(2,1)} %get-tuple-element.65) | copy-start | bytes 3932164
  231.5 2.9 collective-permute-start.8
  231.5 4.4 collective-permute-start.9
  232.0 5.4 collective-permute-start.10
  232.1 6.8 %collective-permute-start.11 = (bf16[2,128,2048]{2,1,0:T(8,128)(2,1)}, bf16[2,128,2048]{2,1,0:T(8,128)(2,1)S(1)}, u32[]{:S(2)}, u32[]{:S(2)}) collective-permute-start(bf16[2,128,2048]{2,1,0:T(8,128)(2,1)} %get-tuple-element.74), channel_id=1, source_target_pairs={{0,4},{4,0},{8,12},{12,8},{16,20},{20,16},{24,28},{28,24},{1,5},{5... | collective-permute-start | bytes 3145736 | tf_op jit(solution)/shard_map/ppermute | solution.py:692
  232.5 30.8 %collective-permute-start.7 = (bf16[2,320,1024]{2,1,0:T(8,128)(2,1)S(1)}, bf16[2,320,1024]{2,1,0:T(8,128)(2,1)S(1)}, u32[]{:S(2)}, u32[]{:S(2)}) collective-permute-start(bf16[2,320,1024]{2,1,0:T(8,128)(2,1)S(1)} %copy-done.57), channel_id=1, source_target_pairs={{0,1},{1,0},{2,3},{3,2},{4,5},{5,4},{6,7},{7,6},{8,9},{9,8},{10,11... | collective-permute-start | bytes 3932168 | tf_op jit(solution)/shard_map/ppermute | solution.py:862
  250.3 52.9 %all-to-all-start.4 = ((bf16[4,2,128,2048]{3,2,1,0:T(8,128)(2,1)}), bf16[4,2,128,2048]{3,2,1,0:T(8,128)(2,1)}, u32[]{:S(2)}, u32[]{:S(2)}) async-start(bf16[4,2,128,2048]{3,2,1,0:T(8,128)(2,1)} %weight_grad.7.refs_13_), calls=%async_computation.4 | async-start | bytes 8388608 | tf_op jit(solution)/shard_map/all_to_all | solution.py:689
  255.1 108.1 %all-gather.9.cloned.1.call-start = ((), (), s32[]{:S(2)}) async-start(), calls=%async_computation.11 | async-start | bytes 3276800 | tf_op jit(solution)/shard_map/all_gather | solution.py:919
  282.9 9.1 %collective-permute-start.14 = (bf16[2,320,128]{2,1,0:T(8,128)(2,1)S(1)}, bf16[2,320,128]{2,1,0:T(8,128)(2,1)S(1)}, u32[]{:S(2)}, u32[]{:S(2)}) collective-permute-start(bf16[2,320,128]{2,1,0:T(8,128)(2,1)S(1)} %get-tuple-element.154), channel_id=1, source_target_pairs={{0,3},{1,2},{2,1},{3,0},{4,7},{5,6},{6,5},{7,4},{8,11},{9,10},{10,... | collective-permute-start | bytes 491528 | tf_op jit(solution)/shard_map/ppermute | solution.py:685
  285.1 13.6 %collective-permute-start.13 = (bf16[2,320,128]{2,1,0:T(8,128)(2,1)S(1)}, bf16[2,320,128]{2,1,0:T(8,128)(2,1)S(1)}, u32[]{:S(2)}, u32[]{:S(2)}) collective-permute-start(bf16[2,320,128]{2,1,0:T(8,128)(2,1)S(1)} %get-tuple-element.155), channel_id=1, source_target_pairs={{0,2},{1,3},{2,0},{3,1},{4,6},{5,7},{6,4},{7,5},{8,10},{9,11},{10,... | collective-permute-start | bytes 491528 | tf_op jit(solution)/shard_map/ppermute | solution.py:685
  285.1 13.6 %collective-permute-start.12 = (bf16[2,320,128]{2,1,0:T(8,128)(2,1)S(1)}, bf16[2,320,128]{2,1,0:T(8,128)(2,1)S(1)}, u32[]{:S(2)}, u32[]{:S(2)}) collective-permute-start(bf16[2,320,128]{2,1,0:T(8,128)(2,1)S(1)} %get-tuple-element.156), channel_id=1, source_target_pairs={{0,1},{1,0},{2,3},{3,2},{4,5},{5,4},{6,7},{7,6},{8,9},{9,8},{10,11... | collective-permute-start | bytes 491528 | tf_op jit(solution)/shard_map/ppermute | solution.py:685
  289.9 17.1 %collective-permute-start.15 = (bf16[4,80,2048]{2,1,0:T(8,128)(2,1)}, bf16[4,80,2048]{2,1,0:T(8,128)(2,1)}, u32[]{:S(2)}, u32[]{:S(2)}) collective-permute-start(bf16[4,80,2048]{2,1,0:T(8,128)(2,1)} %dynamic-slice_bitcast_fusion), channel_id=1, source_target_pairs={{0,4},{4,0},{8,12},{12,8},{16,20},{20,16},{24,28},{28,24},{1,5},{5... | collective-permute-start | bytes 3932168 | tf_op jit(solution)/shard_map/ppermute | solution.py:692
  303.1 14.9 %all-to-all-start.5 = ((bf16[8,5,64,128]{3,2,1,0:T(8,128)(2,1)}), bf16[8,5,64,128]{3,2,1,0:T(8,128)(2,1)S(1)}, u32[]{:S(2)}, u32[]{:S(2)}) async-start(bf16[8,5,64,128]{3,2,1,0:T(8,128)(2,1)} %tied.27), calls=%async_computation.5 | async-start | bytes 1310720 | tf_op jit(solution)/shard_map/all_to_all | solution.py:927
  318.9 19.4 %all-to-all-start.6 = ((bf16[4,80,2048]{2,1,0:T(8,128)(2,1)}), bf16[4,80,2048]{2,1,0:T(8,128)(2,1)S(1)}, u32[]{:S(2)}, u32[]{:S(2)}) async-start(bf16[4,80,2048]{2,1,0:T(8,128)(2,1)} %tied.28), calls=%async_computation.6 | async-start | bytes 2621440 | tf_op jit(solution)/shard_map/all_to_all | solution.py:689
  339.3 50.4 %all-to-all-start.7 = ((bf16[8,5,64,384]{3,2,1,0:T(8,128)(2,1)}), bf16[8,5,64,384]{3,2,1,0:T(8,128)(2,1)S(1)}, u32[]{:S(2)}, u32[]{:S(2)}) async-start(bf16[8,5,64,384]{3,2,1,0:T(8,128)(2,1)} %tied.29.refs_4_), calls=%async_computation.7 | async-start | bytes 3932160 | tf_op jit(solution)/shard_map/all_to_all | solution.py:947
  362.2 4.5 collective-permute-start.16
  362.7 4.9 collective-permute-start.17
  362.8 6.7 %collective-permute-start.18 = (bf16[5,128,1024]{2,1,0:T(8,128)(2,1)}, bf16[5,128,1024]{2,1,0:T(8,128)(2,1)}, u32[]{:S(2)}, u32[]{:S(2)}) collective-permute-start(bf16[5,128,1024]{2,1,0:T(8,128)(2,1)} %get-tuple-element.86), channel_id=1, source_target_pairs={{0,4},{4,0},{8,12},{12,8},{16,20},{20,16},{24,28},{28,24},{1,5},{5... | collective-permute-start | bytes 3932168 | tf_op jit(solution)/shard_map/ppermute | solution.py:692
  363.2 8.1 %collective-permute-start.19 = (bf16[5,128,1024]{2,1,0:T(8,128)(2,1)}, bf16[5,128,1024]{2,1,0:T(8,128)(2,1)}, u32[]{:S(2)}, u32[]{:S(2)}) collective-permute-start(bf16[5,128,1024]{2,1,0:T(8,128)(2,1)} %get-tuple-element.87), channel_id=1, source_target_pairs={{0,4},{4,0},{8,12},{12,8},{16,20},{20,16},{24,28},{28,24},{1,5},{5... | collective-permute-start | bytes 3932168 | tf_op jit(solution)/shard_map/ppermute | solution.py:692
  363.3 26.4 %collective-permute-start.20 = (bf16[2,128,1024]{2,1,0:T(8,128)(2,1)}, bf16[2,128,1024]{2,1,0:T(8,128)(2,1)}, u32[]{:S(2)}, u32[]{:S(2)}) collective-permute-start(bf16[2,128,1024]{2,1,0:T(8,128)(2,1)} %tied.30), channel_id=1, source_target_pairs={{0,2},{1,3},{2,0},{3,1},{4,6},{5,7},{6,4},{7,5},{8,10},{9,11},{10,... | collective-permute-start | bytes 1572872 | tf_op jit(solution)/shard_map/ppermute | solution.py:963
  396.9 72.5 %all-to-all-start.8 = ((bf16[4,320,1024]{2,1,0:T(8,128)(2,1)}), bf16[4,320,1024]{2,1,0:T(8,128)(2,1)}, u32[]{:S(2)}, u32[]{:S(2)}) async-start(bf16[4,320,1024]{2,1,0:T(8,128)(2,1)} %get-tuple-element.90.refs_6_.refs_0_), calls=%async_computation.8 | async-start | bytes 5242880 | tf_op jit(solution)/shard_map/all_to_all | solution.py:1001
  401.4 132.3 %all-gather.13.cloned.1.call-start = ((), (), s32[]{:S(2)}) async-start(), calls=%async_computation.13 | async-start | bytes 5898240 | tf_op jit(solution)/shard_map/all_gather | solution.py:1033
  401.5 31.9 %collective-permute-start.21 = (bf16[5,128,1024]{2,1,0:T(8,128)(2,1)}, bf16[5,128,1024]{2,1,0:T(8,128)(2,1)S(1)}, u32[]{:S(2)}, u32[]{:S(2)}) collective-permute-start(bf16[5,128,1024]{2,1,0:T(8,128)(2,1)} %get-tuple-element.92), channel_id=1, source_target_pairs={{0,8},{4,12},{8,0},{12,4},{16,24},{20,28},{24,16},{28,20},{1,9},{5... | collective-permute-start | bytes 3932168 | tf_op jit(solution)/shard_map/ppermute | solution.py:711
  403.2 58.7 %collective-permute-start.22 = (bf16[5,128,1024]{2,1,0:T(8,128)(2,1)}, bf16[5,128,1024]{2,1,0:T(8,128)(2,1)S(1)}, u32[]{:S(2)}, u32[]{:S(2)}) collective-permute-start(bf16[5,128,1024]{2,1,0:T(8,128)(2,1)} %get-tuple-element.93), channel_id=1, source_target_pairs={{0,16},{4,20},{8,24},{12,28},{16,0},{20,4},{24,8},{28,12},{1,17},{... | collective-permute-start | bytes 3932168 | tf_op jit(solution)/shard_map/ppermute | solution.py:711
  404.7 57.3 %collective-permute-start.23 = (bf16[5,128,1024]{2,1,0:T(8,128)(2,1)}, bf16[5,128,1024]{2,1,0:T(8,128)(2,1)}, u32[]{:S(2)}, u32[]{:S(2)}) collective-permute-start(bf16[5,128,1024]{2,1,0:T(8,128)(2,1)} %get-tuple-element.94), channel_id=1, source_target_pairs={{0,24},{4,28},{8,16},{12,20},{16,8},{20,12},{24,0},{28,4},{1,25},{... | collective-permute-start | bytes 3932168 | tf_op jit(solution)/shard_map/ppermute | solution.py:711
  409.9 1.7 collective-permute-start.24
  409.9 1.9 collective-permute-start.25
  411.5 23.8 %copy-start.45 = (bf16[1,128,768]{2,1,0:T(8,128)(2,1)}, bf16[1,128,768]{2,1,0:T(8,128)(2,1)S(1)}, u32[]{:S(2)}) copy-start(bf16[1,128,768]{2,1,0:T(8,128)(2,1)S(1)} %collective-permute-done.24.refs_6_) | copy-start | bytes 589828
  411.5 1.7 collective-permute-start.26
  411.8 23.5 %copy-start.46 = (bf16[1,128,768]{2,1,0:T(8,128)(2,1)}, bf16[1,128,768]{2,1,0:T(8,128)(2,1)S(1)}, u32[]{:S(2)}) copy-start(bf16[1,128,768]{2,1,0:T(8,128)(2,1)S(1)} %collective-permute-done.25.refs_7_) | copy-start | bytes 589828
  411.8 5.0 collective-permute-start.27
  413.2 22.2 %copy-start.47 = (bf16[1,128,768]{2,1,0:T(8,128)(2,1)}, bf16[1,128,768]{2,1,0:T(8,128)(2,1)S(1)}, u32[]{:S(2)}) copy-start(bf16[1,128,768]{2,1,0:T(8,128)(2,1)S(1)} %collective-permute-done.26.refs_8_) | copy-start | bytes 589828
  413.2 61.2 %collective-permute-start.30 = (bf16[80,1024]{1,0:T(8,128)(2,1)S(1)}, bf16[80,1024]{1,0:T(8,128)(2,1)S(1)}, u32[]{:S(2)}, u32[]{:S(2)}) collective-permute-start(bf16[80,1024]{1,0:T(8,128)(2,1)S(1)} %copy-done.19), channel_id=1, source_target_pairs={{0,3},{1,2},{2,1},{3,0},{4,7},{5,6},{6,5},{7,4},{8,11},{9,10},{10,... | collective-permute-start | bytes 491528 | tf_op jit(solution)/shard_map/ppermute | solution.py:685
  416.8 18.5 %copy-start.48 = (bf16[1,128,768]{2,1,0:T(8,128)(2,1)}, bf16[1,128,768]{2,1,0:T(8,128)(2,1)S(1)}, u32[]{:S(2)}) copy-start(bf16[1,128,768]{2,1,0:T(8,128)(2,1)S(1)} %collective-permute-done.27.refs_9_) | copy-start | bytes 589828
  416.8 58.6 %collective-permute-start.29 = (bf16[80,1024]{1,0:T(8,128)(2,1)S(1)}, bf16[80,1024]{1,0:T(8,128)(2,1)S(1)}, u32[]{:S(2)}, u32[]{:S(2)}) collective-permute-start(bf16[80,1024]{1,0:T(8,128)(2,1)S(1)} %copy-done.19), channel_id=1, source_target_pairs={{0,2},{1,3},{2,0},{3,1},{4,6},{5,7},{6,4},{7,5},{8,10},{9,11},{10,... | collective-permute-start | bytes 491528 | tf_op jit(solution)/shard_map/ppermute | solution.py:685
  433.4 42.7 %collective-permute-start.28 = (bf16[80,1024]{1,0:T(8,128)(2,1)S(1)}, bf16[80,1024]{1,0:T(8,128)(2,1)S(1)}, u32[]{:S(2)}, u32[]{:S(2)}) collective-permute-start(bf16[80,1024]{1,0:T(8,128)(2,1)S(1)} %copy-done.19), channel_id=1, source_target_pairs={{0,1},{1,0},{2,3},{3,2},{4,5},{5,4},{6,7},{7,6},{8,9},{9,8},{10,11... | collective-permute-start | bytes 491528 | tf_op jit(solution)/shard_map/ppermute | solution.py:685
  479.6 71.2 %all-to-all-start.9 = ((bf16[4,320,1024]{2,1,0:T(8,128)(2,1)}), bf16[4,320,1024]{2,1,0:T(8,128)(2,1)S(1)}, u32[]{:S(2)}, u32[]{:S(2)}) async-start(bf16[4,320,1024]{2,1,0:T(8,128)(2,1)} %to_frames.1.refs_1_), calls=%async_computation.9 | async-start | bytes 5242880 | tf_op jit(solution)/shard_map/all_to_all | solution.py:1051
  496.9 3.1 collective-permute-start.31
  500.0 12.9 %collective-permute-start.32 = (f32[6,1024]{1,0:T(8,128)S(1)}, f32[6,1024]{1,0:T(8,128)S(1)}, u32[]{:S(2)}, u32[]{:S(2)}) collective-permute-start(f32[6,1024]{1,0:T(8,128)S(1)} %add.164), channel_id=1, source_target_pairs={{0,8},{4,12},{8,0},{12,4},{16,24},{20,28},{24,16},{28,20},{1,9},{5... | collective-permute-start | bytes 73736 | tf_op jit(solution)/shard_map/ppermute | solution.py:1056
  509.4 17.2 %collective-permute-start.37 = (bf16[1,128,768]{2,1,0:T(8,128)(2,1)}, bf16[1,128,768]{2,1,0:T(8,128)(2,1)S(1)}, u32[]{:S(2)}, u32[]{:S(2)}) collective-permute-start(bf16[1,128,768]{2,1,0:T(8,128)(2,1)} %get-tuple-element.103), channel_id=1, source_target_pairs={{0,8},{4,12},{8,0},{12,4},{16,24},{20,28},{24,16},{28,20},{1,9},{5... | collective-permute-start | bytes 589832 | tf_op jit(solution)/shard_map/ppermute | solution.py:711
  509.8 17.4 %collective-permute-start.38 = (bf16[1,128,768]{2,1,0:T(8,128)(2,1)}, bf16[1,128,768]{2,1,0:T(8,128)(2,1)}, u32[]{:S(2)}, u32[]{:S(2)}) collective-permute-start(bf16[1,128,768]{2,1,0:T(8,128)(2,1)} %get-tuple-element.104), channel_id=1, source_target_pairs={{0,16},{4,20},{8,24},{12,28},{16,0},{20,4},{24,8},{28,12},{1,17},{... | collective-permute-start | bytes 589832 | tf_op jit(solution)/shard_map/ppermute | solution.py:711
  511.6 16.9 %collective-permute-start.39 = (bf16[1,128,768]{2,1,0:T(8,128)(2,1)}, bf16[1,128,768]{2,1,0:T(8,128)(2,1)}, u32[]{:S(2)}, u32[]{:S(2)}) collective-permute-start(bf16[1,128,768]{2,1,0:T(8,128)(2,1)} %get-tuple-element.105), channel_id=1, source_target_pairs={{0,24},{4,28},{8,16},{12,20},{16,8},{20,12},{24,0},{28,4},{1,25},{... | collective-permute-start | bytes 589832 | tf_op jit(solution)/shard_map/ppermute | solution.py:711
  512.9 11.3 %collective-permute-start.33 = (f32[6,1024]{1,0:T(8,128)S(1)}, f32[6,1024]{1,0:T(8,128)S(1)}, u32[]{:S(2)}, u32[]{:S(2)}) collective-permute-start(f32[6,1024]{1,0:T(8,128)S(1)} %add.165), channel_id=1, source_target_pairs={{0,16},{4,20},{8,24},{12,28},{16,0},{20,4},{24,8},{28,12},{1,17},{... | collective-permute-start | bytes 73736 | tf_op jit(solution)/shard_map/ppermute | solution.py:1056
  522.6 44.8 %collective-permute-start.40 = (bf16[5,128,256]{2,1,0:T(8,128)(2,1)}, bf16[5,128,256]{2,1,0:T(8,128)(2,1)}, u32[]{:S(2)}, u32[]{:S(2)}) collective-permute-start(bf16[5,128,256]{2,1,0:T(8,128)(2,1)} %bitcast.46), channel_id=1, source_target_pairs={{0,1},{1,0},{2,3},{3,2},{4,5},{5,4},{6,7},{7,6},{8,9},{9,8},{10,11... | collective-permute-start | bytes 983048 | tf_op jit(solution)/shard_map/ppermute | solution.py:685
  524.2 43.2 %collective-permute-start.41 = (bf16[5,128,256]{2,1,0:T(8,128)(2,1)}, bf16[5,128,256]{2,1,0:T(8,128)(2,1)}, u32[]{:S(2)}, u32[]{:S(2)}) collective-permute-start(bf16[5,128,256]{2,1,0:T(8,128)(2,1)} %bitcast.147), channel_id=1, source_target_pairs={{0,2},{1,3},{2,0},{3,1},{4,6},{5,7},{6,4},{7,5},{8,10},{9,11},{10,... | collective-permute-start | bytes 983048 | tf_op jit(solution)/shard_map/ppermute | solution.py:685
  526.6 32.8 %collective-permute-start.35 = (f32[6,128]{1,0:T(8,128)S(1)}, f32[6,128]{1,0:T(8,128)S(1)}, u32[]{:S(2)}, u32[]{:S(2)}) collective-permute-start(f32[6,128]{1,0:T(8,128)S(1)} %fusion.6), channel_id=1, source_target_pairs={{0,2},{1,3},{2,0},{3,1},{4,6},{5,7},{6,4},{7,5},{8,10},{9,11},{10,... | collective-permute-start | bytes 9224 | tf_op jit(solution)/shard_map/ppermute | solution.py:685
  527.2 32.8 %collective-permute-start.34 = (f32[6,128]{1,0:T(8,128)S(1)}, f32[6,128]{1,0:T(8,128)S(1)}, u32[]{:S(2)}, u32[]{:S(2)}) collective-permute-start(f32[6,128]{1,0:T(8,128)S(1)} %fusion.6), channel_id=1, source_target_pairs={{0,1},{1,0},{2,3},{3,2},{4,5},{5,4},{6,7},{7,6},{8,9},{9,8},{10,11... | collective-permute-start | bytes 9224 | tf_op jit(solution)/shard_map/ppermute | solution.py:685
  528.5 28.6 %collective-permute-start.36 = (f32[6,128]{1,0:T(8,128)S(1)}, f32[6,128]{1,0:T(8,128)S(1)}, u32[]{:S(2)}, u32[]{:S(2)}) collective-permute-start(f32[6,128]{1,0:T(8,128)S(1)} %fusion.6), channel_id=1, source_target_pairs={{0,3},{1,2},{2,1},{3,0},{4,7},{5,6},{6,5},{7,4},{8,11},{9,10},{10,... | collective-permute-start | bytes 9224 | tf_op jit(solution)/shard_map/ppermute | solution.py:685
  557.1 9.6 %collective-permute-start.42 = (bf16[5,128,256]{2,1,0:T(8,128)(2,1)S(1)}, bf16[5,128,256]{2,1,0:T(8,128)(2,1)S(1)}, u32[]{:S(2)}, u32[]{:S(2)}) collective-permute-start(bf16[5,128,256]{2,1,0:T(8,128)(2,1)S(1)} %bitcast.148), channel_id=1, source_target_pairs={{0,3},{1,2},{2,1},{3,0},{4,7},{5,6},{6,5},{7,4},{8,11},{9,10},{10,... | collective-permute-start | bytes 983048 | tf_op jit(solution)/shard_map/ppermute | solution.py:685
  (51 other events, 140.1 us)
Sparse Core Ops, SparseCore 0:
  11.8 35.4 all-gather.10
  157.6 35.8 all-gather.6
  300.2 53.5 all-gather.8
  479.7 46.0 all-gather.12

commit v5 on v4

--- a/solution.py
+++ b/solution.py
@@ -466,18 +466,26 @@
 
         @pl.when(step // tiles == g)
         def _(g=g):
-            w_up, w_down = refs[2 * g][...], refs[2 * g + 1][...]
             into, out_of = (NN, NT) if g else (NT, NN)
-            up = dot(h_ref[...], w_up, NN)
-            d_act = dot(ct_ref[...], w_down, into)
-            cdf = 0.5 * (1.0 + lax.erf(up * (0.5**0.5)))
-            slope = cdf + up * jnp.exp(-0.5 * up * up) * 0.3989422804014327
-            act = (up * cdf).astype(BF)
-            d_up = (d_act * slope).astype(BF)
-            act_ref[...] = act
-            dup_ref[...] = d_up
-            dh_acc[...] += dot(d_up, w_up, NT)
-            out_acc[...] += dot(act, w_down, out_of)
+            size = refs[2 * g].shape[1] // 2
+            parts = [slice(k * size, (k + 1) * size) for k in range(2)]
+            w_up = [refs[2 * g][:, p] for p in parts]
+            w_down = [refs[2 * g + 1][:, p] if g else refs[2 * g + 1][p, :] for p in parts]
+            ups = [dot(h_ref[...], w, NN) for w in w_up]
+            d_acts = [dot(ct_ref[...], w, into) for w in w_down]
+            d_h, out = 0.0, 0.0
+            for k, p in enumerate(parts):
+                up = ups[k]
+                cdf = 0.5 * (1.0 + lax.erf(up * (0.5**0.5)))
+                slope = cdf + up * jnp.exp(-0.5 * up * up) * 0.3989422804014327
+                act = (up * cdf).astype(BF)
+                d_up = (d_acts[k] * slope).astype(BF)
+                act_ref[:, p] = act
+                dup_ref[:, p] = d_up
+                d_h += dot(d_up, w_up[k], NT)
+                out += dot(act, w_down[k], out_of)
+            dh_acc[...] += d_h
+            out_acc[...] += out
 
     @pl.when(step == groups * tiles - 1)
     def _():
@@ -527,11 +535,12 @@
     outs = refs[-chips:] if apart else [refs[-1].at[j] for j in range(chips)]
     at = 0
     for p, terms in enumerate(sums):
-        total = 0.0
+        lefts, rights = [], []
         for _ in range(terms):
-            left = jnp.concatenate([r[...] for r in refs[at : at + chips]], axis=1)
-            total += dot(left, refs[at + chips][...], TN)
+            lefts.append(jnp.concatenate([r[...] for r in refs[at : at + chips]], axis=1))
+            rights.append(refs[at + chips][...])
             at += chips + 1
+        total = dot(jnp.concatenate(lefts, axis=0), jnp.concatenate(rights, axis=0), TN)
         share = total.shape[0] // chips
         for j in range(chips):
             block = total[j * share : (j + 1) * share]

time: 591 us -> 590 us (level)
  transfers between devices with their start and end apart: 57 -> 57, of which waited for: 35 -> 34; matrix products, arithmetic and copies ran while one was open for 12% -> 12% of each run, Pallas kernels for 24% -> 24%
where the time goes in v5:
time: 590 us; the launch traced here: 579 us
  waiting for transfers between devices  212 us (36%)
  Pallas kernels  167 us (28%)
  starting transfers between devices  82.7 us (14%)
  local copies, waits for them, and re-layouts  66.8 us (11%)
  other arithmetic  36.1 us (6%)
  between operations  14.6 us (2%)
    pallas_call x21, Pallas kernels, call(): pl.pallas_call(body, out_shape=[o for o, _ in outs], grid_spec=pltpu.Pref...  167 us
    ppermute x6, waiting for transfers between devices, from_chips(): lax.ppermute(blocks[j], 'blk', swapped(blk, 2 * j))  38.4 us
    unnamed x130, local copies, waits for them, and re-layouts  29.3 us
    ppermute x15, starting transfers between devices, from_ranks(): lax.ppermute(values[j], 'tp', swapped(tp, j))  25.4 us
    ppermute x1, waiting for transfers between devices, shards(): lax.ppermute(piece, 'tp', swapped(tp, 2 * j))  25.1 us
    ppermute x15, waiting for transfers between devices, from_ranks(): lax.ppermute(values[j], 'tp', swapped(tp, j))  23.5 us
    all_gather x1, waiting for transfers between devices, shards(): shared = lax.all_gather(shared, 'tp')  21.4 us
    ppermute x15, waiting for transfers between devices, other_core(): return lax.ppermute(values, 'blk', swapped(blk, 1))  21 us
  transfers between devices with their start and end apart: 57, of which 34 were waited for; matrix products, arithmetic and copies ran while one was open for 12% of the time, Pallas kernels for 24%

profile of v5, /device:TPU:0, one launch (start us, length us, event | category | flops | bytes accessed | tf_op | source)
XLA Modules:
  0.0 579.2 jit_solution(10514130082274948591)
XLA Ops:
  14.0 6.8 %qkv.1 = (bf16[4,2,320,384]{3,2,1,0:T(8,128)(2,1)}, bf16[1280,1024]{1,0:T(8,128)(2,1)}) custom-call(bf16[20,64,1024]{2,1,0:T(8,128)(2,1)} %refs_0_.1, f32[2,1024]{1,0:T(2,128)} %pad_maximum_fusion.5.refs_1_.refs_3_, bf16[3,1024,256]{2,1,0:T(8,128)(2,1)} %refs_1_.1, bf16[128,1280]{1,0:T(8,128)(2,1)} %copy-done.42), custom_call_target="tpu_custom_call" | custom-call | flops 2013265920 | bytes 8790016 | tf_op jit(solution)/shard_map/qkv/pallas_call | solution.py:43
  20.8 5.2 all-to-all-start
  25.9 21.4 %all-gather.11.cloned.1.call-done = bf16[512,1280]{1,0:T(8,128)(2,1)} async-done(((bf16[128,1280]{1,0:T(8,128)(2,1)}), bf16[512,1280]{1,0:T(8,128)(2,1)}) %all-gather.11.cloned.1.call-update) | async-done | bytes 1310736 | tf_op jit(solution)/shard_map/all_gather | solution.py:757
  48.4 2.8 all-to-all-done.refs_1_
  53.2 3.7 all-to-all-start.1
  59.8 2.6 constant_dynamic-slice_fusion.9
  63.6 7.5 %self_forward.1.refs_0_ = bf16[8,5,64,128]{3,2,1,0:T(8,128)(2,1)} custom-call(s32[5,2]{1,0:T(8,128)} %get-tuple-element.167.refs_0_, bf16[8,5,64,384]{3,2,1,0:T(8,128)(2,1)} %copy-done.7, bf16[320,1024]{1,0:T(8,128)(2,1)} %bitcast.94, bf16[320,1024]{1,0:T(8,128)(2,1)} %bitcast.105, bf16[320,1024]{1,0:T(8,128)(2,1)} %bitcast.120, bf16[640,1024]{1,0:T(8,128)(2,1)} %bitcast.124), custom_call_target="tpu_custom_call" | custom-call | flops 671088640 | bytes 2621440 | tf_op jit(solution)/shard_map/self_forward/pallas_call | solution.py:43
  71.1 9.9 %all-to-all-done.1.refs_1_.refs_2_ = bf16[4,4,128,512]{3,2,1,0:T(8,128)(2,1)S(1)} async-done(((bf16[4,4,128,512]{3,2,1,0:T(8,128)(2,1)}), bf16[4,4,128,512]{3,2,1,0:T(8,128)(2,1)S(1)}, u32[]{:S(2)}, u32[]{:S(2)}) %all-to-all-start.1) | async-done | bytes 2097184 | tf_op jit(solution)/shard_map/all_to_all | solution.py:698
  82.4 3.7 all-to-all-start.2
  86.1 11.1 %all-to-all-done.2 = bf16[8,5,64,128]{3,2,1,0:T(8,128)(2,1)S(1)} async-done(((bf16[8,5,64,128]{3,2,1,0:T(8,128)(2,1)}), bf16[8,5,64,128]{3,2,1,0:T(8,128)(2,1)S(1)}, u32[]{:S(2)}, u32[]{:S(2)}) %all-to-all-start.2) | async-done | bytes 655392 | tf_op jit(solution)/shard_map/all_to_all | solution.py:769
  97.8 3.6 collective-permute-start.2
  102.3 4.1 collective-permute-done.2.refs_4_.refs_8_
  106.4 6.1 %collective-permute-done.1.refs_3_.refs_7_ = bf16[2,320,128]{2,1,0:T(8,128)(2,1)S(1)} collective-permute-done((bf16[2,320,128]{2,1,0:T(8,128)(2,1)S(1)}, bf16[2,320,128]{2,1,0:T(8,128)(2,1)S(1)}, u32[]{:S(2)}, u32[]{:S(2)}) %collective-permute-start.1) | collective-permute-done | bytes 163872 | tf_op jit(solution)/shard_map/ppermute | solution.py:694
  114.5 4.9 all-to-all-start.3
  124.0 25.1 %collective-permute-done.5.refs_0_ = bf16[128,2048]{1,0:T(8,128)(2,1)} collective-permute-done((bf16[128,2048]{1,0:T(8,128)(2,1)}, bf16[128,2048]{1,0:T(8,128)(2,1)}, u32[]{:S(2)}, u32[]{:S(2)}) %collective-permute-start.5) | collective-permute-done | bytes 524320 | tf_op jit(solution)/shard_map/ppermute | solution.py:783
  149.0 6.8 %all-to-all-done.3.refs_3_.refs_5_.refs_1_.refs_9_.refs_11_ = bf16[4,4,128,768]{3,2,1,0:T(8,128)(2,1)S(1)} async-done(((bf16[4,4,128,768]{3,2,1,0:T(8,128)(2,1)}), bf16[4,4,128,768]{3,2,1,0:T(8,128)(2,1)S(1)}, u32[]{:S(2)}, u32[]{:S(2)}) %all-to-all-start.3) | async-done | bytes 3145760 | tf_op jit(solution)/shard_map/all_to_all | solution.py:698
  160.2 6.0 %collective-permute-done.4.refs_3_ = bf16[4,4,128,512]{3,2,1,0:T(8,128)(2,1)} collective-permute-done((bf16[4,4,128,512]{3,2,1,0:T(8,128)(2,1)}, bf16[4,4,128,512]{3,2,1,0:T(8,128)(2,1)}, u32[]{:S(2)}, u32[]{:S(2)}) %collective-permute-start.4) | collective-permute-done | bytes 2097184 | tf_op jit(solution)/shard_map/ppermute | solution.py:701
  166.2 7.7 %memory.1.refs_9_ = bf16[640,2048]{1,0:T(8,128)(2,1)} custom-call(s32[2]{0:T(128)} %pad_add_fusion.refs_0_, bf16[640,1024]{1,0:T(8,128)(2,1)} %bitcast.125, bf16[4,4,128,512]{3,2,1,0:T(8,128)(2,1)} %copy-done.6, bf16[4,4,128,512]{3,2,1,0:T(8,128)(2,1)} %collective-permute-done.4.refs_3_), custom_call_target="tpu_custom_call" | custom-call | flops 2684354560 | bytes 8126464 | tf_op jit(solution)/shard_map/memory/pallas_call | solution.py:43
  175.6 6.7 %to_cross.1 = (f32[320,1024]{1,0:T(8,128)}, bf16[320,1024]{1,0:T(8,128)(2,1)}, bf16[320,1024]{1,0:T(8,128)(2,1)}, bf16[320,1024]{1,0:T(8,128)(2,1)}) custom-call(s32[2]{0:T(128)} %pad_add_fusion.refs_0_, bf16[320,1024]{1,0:T(8,128)(2,1)} %bitcast.121, f32[2,1024]{1,0:T(2,128)} %get-tuple-element.173.refs_2_, bf16[4,4,128,768]{3,2,1,0:T(8,128)(2,1)} %copy-done.2, ...), custom_call_target="tpu_custom_call" | custom-call | flops 1342177280 | bytes 10887168 | tf_op jit(solution)/shard_map/to_cross/pallas_call | solution.py:43
  182.2 10.3 %cross_forward.1 = (bf16[320,1024]{1,0:T(8,128)(2,1)}, f32[320,1024]{1,0:T(8,128)}, bf16[320,1024]{1,0:T(8,128)(2,1)}) custom-call(s32[5,7]{1,0:T(8,128)} %concatenate.12.refs_0_, f32[320,1024]{1,0:T(8,128)} %get-tuple-element.60.refs_1_.refs_5_, bf16[320,1024]{1,0:T(8,128)(2,1)} %get-tuple-element.61.refs_2_.refs_6_, bf16[5,128,2048]{2,1,0:T(8,128)(2,1)} %bitcast.117, ...), custom_call_target="tpu_custom_call" | custom-call | flops 838860800 | bytes 13508608 | tf_op jit(solution)/shard_map/cross_forward/pallas_call | solution.py:43
  193.5 12.1 %feed_forward.2 = (bf16[320,2048]{1,0:T(8,128)(2,1)}, bf16[320,2048]{1,0:T(8,128)(2,1)}, f32[320,1024]{1,0:T(8,128)}, f32[320,1024]{1,0:T(8,128)}) custom-call(bf16[320,1024]{1,0:T(8,128)(2,1)} %get-tuple-element.63.refs_0_.refs_1_.refs_2_.refs_3_.refs_4_, bf16[320,1024]{1,0:T(8,128)(2,1)} %bitcast.95, bf16[1024,1024]{1,0:T(8,128)(2,1)} %refs_2_.5, ...), custom_call_target="tpu_custom_call" | custom-call | flops 5368709120 | bytes 19136512 | tf_op jit(solution)/shard_map/feed_forward/pallas_call | solution.py:43
  205.6 4.2 collective-permute-done.6.refs_0_.refs_6_.refs_7_.refs_8_.refs_9_
  210.7 11.6 %feed_forward.3 = (bf16[320,2048]{1,0:T(8,128)(2,1)}, bf16[320,2048]{1,0:T(8,128)(2,1)}, bf16[2,320,1024]{2,1,0:T(8,128)(2,1)}) custom-call(bf16[320,1024]{1,0:T(8,128)(2,1)} %copy-done.4, bf16[320,1024]{1,0:T(8,128)(2,1)} %bitcast.106, bf16[1024,1024]{1,0:T(8,128)(2,1)} %refs_2_.5, bf16[1024,1024]{1,0:T(8,128)(2,1)} %refs_3_.3, ...), custom_call_target="tpu_custom_call" | custom-call | flops 5368709120 | bytes 17825792 | tf_op jit(solution)/shard_map/feed_forward/pallas_call | solution.py:43
  222.2 8.4 %weight_grad.6 = (bf16[2,128,2048]{2,1,0:T(8,128)(2,1)}, bf16[2,128,2048]{2,1,0:T(8,128)(2,1)}, bf16[2,128,2048]{2,1,0:T(8,128)(2,1)}, bf16[2,128,2048]{2,1,0:T(8,128)(2,1)}) custom-call(s32[4]{0:T(128)} %add_subtract_fusion.1.refs_0_, bf16[320,1024]{1,0:T(8,128)(2,1)} %get-tuple-element.63.refs_0_.refs_1_.refs_2_.refs_3_.refs_4_, ...), custom_call_target="tpu_custom_call" | custom-call | flops 2684354560 | bytes 19922944 | tf_op jit(solution)/shard_map/weight_grad/pallas_call | solution.py:43
  239.1 9.6 %weight_grad.7.refs_13_ = bf16[4,2,128,2048]{3,2,1,0:T(8,128)(2,1)} custom-call(s32[4]{0:T(128)} %fusion.8.refs_0_, bf16[320,1024]{1,0:T(8,128)(2,1)} %get-tuple-element.63.refs_0_.refs_1_.refs_2_.refs_3_.refs_4_, bf16[320,1024]{1,0:T(8,128)(2,1)} %get-tuple-element.63.refs_0_.refs_1_.refs_2_.refs_3_.refs_4_, ...), custom_call_target="tpu_custom_call" | custom-call | flops 2684354560 | bytes 24117248 | tf_op jit(solution)/shard_map/weight_grad/pallas_call | solution.py:43
  248.7 4.9 all-to-all-start.4
  253.6 8.9 %collective-permute-done.7.refs_2_ = bf16[2,320,1024]{2,1,0:T(8,128)(2,1)S(1)} collective-permute-done((bf16[2,320,1024]{2,1,0:T(8,128)(2,1)S(1)}, bf16[2,320,1024]{2,1,0:T(8,128)(2,1)S(1)}, u32[]{:S(2)}, u32[]{:S(2)}) %collective-permute-start.7) | collective-permute-done | bytes 1310752 | tf_op jit(solution)/shard_map/ppermute | solution.py:871
  263.6 17.2 %cross_backward.1 = (bf16[320,1024]{1,0:T(8,128)(2,1)}, bf16[320,1024]{1,0:T(8,128)(2,1)}, f32[320,1024]{1,0:T(8,128)}, bf16[320,1024]{1,0:T(8,128)(2,1)}, bf16[...) custom-call(s32[5,7]{1,0:T(8,128)} %concatenate.12.refs_0_, ...), custom_call_target="tpu_custom_call" | custom-call | flops 2432696320 | bytes 28340224 | tf_op jit(solution)/shard_map/cross_backward/pallas_call | solution.py:43
  286.6 2.5 dynamic-slice_bitcast_fusion
  291.2 6.7 %collective-permute-done.13.refs_2_ = bf16[2,320,128]{2,1,0:T(8,128)(2,1)S(1)} collective-permute-done((bf16[2,320,128]{2,1,0:T(8,128)(2,1)S(1)}, bf16[2,320,128]{2,1,0:T(8,128)(2,1)S(1)}, u32[]{:S(2)}, u32[]{:S(2)}) %collective-permute-start.13) | collective-permute-done | bytes 163872 | tf_op jit(solution)/shard_map/ppermute | solution.py:694
  301.9 3.8 all-to-all-start.5
  305.8 2.9 fusion.refs_0_
  308.7 8.1 %all-to-all-done.5.refs_2_.refs_1_ = bf16[8,5,64,128]{3,2,1,0:T(8,128)(2,1)S(1)} async-done(((bf16[8,5,64,128]{3,2,1,0:T(8,128)(2,1)}), bf16[8,5,64,128]{3,2,1,0:T(8,128)(2,1)S(1)}, u32[]{:S(2)}, u32[]{:S(2)}) %all-to-all-start.5) | async-done | bytes 655392 | tf_op jit(solution)/shard_map/all_to_all | solution.py:936
  317.7 3.5 all-to-all-start.6
  321.2 13.3 %self_backward.1.refs_0_ = bf16[8,5,64,384]{3,2,1,0:T(8,128)(2,1)} custom-call(s32[5,2]{1,0:T(8,128)} %get-tuple-element.167.refs_0_, bf16[8,5,64,384]{3,2,1,0:T(8,128)(2,1)} %copy-done.7, bf16[8,5,64,128]{3,2,1,0:T(8,128)(2,1)} %copy-done.17), custom_call_target="tpu_custom_call" | custom-call | flops 1342177280 | bytes 4587520 | tf_op jit(solution)/shard_map/self_backward/pallas_call | solution.py:43
  334.5 2.5 all-to-all-done.6.refs_1_
  338.1 4.0 all-to-all-start.7
  344.2 3.7 ffn_sum.1
  348.9 5.3 text_grad.1.refs_26_
  354.2 6.8 %weight_grad.8 = (bf16[5,128,1024]{2,1,0:T(8,128)(2,1)}, bf16[5,128,1024]{2,1,0:T(8,128)(2,1)}, bf16[5,128,1024]{2,1,0:T(8,128)(2,1)}, bf16[5,128,1024]{2,1,0:T(8,128)(2,1)}) custom-call(s32[4]{0:T(128)} %add_subtract_fusion.refs_0_, bf16[320,1024]{1,0:T(8,128)(2,1)} %get-tuple-element.77.refs_1_.refs_2_.refs_3_.refs_4_, ...), custom_call_target="tpu_custom_call" | custom-call | flops 1174405120 | bytes 17039360 | tf_op jit(solution)/shard_map/weight_grad/pallas_call | solution.py:43
  363.1 2.4 collective-permute-done.16.refs_26_
  370.1 8.0 %weight_grad.9 = (bf16[5,128,1024]{2,1,0:T(8,128)(2,1)}, bf16[5,128,1024]{2,1,0:T(8,128)(2,1)}, bf16[5,128,1024]{2,1,0:T(8,128)(2,1)}, bf16[5,128,1024]{2,1,0:T(8,128)(2,1)}) custom-call(s32[4]{0:T(128)} %fusion.9.refs_0_, bf16[320,1024]{1,0:T(8,128)(2,1)} %get-tuple-element.77.refs_1_.refs_2_.refs_3_.refs_4_, ...), custom_call_target="tpu_custom_call" | custom-call | flops 1174405120 | bytes 22282240 | tf_op jit(solution)/shard_map/weight_grad/pallas_call | solution.py:43
  378.1 10.2 %collective-permute-done.20.refs_3_ = bf16[2,128,1024]{2,1,0:T(8,128)(2,1)} collective-permute-done((bf16[2,128,1024]{2,1,0:T(8,128)(2,1)}, bf16[2,128,1024]{2,1,0:T(8,128)(2,1)}, u32[]{:S(2)}, u32[]{:S(2)}) %collective-permute-start.20) | collective-permute-done | bytes 524320 | tf_op jit(solution)/shard_map/ppermute | solution.py:972
  389.6 5.9 %qkv_grad.1 = (bf16[4,320,1024]{2,1,0:T(8,128)(2,1)}, bf16[1280,768]{1,0:T(8,128)(2,1)}) custom-call(bf16[4,2,320,384]{3,2,1,0:T(8,128)(2,1)} %bitcast.134, bf16[3,1024,256]{2,1,0:T(8,128)(2,1)} %refs_1_.1, bf16[5,128,1024]{2,1,0:T(8,128)(2,1)} %get-tuple-element.88.refs_2_, bf16[2,128,1024]{2,1,0:T(8,128)(2,1)} %collective-permute-done.20.refs_3_), custom_call_target="tpu_custom_call" | custom-call | flops 2013265920 | bytes 8126464 | tf_op jit(solution)/shard_map/qkv_grad/pallas_call | solution.py:43
  395.5 4.6 all-to-all-start.8
  403.7 4.8 weight_grad.10
  411.8 3.7 collective-permute-start.30
  415.5 16.6 %collective-permute-done.21.refs_10_.refs_4_ = bf16[5,128,1024]{2,1,0:T(8,128)(2,1)S(1)} collective-permute-done((bf16[5,128,1024]{2,1,0:T(8,128)(2,1)}, bf16[5,128,1024]{2,1,0:T(8,128)(2,1)S(1)}, u32[]{:S(2)}, u32[]{:S(2)}) %collective-permute-start.21) | collective-permute-done | bytes 1310752 | tf_op jit(solution)/shard_map/ppermute | solution.py:720
  434.0 4.8 weight_grad.11
  438.8 21.8 %collective-permute-done.22.refs_5_ = bf16[5,128,1024]{2,1,0:T(8,128)(2,1)S(1)} collective-permute-done((bf16[5,128,1024]{2,1,0:T(8,128)(2,1)}, bf16[5,128,1024]{2,1,0:T(8,128)(2,1)S(1)}, u32[]{:S(2)}, u32[]{:S(2)}) %collective-permute-start.22) | collective-permute-done | bytes 1310752 | tf_op jit(solution)/shard_map/ppermute | solution.py:720
  460.6 7.4 %all-to-all-done.8.refs_0_ = bf16[4,320,1024]{2,1,0:T(8,128)(2,1)} async-done(((bf16[4,320,1024]{2,1,0:T(8,128)(2,1)}), bf16[4,320,1024]{2,1,0:T(8,128)(2,1)}, u32[]{:S(2)}, u32[]{:S(2)}) %all-to-all-start.8) | async-done | bytes 2621472 | tf_op jit(solution)/shard_map/all_to_all | solution.py:1010
  468.0 5.0 to_frames.1.refs_1_
  478.2 3.8 all-to-all-start.9
  482.1 4.8 convert.8
  489.2 5.0 first_norm.1
  500.3 5.3 add_convert_fusion
  505.7 2.4 copy.79
  522.9 2.4 collective-permute-start.41
  527.1 2.9 collective-permute-start.36
  532.4 7.0 %text_out.1 = f32[4,640,1024]{2,1,0:T(8,128)} custom-call(bf16[8,4,80,1024]{3,2,1,0:T(8,128)(2,1)} %bitcast.129), custom_call_target="tpu_custom_call" | custom-call | bytes 15728640 | tf_op jit(solution)/shard_map/text_out/pallas_call | solution.py:43
  539.5 9.9 %all-to-all-done.9.refs_0_ = bf16[4,320,1024]{2,1,0:T(8,128)(2,1)S(1)} async-done(((bf16[4,320,1024]{2,1,0:T(8,128)(2,1)}), bf16[4,320,1024]{2,1,0:T(8,128)(2,1)S(1)}, u32[]{:S(2)}, u32[]{:S(2)}) %all-to-all-start.9) | async-done | bytes 2621472 | tf_op jit(solution)/shard_map/all_to_all | solution.py:1060
  550.9 4.8 convert.6.refs_1_
  555.7 2.3 collective-permute-start.42
  560.0 5.3 collective-permute-done.42.refs_0_
  (291 shorter events, 117.6 us)
Async XLA Ops:
  7.2 150.9 %copy-start = (s32[20,2]{0,1:T(2,128)S(1)}, s32[20,2]{0,1:T(2,128)}, u32[]{:S(2)}) copy-start(s32[20,2]{0,1:T(2,128)} %param.17) | copy-start | bytes 484
  7.2 40.2 %all-gather.11.cloned.1.call-start = ((), (), s32[]{:S(2)}) async-start(), calls=%async_computation.12 | async-start | bytes 1638400 | tf_op jit(solution)/shard_map/all_gather | solution.py:757
  20.8 30.4 %all-to-all-start = ((bf16[8,5,64,384]{3,2,1,0:T(8,128)(2,1)}), bf16[8,5,64,384]{3,2,1,0:T(8,128)(2,1)S(1)}, u32[]{:S(2)}, u32[]{:S(2)}) async-start(bf16[8,5,64,384]{3,2,1,0:T(8,128)(2,1)} %bitcast.135), calls=%async_computation | async-start | bytes 3932160 | tf_op jit(solution)/shard_map/all_to_all | solution.py:752
  53.2 27.9 %all-to-all-start.1 = ((bf16[4,4,128,512]{3,2,1,0:T(8,128)(2,1)}), bf16[4,4,128,512]{3,2,1,0:T(8,128)(2,1)S(1)}, u32[]{:S(2)}, u32[]{:S(2)}) async-start(bf16[4,4,128,512]{3,2,1,0:T(8,128)(2,1)} %tied.21), calls=%async_computation.1 | async-start | bytes 4194304 | tf_op jit(solution)/shard_map/all_to_all | solution.py:698
  82.4 19.9 %copy-start.26 = (bf16[512,1280]{1,0:T(8,128)(2,1)S(1)}, bf16[512,1280]{1,0:T(8,128)(2,1)}, u32[]{:S(2)}) copy-start(bf16[512,1280]{1,0:T(8,128)(2,1)} %all-gather.11.cloned.1.call-done) | copy-start | bytes 3932164
  82.4 14.8 %all-to-all-start.2 = ((bf16[8,5,64,128]{3,2,1,0:T(8,128)(2,1)}), bf16[8,5,64,128]{3,2,1,0:T(8,128)(2,1)S(1)}, u32[]{:S(2)}, u32[]{:S(2)}) async-start(bf16[8,5,64,128]{3,2,1,0:T(8,128)(2,1)} %tied.22), calls=%async_computation.2 | async-start | bytes 1310720 | tf_op jit(solution)/shard_map/all_to_all | solution.py:769
  97.8 8.6 %collective-permute-start.2 = (bf16[2,320,128]{2,1,0:T(8,128)(2,1)S(1)}, bf16[2,320,128]{2,1,0:T(8,128)(2,1)S(1)}, u32[]{:S(2)}, u32[]{:S(2)}) collective-permute-start(bf16[2,320,128]{2,1,0:T(8,128)(2,1)S(1)} %get-tuple-element.157), channel_id=1, source_target_pairs={{0,3},{1,2},{2,1},{3,0},{4,7},{5,6},{6,5},{7,4},{8,11},{9,10},{10,... | collective-permute-start | bytes 491528 | tf_op jit(solution)/shard_map/ppermute | solution.py:694
  101.4 11.0 %collective-permute-start.1 = (bf16[2,320,128]{2,1,0:T(8,128)(2,1)S(1)}, bf16[2,320,128]{2,1,0:T(8,128)(2,1)S(1)}, u32[]{:S(2)}, u32[]{:S(2)}) collective-permute-start(bf16[2,320,128]{2,1,0:T(8,128)(2,1)S(1)} %get-tuple-element.158), channel_id=1, source_target_pairs={{0,2},{1,3},{2,0},{3,1},{4,6},{5,7},{6,4},{7,5},{8,10},{9,11},{10,... | collective-permute-start | bytes 491528 | tf_op jit(solution)/shard_map/ppermute | solution.py:694
  101.4 11.0 %collective-permute-start = (bf16[2,320,128]{2,1,0:T(8,128)(2,1)S(1)}, bf16[2,320,128]{2,1,0:T(8,128)(2,1)S(1)}, u32[]{:S(2)}, u32[]{:S(2)}) collective-permute-start(bf16[2,320,128]{2,1,0:T(8,128)(2,1)S(1)} %get-tuple-element.159), channel_id=1, source_target_pairs={{0,1},{1,0},{2,3},{3,2},{4,5},{5,4},{6,7},{7,6},{8,9},{9,8},{10,11... | collective-permute-start | bytes 491528 | tf_op jit(solution)/shard_map/ppermute | solution.py:694
  114.5 41.4 %all-to-all-start.3 = ((bf16[4,4,128,768]{3,2,1,0:T(8,128)(2,1)}), bf16[4,4,128,768]{3,2,1,0:T(8,128)(2,1)S(1)}, u32[]{:S(2)}, u32[]{:S(2)}) async-start(bf16[4,4,128,768]{3,2,1,0:T(8,128)(2,1)} %tied.23), calls=%async_computation.3 | async-start | bytes 6291456 | tf_op jit(solution)/shard_map/all_to_all | solution.py:698
  119.4 74.1 %all-gather.7.cloned.1.call-start = ((), (), s32[]{:S(2)}) async-start(), calls=%async_computation.10 | async-start | bytes 4718592 | tf_op jit(solution)/shard_map/all_gather | solution.py:785
  124.0 25.1 %collective-permute-start.5 = (bf16[128,2048]{1,0:T(8,128)(2,1)}, bf16[128,2048]{1,0:T(8,128)(2,1)}, u32[]{:S(2)}, u32[]{:S(2)}) collective-permute-start(bf16[128,2048]{1,0:T(8,128)(2,1)} %tied.24), channel_id=1, source_target_pairs={{0,2},{1,3},{2,0},{3,1},{4,6},{5,7},{6,4},{7,5},{8,10},{9,11},{10,... | collective-permute-start | bytes 1572872 | tf_op jit(solution)/shard_map/ppermute | solution.py:783
  157.5 16.4 %collective-permute-start.3 = (bf16[4,4,128,768]{3,2,1,0:T(8,128)(2,1)}, bf16[4,4,128,768]{3,2,1,0:T(8,128)(2,1)S(1)}, u32[]{:S(2)}, u32[]{:S(2)}) collective-permute-start(bf16[4,4,128,768]{3,2,1,0:T(8,128)(2,1)} %copy-done.2), channel_id=1, source_target_pairs={{0,4},{4,0},{8,12},{12,8},{16,20},{20,16},{24,28},{28,24},{1,5},{5... | collective-permute-start | bytes 9437192 | tf_op jit(solution)/shard_map/ppermute | solution.py:701
  157.6 8.6 %collective-permute-start.4 = (bf16[4,4,128,512]{3,2,1,0:T(8,128)(2,1)}, bf16[4,4,128,512]{3,2,1,0:T(8,128)(2,1)}, u32[]{:S(2)}, u32[]{:S(2)}) collective-permute-start(bf16[4,4,128,512]{3,2,1,0:T(8,128)(2,1)} %copy-done.6), channel_id=1, source_target_pairs={{0,4},{4,0},{8,12},{12,8},{16,20},{20,16},{24,28},{28,24},{1,5},{5... | collective-permute-start | bytes 6291464 | tf_op jit(solution)/shard_map/ppermute | solution.py:701
  192.5 17.3 %collective-permute-start.6 = (bf16[320,1024]{1,0:T(8,128)(2,1)}, bf16[320,1024]{1,0:T(8,128)(2,1)S(1)}, u32[]{:S(2)}, u32[]{:S(2)}) collective-permute-start(bf16[320,1024]{1,0:T(8,128)(2,1)} %get-tuple-element.63.refs_0_.refs_1_.refs_2_.refs_3_.refs_4_), channel_id=1, source_target_pairs={{0,1},{1,0},{2,3},{3,2},{4,5},{5,4},{6,7},{7,6},{8,9},{9,8},{10,11... | collective-permute-start | bytes 1966088 | tf_op jit(solution)/shard_map/ppermute | solution.py:865
  222.2 9.5 %copy-start.57 = (bf16[2,320,1024]{2,1,0:T(8,128)(2,1)S(1)}, bf16[2,320,1024]{2,1,0:T(8,128)(2,1)}, u32[]{:S(2)}) copy-start(bf16[2,320,1024]{2,1,0:T(8,128)(2,1)} %get-tuple-element.65) | copy-start | bytes 3932164
  230.7 2.9 collective-permute-start.8
  230.7 4.4 collective-permute-start.9
  231.2 5.4 collective-permute-start.10
  231.3 6.8 %collective-permute-start.11 = (bf16[2,128,2048]{2,1,0:T(8,128)(2,1)}, bf16[2,128,2048]{2,1,0:T(8,128)(2,1)S(1)}, u32[]{:S(2)}, u32[]{:S(2)}) collective-permute-start(bf16[2,128,2048]{2,1,0:T(8,128)(2,1)} %get-tuple-element.74), channel_id=1, source_target_pairs={{0,4},{4,0},{8,12},{12,8},{16,20},{20,16},{24,28},{28,24},{1,5},{5... | collective-permute-start | bytes 3145736 | tf_op jit(solution)/shard_map/ppermute | solution.py:701
  231.7 30.8 %collective-permute-start.7 = (bf16[2,320,1024]{2,1,0:T(8,128)(2,1)S(1)}, bf16[2,320,1024]{2,1,0:T(8,128)(2,1)S(1)}, u32[]{:S(2)}, u32[]{:S(2)}) collective-permute-start(bf16[2,320,1024]{2,1,0:T(8,128)(2,1)S(1)} %copy-done.57), channel_id=1, source_target_pairs={{0,1},{1,0},{2,3},{3,2},{4,5},{5,4},{6,7},{7,6},{8,9},{9,8},{10,11... | collective-permute-start | bytes 3932168 | tf_op jit(solution)/shard_map/ppermute | solution.py:871
  248.7 53.2 %all-to-all-start.4 = ((bf16[4,2,128,2048]{3,2,1,0:T(8,128)(2,1)}), bf16[4,2,128,2048]{3,2,1,0:T(8,128)(2,1)}, u32[]{:S(2)}, u32[]{:S(2)}) async-start(bf16[4,2,128,2048]{3,2,1,0:T(8,128)(2,1)} %weight_grad.7.refs_13_), calls=%async_computation.4 | async-start | bytes 8388608 | tf_op jit(solution)/shard_map/all_to_all | solution.py:698
  253.6 108.5 %all-gather.9.cloned.1.call-start = ((), (), s32[]{:S(2)}) async-start(), calls=%async_computation.11 | async-start | bytes 3276800 | tf_op jit(solution)/shard_map/all_gather | solution.py:928
  282.1 9.1 %collective-permute-start.14 = (bf16[2,320,128]{2,1,0:T(8,128)(2,1)S(1)}, bf16[2,320,128]{2,1,0:T(8,128)(2,1)S(1)}, u32[]{:S(2)}, u32[]{:S(2)}) collective-permute-start(bf16[2,320,128]{2,1,0:T(8,128)(2,1)S(1)} %get-tuple-element.154), channel_id=1, source_target_pairs={{0,3},{1,2},{2,1},{3,0},{4,7},{5,6},{6,5},{7,4},{8,11},{9,10},{10,... | collective-permute-start | bytes 491528 | tf_op jit(solution)/shard_map/ppermute | solution.py:694
  284.3 13.5 %collective-permute-start.13 = (bf16[2,320,128]{2,1,0:T(8,128)(2,1)S(1)}, bf16[2,320,128]{2,1,0:T(8,128)(2,1)S(1)}, u32[]{:S(2)}, u32[]{:S(2)}) collective-permute-start(bf16[2,320,128]{2,1,0:T(8,128)(2,1)S(1)} %get-tuple-element.155), channel_id=1, source_target_pairs={{0,2},{1,3},{2,0},{3,1},{4,6},{5,7},{6,4},{7,5},{8,10},{9,11},{10,... | collective-permute-start | bytes 491528 | tf_op jit(solution)/shard_map/ppermute | solution.py:694
  284.3 13.5 %collective-permute-start.12 = (bf16[2,320,128]{2,1,0:T(8,128)(2,1)S(1)}, bf16[2,320,128]{2,1,0:T(8,128)(2,1)S(1)}, u32[]{:S(2)}, u32[]{:S(2)}) collective-permute-start(bf16[2,320,128]{2,1,0:T(8,128)(2,1)S(1)} %get-tuple-element.156), channel_id=1, source_target_pairs={{0,1},{1,0},{2,3},{3,2},{4,5},{5,4},{6,7},{7,6},{8,9},{9,8},{10,11... | collective-permute-start | bytes 491528 | tf_op jit(solution)/shard_map/ppermute | solution.py:694
  289.1 16.6 %collective-permute-start.15 = (bf16[4,80,2048]{2,1,0:T(8,128)(2,1)}, bf16[4,80,2048]{2,1,0:T(8,128)(2,1)}, u32[]{:S(2)}, u32[]{:S(2)}) collective-permute-start(bf16[4,80,2048]{2,1,0:T(8,128)(2,1)} %dynamic-slice_bitcast_fusion), channel_id=1, source_target_pairs={{0,4},{4,0},{8,12},{12,8},{16,20},{20,16},{24,28},{28,24},{1,5},{5... | collective-permute-start | bytes 3932168 | tf_op jit(solution)/shard_map/ppermute | solution.py:701
  301.9 14.9 %all-to-all-start.5 = ((bf16[8,5,64,128]{3,2,1,0:T(8,128)(2,1)}), bf16[8,5,64,128]{3,2,1,0:T(8,128)(2,1)S(1)}, u32[]{:S(2)}, u32[]{:S(2)}) async-start(bf16[8,5,64,128]{3,2,1,0:T(8,128)(2,1)} %tied.27), calls=%async_computation.5 | async-start | bytes 1310720 | tf_op jit(solution)/shard_map/all_to_all | solution.py:936
  317.7 19.4 %all-to-all-start.6 = ((bf16[4,80,2048]{2,1,0:T(8,128)(2,1)}), bf16[4,80,2048]{2,1,0:T(8,128)(2,1)S(1)}, u32[]{:S(2)}, u32[]{:S(2)}) async-start(bf16[4,80,2048]{2,1,0:T(8,128)(2,1)} %tied.28), calls=%async_computation.6 | async-start | bytes 2621440 | tf_op jit(solution)/shard_map/all_to_all | solution.py:698
  338.1 50.2 %all-to-all-start.7 = ((bf16[8,5,64,384]{3,2,1,0:T(8,128)(2,1)}), bf16[8,5,64,384]{3,2,1,0:T(8,128)(2,1)S(1)}, u32[]{:S(2)}, u32[]{:S(2)}) async-start(bf16[8,5,64,384]{3,2,1,0:T(8,128)(2,1)} %tied.29.refs_4_), calls=%async_computation.7 | async-start | bytes 3932160 | tf_op jit(solution)/shard_map/all_to_all | solution.py:956
  361.0 4.5 collective-permute-start.16
  361.5 4.9 collective-permute-start.17
  361.6 6.7 %collective-permute-start.18 = (bf16[5,128,1024]{2,1,0:T(8,128)(2,1)}, bf16[5,128,1024]{2,1,0:T(8,128)(2,1)}, u32[]{:S(2)}, u32[]{:S(2)}) collective-permute-start(bf16[5,128,1024]{2,1,0:T(8,128)(2,1)} %get-tuple-element.86), channel_id=1, source_target_pairs={{0,4},{4,0},{8,12},{12,8},{16,20},{20,16},{24,28},{28,24},{1,5},{5... | collective-permute-start | bytes 3932168 | tf_op jit(solution)/shard_map/ppermute | solution.py:701
  362.0 8.1 %collective-permute-start.19 = (bf16[5,128,1024]{2,1,0:T(8,128)(2,1)}, bf16[5,128,1024]{2,1,0:T(8,128)(2,1)}, u32[]{:S(2)}, u32[]{:S(2)}) collective-permute-start(bf16[5,128,1024]{2,1,0:T(8,128)(2,1)} %get-tuple-element.87), channel_id=1, source_target_pairs={{0,4},{4,0},{8,12},{12,8},{16,20},{20,16},{24,28},{28,24},{1,5},{5... | collective-permute-start | bytes 3932168 | tf_op jit(solution)/shard_map/ppermute | solution.py:701
  362.1 26.3 %collective-permute-start.20 = (bf16[2,128,1024]{2,1,0:T(8,128)(2,1)}, bf16[2,128,1024]{2,1,0:T(8,128)(2,1)}, u32[]{:S(2)}, u32[]{:S(2)}) collective-permute-start(bf16[2,128,1024]{2,1,0:T(8,128)(2,1)} %tied.30), channel_id=1, source_target_pairs={{0,2},{1,3},{2,0},{3,1},{4,6},{5,7},{6,4},{7,5},{8,10},{9,11},{10,... | collective-permute-start | bytes 1572872 | tf_op jit(solution)/shard_map/ppermute | solution.py:972
  395.5 72.5 %all-to-all-start.8 = ((bf16[4,320,1024]{2,1,0:T(8,128)(2,1)}), bf16[4,320,1024]{2,1,0:T(8,128)(2,1)}, u32[]{:S(2)}, u32[]{:S(2)}) async-start(bf16[4,320,1024]{2,1,0:T(8,128)(2,1)} %get-tuple-element.90.refs_6_.refs_0_), calls=%async_computation.8 | async-start | bytes 5242880 | tf_op jit(solution)/shard_map/all_to_all | solution.py:1010
  400.1 132.4 %all-gather.13.cloned.1.call-start = ((), (), s32[]{:S(2)}) async-start(), calls=%async_computation.13 | async-start | bytes 5898240 | tf_op jit(solution)/shard_map/all_gather | solution.py:1042
  400.1 31.9 %collective-permute-start.21 = (bf16[5,128,1024]{2,1,0:T(8,128)(2,1)}, bf16[5,128,1024]{2,1,0:T(8,128)(2,1)S(1)}, u32[]{:S(2)}, u32[]{:S(2)}) collective-permute-start(bf16[5,128,1024]{2,1,0:T(8,128)(2,1)} %get-tuple-element.92), channel_id=1, source_target_pairs={{0,8},{4,12},{8,0},{12,4},{16,24},{20,28},{24,16},{28,20},{1,9},{5... | collective-permute-start | bytes 3932168 | tf_op jit(solution)/shard_map/ppermute | solution.py:720
  401.9 58.7 %collective-permute-start.22 = (bf16[5,128,1024]{2,1,0:T(8,128)(2,1)}, bf16[5,128,1024]{2,1,0:T(8,128)(2,1)S(1)}, u32[]{:S(2)}, u32[]{:S(2)}) collective-permute-start(bf16[5,128,1024]{2,1,0:T(8,128)(2,1)} %get-tuple-element.93), channel_id=1, source_target_pairs={{0,16},{4,20},{8,24},{12,28},{16,0},{20,4},{24,8},{28,12},{1,17},{... | collective-permute-start | bytes 3932168 | tf_op jit(solution)/shard_map/ppermute | solution.py:720
  403.4 57.3 %collective-permute-start.23 = (bf16[5,128,1024]{2,1,0:T(8,128)(2,1)}, bf16[5,128,1024]{2,1,0:T(8,128)(2,1)}, u32[]{:S(2)}, u32[]{:S(2)}) collective-permute-start(bf16[5,128,1024]{2,1,0:T(8,128)(2,1)} %get-tuple-element.94), channel_id=1, source_target_pairs={{0,24},{4,28},{8,16},{12,20},{16,8},{20,12},{24,0},{28,4},{1,25},{... | collective-permute-start | bytes 3932168 | tf_op jit(solution)/shard_map/ppermute | solution.py:720
  408.5 1.7 collective-permute-start.24
  408.5 1.9 collective-permute-start.25
  410.1 23.8 %copy-start.45 = (bf16[1,128,768]{2,1,0:T(8,128)(2,1)}, bf16[1,128,768]{2,1,0:T(8,128)(2,1)S(1)}, u32[]{:S(2)}) copy-start(bf16[1,128,768]{2,1,0:T(8,128)(2,1)S(1)} %collective-permute-done.24.refs_6_) | copy-start | bytes 589828
  410.2 1.7 collective-permute-start.26
  410.4 23.5 %copy-start.46 = (bf16[1,128,768]{2,1,0:T(8,128)(2,1)}, bf16[1,128,768]{2,1,0:T(8,128)(2,1)S(1)}, u32[]{:S(2)}) copy-start(bf16[1,128,768]{2,1,0:T(8,128)(2,1)S(1)} %collective-permute-done.25.refs_7_) | copy-start | bytes 589828
  410.4 5.0 collective-permute-start.27
  411.8 22.2 %copy-start.47 = (bf16[1,128,768]{2,1,0:T(8,128)(2,1)}, bf16[1,128,768]{2,1,0:T(8,128)(2,1)S(1)}, u32[]{:S(2)}) copy-start(bf16[1,128,768]{2,1,0:T(8,128)(2,1)S(1)} %collective-permute-done.26.refs_8_) | copy-start | bytes 589828
  411.8 61.2 %collective-permute-start.30 = (bf16[80,1024]{1,0:T(8,128)(2,1)S(1)}, bf16[80,1024]{1,0:T(8,128)(2,1)S(1)}, u32[]{:S(2)}, u32[]{:S(2)}) collective-permute-start(bf16[80,1024]{1,0:T(8,128)(2,1)S(1)} %copy-done.19), channel_id=1, source_target_pairs={{0,3},{1,2},{2,1},{3,0},{4,7},{5,6},{6,5},{7,4},{8,11},{9,10},{10,... | collective-permute-start | bytes 491528 | tf_op jit(solution)/shard_map/ppermute | solution.py:694
  415.5 18.5 %copy-start.48 = (bf16[1,128,768]{2,1,0:T(8,128)(2,1)}, bf16[1,128,768]{2,1,0:T(8,128)(2,1)S(1)}, u32[]{:S(2)}) copy-start(bf16[1,128,768]{2,1,0:T(8,128)(2,1)S(1)} %collective-permute-done.27.refs_9_) | copy-start | bytes 589828
  415.5 58.6 %collective-permute-start.29 = (bf16[80,1024]{1,0:T(8,128)(2,1)S(1)}, bf16[80,1024]{1,0:T(8,128)(2,1)S(1)}, u32[]{:S(2)}, u32[]{:S(2)}) collective-permute-start(bf16[80,1024]{1,0:T(8,128)(2,1)S(1)} %copy-done.19), channel_id=1, source_target_pairs={{0,2},{1,3},{2,0},{3,1},{4,6},{5,7},{6,4},{7,5},{8,10},{9,11},{10,... | collective-permute-start | bytes 491528 | tf_op jit(solution)/shard_map/ppermute | solution.py:694
  432.1 42.7 %collective-permute-start.28 = (bf16[80,1024]{1,0:T(8,128)(2,1)S(1)}, bf16[80,1024]{1,0:T(8,128)(2,1)S(1)}, u32[]{:S(2)}, u32[]{:S(2)}) collective-permute-start(bf16[80,1024]{1,0:T(8,128)(2,1)S(1)} %copy-done.19), channel_id=1, source_target_pairs={{0,1},{1,0},{2,3},{3,2},{4,5},{5,4},{6,7},{7,6},{8,9},{9,8},{10,11... | collective-permute-start | bytes 491528 | tf_op jit(solution)/shard_map/ppermute | solution.py:694
  478.2 71.2 %all-to-all-start.9 = ((bf16[4,320,1024]{2,1,0:T(8,128)(2,1)}), bf16[4,320,1024]{2,1,0:T(8,128)(2,1)S(1)}, u32[]{:S(2)}, u32[]{:S(2)}) async-start(bf16[4,320,1024]{2,1,0:T(8,128)(2,1)} %to_frames.1.refs_1_), calls=%async_computation.9 | async-start | bytes 5242880 | tf_op jit(solution)/shard_map/all_to_all | solution.py:1060
  495.5 3.1 collective-permute-start.31
  498.6 12.9 %collective-permute-start.32 = (f32[6,1024]{1,0:T(8,128)S(1)}, f32[6,1024]{1,0:T(8,128)S(1)}, u32[]{:S(2)}, u32[]{:S(2)}) collective-permute-start(f32[6,1024]{1,0:T(8,128)S(1)} %add.164), channel_id=1, source_target_pairs={{0,8},{4,12},{8,0},{12,4},{16,24},{20,28},{24,16},{28,20},{1,9},{5... | collective-permute-start | bytes 73736 | tf_op jit(solution)/shard_map/ppermute | solution.py:1065
  508.1 17.2 %collective-permute-start.37 = (bf16[1,128,768]{2,1,0:T(8,128)(2,1)}, bf16[1,128,768]{2,1,0:T(8,128)(2,1)S(1)}, u32[]{:S(2)}, u32[]{:S(2)}) collective-permute-start(bf16[1,128,768]{2,1,0:T(8,128)(2,1)} %get-tuple-element.103), channel_id=1, source_target_pairs={{0,8},{4,12},{8,0},{12,4},{16,24},{20,28},{24,16},{28,20},{1,9},{5... | collective-permute-start | bytes 589832 | tf_op jit(solution)/shard_map/ppermute | solution.py:720
  508.4 17.5 %collective-permute-start.38 = (bf16[1,128,768]{2,1,0:T(8,128)(2,1)}, bf16[1,128,768]{2,1,0:T(8,128)(2,1)}, u32[]{:S(2)}, u32[]{:S(2)}) collective-permute-start(bf16[1,128,768]{2,1,0:T(8,128)(2,1)} %get-tuple-element.104), channel_id=1, source_target_pairs={{0,16},{4,20},{8,24},{12,28},{16,0},{20,4},{24,8},{28,12},{1,17},{... | collective-permute-start | bytes 589832 | tf_op jit(solution)/shard_map/ppermute | solution.py:720
  510.2 16.9 %collective-permute-start.39 = (bf16[1,128,768]{2,1,0:T(8,128)(2,1)}, bf16[1,128,768]{2,1,0:T(8,128)(2,1)}, u32[]{:S(2)}, u32[]{:S(2)}) collective-permute-start(bf16[1,128,768]{2,1,0:T(8,128)(2,1)} %get-tuple-element.105), channel_id=1, source_target_pairs={{0,24},{4,28},{8,16},{12,20},{16,8},{20,12},{24,0},{28,4},{1,25},{... | collective-permute-start | bytes 589832 | tf_op jit(solution)/shard_map/ppermute | solution.py:720
  511.6 11.3 %collective-permute-start.33 = (f32[6,1024]{1,0:T(8,128)S(1)}, f32[6,1024]{1,0:T(8,128)S(1)}, u32[]{:S(2)}, u32[]{:S(2)}) collective-permute-start(f32[6,1024]{1,0:T(8,128)S(1)} %add.165), channel_id=1, source_target_pairs={{0,16},{4,20},{8,24},{12,28},{16,0},{20,4},{24,8},{28,12},{1,17},{... | collective-permute-start | bytes 73736 | tf_op jit(solution)/shard_map/ppermute | solution.py:1065
  521.3 44.8 %collective-permute-start.40 = (bf16[5,128,256]{2,1,0:T(8,128)(2,1)}, bf16[5,128,256]{2,1,0:T(8,128)(2,1)}, u32[]{:S(2)}, u32[]{:S(2)}) collective-permute-start(bf16[5,128,256]{2,1,0:T(8,128)(2,1)} %bitcast.46), channel_id=1, source_target_pairs={{0,1},{1,0},{2,3},{3,2},{4,5},{5,4},{6,7},{7,6},{8,9},{9,8},{10,11... | collective-permute-start | bytes 983048 | tf_op jit(solution)/shard_map/ppermute | solution.py:694
  522.9 43.2 %collective-permute-start.41 = (bf16[5,128,256]{2,1,0:T(8,128)(2,1)}, bf16[5,128,256]{2,1,0:T(8,128)(2,1)}, u32[]{:S(2)}, u32[]{:S(2)}) collective-permute-start(bf16[5,128,256]{2,1,0:T(8,128)(2,1)} %bitcast.147), channel_id=1, source_target_pairs={{0,2},{1,3},{2,0},{3,1},{4,6},{5,7},{6,4},{7,5},{8,10},{9,11},{10,... | collective-permute-start | bytes 983048 | tf_op jit(solution)/shard_map/ppermute | solution.py:694
  525.3 32.7 %collective-permute-start.35 = (f32[6,128]{1,0:T(8,128)S(1)}, f32[6,128]{1,0:T(8,128)S(1)}, u32[]{:S(2)}, u32[]{:S(2)}) collective-permute-start(f32[6,128]{1,0:T(8,128)S(1)} %fusion.6), channel_id=1, source_target_pairs={{0,2},{1,3},{2,0},{3,1},{4,6},{5,7},{6,4},{7,5},{8,10},{9,11},{10,... | collective-permute-start | bytes 9224 | tf_op jit(solution)/shard_map/ppermute | solution.py:694
  525.9 32.8 %collective-permute-start.34 = (f32[6,128]{1,0:T(8,128)S(1)}, f32[6,128]{1,0:T(8,128)S(1)}, u32[]{:S(2)}, u32[]{:S(2)}) collective-permute-start(f32[6,128]{1,0:T(8,128)S(1)} %fusion.6), channel_id=1, source_target_pairs={{0,1},{1,0},{2,3},{3,2},{4,5},{5,4},{6,7},{7,6},{8,9},{9,8},{10,11... | collective-permute-start | bytes 9224 | tf_op jit(solution)/shard_map/ppermute | solution.py:694
  527.1 28.6 %collective-permute-start.36 = (f32[6,128]{1,0:T(8,128)S(1)}, f32[6,128]{1,0:T(8,128)S(1)}, u32[]{:S(2)}, u32[]{:S(2)}) collective-permute-start(f32[6,128]{1,0:T(8,128)S(1)} %fusion.6), channel_id=1, source_target_pairs={{0,3},{1,2},{2,1},{3,0},{4,7},{5,6},{6,5},{7,4},{8,11},{9,10},{10,... | collective-permute-start | bytes 9224 | tf_op jit(solution)/shard_map/ppermute | solution.py:694
  555.7 9.6 %collective-permute-start.42 = (bf16[5,128,256]{2,1,0:T(8,128)(2,1)S(1)}, bf16[5,128,256]{2,1,0:T(8,128)(2,1)S(1)}, u32[]{:S(2)}, u32[]{:S(2)}) collective-permute-start(bf16[5,128,256]{2,1,0:T(8,128)(2,1)S(1)} %bitcast.148), channel_id=1, source_target_pairs={{0,3},{1,2},{2,1},{3,0},{4,7},{5,6},{6,5},{7,4},{8,11},{9,10},{10,... | collective-permute-start | bytes 983048 | tf_op jit(solution)/shard_map/ppermute | solution.py:694
  (51 other events, 140.1 us)
Sparse Core Ops, SparseCore 0:
  11.8 35.4 all-gather.10
  157.6 35.8 all-gather.6
  299.4 53.6 all-gather.8
  478.3 46.0 all-gather.12
